TPU v7x, 32 devices: a whole 2x2x4 slice. The times are simulated.
32 devices in a mesh: chan: 4 (over z), inp: 8 (over y, x, core).
Axes of the slice: x: 2, y: 2, z: 4, core: 2. Of those that a mesh axis runs over, the one named last changes fastest.
Arguments:
- voltages: int32 [2, 256, 16, 4096], P(None, 'chan', None, 'inp'), may hold values from -128 to 127
- fir_taps: float32 [4, 16], replicated, may hold values from -3 to 3
Outputs:
- visibilities: float32 [16, 2, 4096, 4096], P('chan', None, 'inp')
All inputs are finite; a program needn't handle non-finite values.
Results may differ from a plain program's by a relative error of at most 0.0036.
Values may be sent and summed in bfloat16 or wider, within the bound.
No kernel may reach another device: no remote copies, remote signals or barrier semaphores. Data moves between devices by JAX's collectives and lax.ppermute only.
A program may use at most 256 MiB of HBM per device.

v0:
```python
import math

import jax
import jax.numpy as jnp
from jax import lax
from jax.sharding import PartitionSpec as P

volt_scale = 1.0 / 256.0


def passed_along(x, axis, by):
    count = lax.axis_size(axis)
    pairs = [(i, i + by) for i in range(count) if 0 <= i + by < count]
    return lax.ppermute(x, axis, pairs)


def dft_tables(count):
    index = jnp.arange(count, dtype=jnp.int32)
    phase = index[:, None] * index[None, :] % count
    angle = phase.astype(jnp.float32) * (2.0 * math.pi / count)
    return (jnp.cos(angle), jnp.sin(angle))


def transform(filtered, count):
    cosine, sine = dft_tables(count)
    real_in = filtered[0]
    imag_in = filtered[1]
    high = lax.Precision.HIGHEST
    real_out = jnp.einsum("cn,snb->csb", cosine, real_in, precision=high) + jnp.einsum(
        "cn,snb->csb", sine, imag_in, precision=high
    )
    imag_out = jnp.einsum("cn,snb->csb", cosine, imag_in, precision=high) - jnp.einsum(
        "cn,snb->csb", sine, real_in, precision=high
    )
    return (jnp.stack([real_out, imag_out], 1) * volt_scale).astype(jnp.bfloat16)


def body(voltages, fir_taps):
    frames = voltages.shape[1]
    chans = voltages.shape[2]
    tap_count = fir_taps.shape[0]
    early_rim = passed_along(voltages[:, frames - (tap_count - 1) :], "chan", 1)
    extended = jnp.concatenate([early_rim, voltages], 1).astype(jnp.float32)
    filtered = (
        fir_taps[0][None, None, :, None] * extended[:, tap_count - 1 : tap_count - 1 + frames]
    )
    for tap_index in range(1, tap_count):
        begin = tap_count - 1 - tap_index
        filtered = (
            filtered
            + fir_taps[tap_index][None, None, :, None] * extended[:, begin : begin + frames]
        )
    spectra = transform(filtered, chans)
    turned = lax.all_to_all(spectra, "chan", split_axis=0, concat_axis=2, tiled=True)
    norm_factor = 1.0 / turned.shape[2]
    piece = lax.all_gather(turned, "inp", axis=3, tiled=True)
    rotated = jnp.concatenate([-piece[:, 1:2], piece[:, 0:1]], axis=1)
    real_part = jnp.einsum("cpsi,cpsj->cij", turned, piece, preferred_element_type=jnp.float32)
    imag_part = jnp.einsum("cpsi,cpsj->cij", turned, rotated, preferred_element_type=jnp.float32)
    return jnp.stack([real_part, imag_part], 1) * norm_factor


def solution(mesh):
    placed = (P(None, "chan", None, "inp"), P())
    return jax.shard_map(
        body, mesh=mesh, in_specs=placed, out_specs=P("chan", None, "inp", None), check_vma=False
    )
```

profile of v0, /device:TPU:0, one launch (start us, length us, event | category | flops | bytes accessed | tf_op | source)
XLA Modules:
  0.0 325.3 jit_solution(13675856872822440595)
XLA Ops:
  6.5 0.0 all-gather.2.cloned.1.call-start
  6.5 0.9 slice.40
  7.5 4.9 %collective-permute-start = (s32[2,3,16,512]{3,2,1,0:T(8,128)S(1)}, s32[2,3,16,512]{3,2,1,0:T(8,128)S(1)}, u32[]{:S(2)}, u32[]{:S(2)}) collective-permute-start(s32[2,3,16,512]{3,2,1,0:T(8,128)S(1)} %slice.40), channel_id=1, source_target_pairs={{0,8},{8,16},{16,24},{1,9},{9,17},{17,25},{2,10},{10,18},{18,26},{... | collective-permute-start | bytes 589832 | tf_op jit(solution)/shard_map/ppermute | solution.py:14
  12.4 0.8 slice_bitcast_fusion.13
  13.3 3.3 %collective-permute-done = s32[2,3,16,512]{3,2,1,0:T(8,128)S(1)} collective-permute-done((s32[2,3,16,512]{3,2,1,0:T(8,128)S(1)}, s32[2,3,16,512]{3,2,1,0:T(8,128)S(1)}, u32[]{:S(2)}, u32[]{:S(2)}) %collective-permute-start) | collective-permute-done | bytes 196640 | tf_op jit(solution)/shard_map/ppermute | solution.py:14
  16.6 2.7 add_convert_fusion
  19.3 2.7 fusion.7
  22.0 1.9 fusion.11
  23.9 1.9 fusion.14
  25.9 1.9 subtract_bitcast_fusion
  27.8 1.9 add_bitcast_fusion
  29.8 0.6 fusion.10
  30.4 1.2 copy.7
  31.6 52.9 %all_to_all.18 = bf16[16,2,64,512]{3,2,1,0:T(8,128)(2,1)S(1)} all-to-all(bf16[16,2,64,512]{3,2,1,0:T(8,128)(2,1)S(1)} %copy.7), channel_id=1, replica_groups=mesh['chan'=4,'inp'=8] {'chan'}, dimensions={0} | all-to-all | bytes 4194304 | tf_op jit(solution)/shard_map/all_to_all | solution.py:54
  84.5 1.5 copy.8
  86.0 0.0 all-gather.2.cloned.1.call-update
  86.1 0.0 copy-start
  86.1 92.4 %all-gather.2.cloned.1.call-done = bf16[4,2,256,4096]{3,2,1,0:T(8,128)(2,1)} async-done(((bf16[4,2,256,512]{3,2,1,0:T(8,128)(2,1)}), bf16[4,2,256,4096]{3,2,1,0:T(8,128)(2,1)}) %all-gather.2.cloned.1.call-update) | async-done | bytes 16777232 | tf_op jit(solution)/shard_map/all_gather | solution.py:56
  178.4 11.3 %slice_negate_fusion = (bf16[4,1,256,4096]{3,2,1,0:T(8,128)(2,1)}, bf16[4,1,256,4096]{3,2,1,0:T(8,128)(2,1)}) fusion(bf16[4,2,256,4096]{3,2,1,0:T(8,128)(2,1)} %all-gather.2.cloned.1.call-done), kind=kLoop, calls=%fused_computation.7 | loop fusion | flops 4194304 | bytes 33554432 | tf_op jit(solution)/shard_map/neg | solution.py:57
  189.8 0.0 copy-done
  189.8 19.7 %fusion.4 = f32[4,1,512,4096]{3,2,0,1:T(8,128)} fusion(bf16[4,2,256,512]{3,2,1,0:T(8,128)(2,1)S(1)} %bitcast.50, bf16[4,1,256,4096]{3,2,1,0:T(8,128)(2,1)} %get-tuple-element.6, bf16[4,1,256,4096]{3,2,1,0:T(8,128)(2,1)} %get-tuple-element.5), kind=kOutput, calls=%fused_computation.6 | convolution fusion | flops 8598323200 | bytes 52428800 | tf_op jit(solution)/shard_map/cpsi,cpsj->cij/dot_general | solution.py:59
  209.5 21.1 %convolution_bitcast_fusion = f32[4,1,512,4096]{3,2,0,1:T(8,128)} fusion(bf16[4,2,256,512]{3,2,1,0:T(8,128)(2,1)S(1)} %bitcast.51, bf16[4,2,256,4096]{3,2,1,0:T(8,128)(2,1)} %all-gather.2.cloned.1.call-done), kind=kOutput, calls=%fused_computation.5 | convolution fusion | flops 8589934592 | bytes 52428800 | tf_op jit(solution)/shard_map/cpsi,cpsj->cij/dot_general | solution.py:58
  230.6 43.6 %maximum_multiply_fusion = f32[4,2,512,4096]{3,2,0,1:T(8,128)} fusion(f32[4,1,512,4096]{3,2,0,1:T(8,128)} %fusion.4, f32[4,1,512,4096]{3,2,0,1:T(8,128)} %convolution_bitcast_fusion), kind=kLoop, calls=%fused_computation | loop fusion | flops 33554432 | bytes 134217728 | tf_op jit(solution)/shard_map/mul | solution.py:60
  274.2 44.2 %copy.11 = f32[4,2,512,4096]{3,2,1,0:T(8,128)} copy(f32[4,2,512,4096]{3,2,0,1:T(8,128)} %maximum_multiply_fusion) | data formatting | bytes 134217728 | tf_op jit(solution)/shard_map/mul | solution.py:60
Async XLA Ops:
  6.5 171.9 %all-gather.2.cloned.1.call-start = ((), (), s32[]{:S(2)}) async-start(), calls=%async_computation.1 | async-start | bytes 18874368 | tf_op jit(solution)/shard_map/all_gather | solution.py:56
  7.5 9.1 %collective-permute-start = (s32[2,3,16,512]{3,2,1,0:T(8,128)S(1)}, s32[2,3,16,512]{3,2,1,0:T(8,128)S(1)}, u32[]{:S(2)}, u32[]{:S(2)}) collective-permute-start(s32[2,3,16,512]{3,2,1,0:T(8,128)S(1)} %slice.40), channel_id=1, source_target_pairs={{0,8},{8,16},{16,24},{1,9},{9,17},{17,25},{2,10},{10,18},{18,26},{... | collective-permute-start | bytes 589832 | tf_op jit(solution)/shard_map/ppermute | solution.py:14
  86.1 103.7 %copy-start = (bf16[4,4,2,64,512]{4,3,0,2,1:T(8,128)(2,1)S(1)}, bf16[4,4,2,64,512]{4,3,0,2,1:T(8,128)(2,1)}, u32[]{:S(2)}) copy-start(bf16[4,4,2,64,512]{4,3,0,2,1:T(8,128)(2,1)} %copy.8) | copy-start | bytes 6291460
Sparse Core Ops, SparseCore 0:
  86.2 92.2 all-gather.1
where the time goes:
time: 326 us; the launch traced here: 325 us
  waiting for transfers between devices  95.7 us (29%)
  other arithmetic  61 us (19%)
  blocking collectives  52.9 us (16%)
  local copies, waits for them, and re-layouts  48.7 us (15%)
  matrix products  48.6 us (15%)
  between operations  13.5 us (4%)
  starting transfers between devices  4.94 us (2%)
    all_gather x1, waiting for transfers between devices, body(): piece = lax.all_gather(turned, 'inp', axis=3, tiled=True)  92.4 us
    all_to_all x1, blocking collectives, body(): lax.all_to_all(spectra, 'chan', split_axis=0, concat_axis=2, tiled=True)  52.9 us
    mul x1, local copies, waits for them, and re-layouts, body(): return jnp.stack([real_part, imag_part], 1) * norm_factor  44.2 us
    mul x1, other arithmetic, body(): return jnp.stack([real_part, imag_part], 1) * norm_factor  43.6 us
    dot_general x1, matrix products, body(): jnp.einsum('cpsi,cpsj->cij', turned, piece, preferred_element_type=jnp.fl...  21.1 us
    dot_general x1, matrix products, body(): jnp.einsum('cpsi,cpsj->cij', turned, rotated, preferred_element_type=jnp....  19.7 us
    neg x1, other arithmetic, body(): rotated = jnp.concatenate([-piece[:, 1:2], piece[:, 0:1]], axis=1)  11.3 us
  transfers between devices with their start and end apart: 2, of which 2 were waited for; matrix products, arithmetic and copies ran while one was open for 0% of the time, Pallas kernels for 0%

commit v1 on v0

v1 whole, which is shorter than its diff:
```python
import functools
import math

import jax
import jax.numpy as jnp
import numpy as np
from jax import lax
from jax.experimental import pallas as pl
from jax.experimental.pallas import tpu as pltpu
from jax.sharding import PartitionSpec as P

VOLT_SCALE = 1.0 / 256.0
GROUP = 16
MIB = 1 << 20
ANY = pl.BlockSpec(memory_space=pl.ANY)


def struct(shape, dtype=jnp.bfloat16):
    return jax.ShapeDtypeStruct(shape, dtype)


def transform_rows(chans, span):
    index = np.arange(chans)
    angle = (index[:, None] * index[None, :] % chans) * (2.0 * math.pi / chans)
    cosine, sine = np.cos(angle), np.sin(angle)
    rows = np.stack([np.stack([cosine, sine], 1), np.stack([-sine, cosine], 1)], 1) * VOLT_SCALE
    rows = np.broadcast_to(rows[:, :, :, None], (chans, 2, 2, span, chans))
    return np.tile(rows.reshape(chans, 2, -1), (2, 1, 1)).astype(np.float32)


def channelize_step(shape, volts, rim, table, taps, *rest):
    devices, mine, tap_count = shape
    outs, (coarse, fine, held) = rest[:-3], rest[-3:]
    _, group, chans, width = volts.shape
    ahead = (tap_count - 1) * chans
    span = ahead + group * chans

    @pl.when(pl.program_id(0) == 0)
    def _():
        column = lax.broadcasted_iota(jnp.int32, (group, 2 * span), 1)
        column = jnp.where(column >= span, column - span, column) // chans
        row = lax.broadcasted_iota(jnp.int32, (group, 2 * span), 0)
        band = jnp.zeros((group, 2 * span), jnp.float32)
        for k in range(tap_count):
            band = band + jnp.where(column == row + (tap_count - 1 - k), taps[k : k + 1, :], 0.0)
        for c in range(table.shape[0]):
            for p in range(2):
                weights = table[c, p : p + 1, :] * band
                high = weights.astype(jnp.bfloat16)
                at = (2 * c + p) * group
                coarse[at : at + group, :] = high
                fine[at : at + group, :] = (weights - high.astype(jnp.float32)).astype(jnp.bfloat16)
        for q in range(2):
            held[q * span : q * span + ahead, :] = rim[q].reshape(ahead, width)

    @pl.when(pl.program_id(0) > 0)
    def _():
        for q in range(2):
            held[q * span : q * span + ahead, :] = held[(q + 1) * span - ahead : (q + 1) * span, :]

    for q in range(2):
        held[q * span + ahead : (q + 1) * span, :] = (
            volts[q].astype(jnp.float32).astype(jnp.bfloat16).reshape(group * chans, width)
        )
    frames = held[...]
    result = jnp.dot(coarse[...], frames, preferred_element_type=jnp.float32)
    result = result + jnp.dot(fine[...], frames, preferred_element_type=jnp.float32)
    result = result.astype(jnp.bfloat16).reshape(devices, mine, 2, group, width)
    outs[0][...] = result[0]
    for d in range(1, devices):
        for k in range(mine):
            outs[1 + (d - 1) * mine + k][...] = result[d, k]


def channelize(voltages, rim, table, taps, devices):
    _, frames, chans, width = voltages.shape
    tap_count = taps.shape[0]
    mine = chans // devices
    span = (GROUP + tap_count - 1) * chans
    flops = 2 * 2 * frames * (chans * 2) * (2 * span) * width
    outs = pl.pallas_call(
        functools.partial(channelize_step, (devices, mine, tap_count)),
        grid=(frames // GROUP,),
        in_specs=[
            pl.BlockSpec((2, GROUP, chans, width), lambda g: (0, g, 0, 0)),
            pl.BlockSpec(rim.shape, lambda g: (0, 0, 0, 0)),
            pl.BlockSpec(table.shape, lambda g: (0, 0, 0)),
            pl.BlockSpec(taps.shape, lambda g: (0, 0)),
        ],
        out_specs=[pl.BlockSpec((mine, 2, GROUP, width), lambda g: (0, 0, g, 0))]
        + [pl.BlockSpec((2, GROUP, width), lambda g: (0, g, 0))] * ((devices - 1) * mine),
        out_shape=[struct((mine, 2, frames, width))] + [struct((2, frames, width))] * ((devices - 1) * mine),
        scratch_shapes=[
            pltpu.VMEM((chans * 2 * GROUP, 2 * span), jnp.bfloat16),
            pltpu.VMEM((chans * 2 * GROUP, 2 * span), jnp.bfloat16),
            pltpu.VMEM((2 * span, width), jnp.bfloat16),
        ],
        compiler_params=pltpu.CompilerParams(vmem_limit_bytes=32 * MIB),
        cost_estimate=pl.CostEstimate(flops=flops, bytes_accessed=6 * voltages.size, transcendentals=0),
        name="channelize",
    )(voltages, rim, table, taps)
    return outs[0], [[outs[1 + (d - 1) * mine + k] for d in range(1, devices)] for k in range(mine)]


def pack_step(*refs):
    for d, ref in enumerate(refs[:-1]):
        refs[-1][d] = ref[...]


def pack(pieces):
    return pl.pallas_call(
        pack_step,
        out_shape=struct((len(pieces),) + pieces[0].shape),
        cost_estimate=pl.CostEstimate(flops=0, bytes_accessed=4 * pieces[0].size * len(pieces), transcendentals=0),
        name="pack",
    )(*pieces)


def products(left, panel, scale, out):
    rows = out.shape[2]
    result = jnp.dot(left, panel, preferred_element_type=jnp.float32) * scale
    out[0, 0] = result[:rows]
    out[0, 1] = result[rows:]


def correlate_here_step(count, scale, has_out, columns, *refs):
    near, far = refs[:count], refs[count : 2 * count]
    out, packed, left = refs[2 * count + has_out :]
    devices, _, frames, width = packed.shape[1:]
    depth = devices * 2 * frames
    for j in range(count):

        @pl.when(pl.program_id(0) == j)
        def _():
            panel = jnp.concatenate([near[j][0].reshape(2 * frames, width), far[j][...].reshape(depth - 2 * frames, width)], 0)
            packed[0] = panel.reshape(devices, 2, frames, width)
            if j == 0:
                for d in range(devices):
                    at = d * 2 * frames
                    real = panel[at : at + frames].T
                    imag = panel[at + frames : at + 2 * frames].T
                    left[:width, at : at + 2 * frames] = jnp.concatenate([real, imag], 1)
                    left[width:, at : at + 2 * frames] = jnp.concatenate([imag, -real], 1)
            products(left[...], panel, scale, out)


def correlate_there_step(scale, columns, panels, left, _, out):
    depth = left.shape[1]
    products(left[...], panels[0].reshape(depth, panels.shape[-1]), scale, out)


def correlate_here(channel, near, far, columns, out, whole):
    count = len(near)
    mine, _, frames, width = near[0].shape
    devices = far[0].shape[0] + 1
    depth = devices * 2 * frames
    has_out = out is not None
    own = lambda j, cols: (0, 0, 0, 0)
    flops = 2 * count * depth * 2 * width * width
    traffic = count * (8 * width * width + 4 * depth * width)
    return pl.pallas_call(
        functools.partial(correlate_here_step, count, 1.0 / (devices * frames), has_out),
        grid_spec=pltpu.PrefetchScalarGridSpec(
            num_scalar_prefetch=1,
            grid=(count,),
            in_specs=[pl.BlockSpec((1, 2, frames, width), lambda j, cols: (channel, 0, 0, 0))] * count
            + [pl.BlockSpec(far[0].shape, own)] * count
            + [ANY] * has_out,
            out_specs=[
                pl.BlockSpec((1, 2, width, width), lambda j, cols: (channel, 0, 0, cols[j])),
                pl.BlockSpec((1, devices, 2, frames, width), lambda j, cols: (j, 0, 0, 0, 0)),
                pl.BlockSpec((2 * width, depth), lambda j, cols: (0, 0)),
            ],
        ),
        out_shape=[whole, struct((count, devices, 2, frames, width)), struct((2 * width, depth))],
        input_output_aliases={1 + 2 * count: 0} if has_out else {},
        compiler_params=pltpu.CompilerParams(vmem_limit_bytes=40 * MIB),
        cost_estimate=pl.CostEstimate(flops=flops, bytes_accessed=traffic, transcendentals=0),
        name="correlate_here",
    )(columns, *near, *far, *([out] if has_out else []))


def correlate_there(channel, panels, left, columns, out):
    count, devices, _, frames, width = panels.shape
    depth = devices * 2 * frames
    flops = 2 * count * depth * 2 * width * width
    traffic = count * (8 * width * width + 2 * depth * width)
    return pl.pallas_call(
        functools.partial(correlate_there_step, 1.0 / (devices * frames)),
        grid_spec=pltpu.PrefetchScalarGridSpec(
            num_scalar_prefetch=1,
            grid=(count,),
            in_specs=[
                pl.BlockSpec((1, devices, 2, frames, width), lambda j, cols: (j, 0, 0, 0, 0)),
                pl.BlockSpec(left.shape, lambda j, cols: (0, 0)),
                ANY,
            ],
            out_specs=pl.BlockSpec((1, 2, width, width), lambda j, cols: (channel, 0, 0, cols[j])),
        ),
        out_shape=struct(out.shape, out.dtype),
        input_output_aliases={3: 0},
        compiler_params=pltpu.CompilerParams(vmem_limit_bytes=24 * MIB),
        cost_estimate=pl.CostEstimate(flops=flops, bytes_accessed=traffic, transcendentals=0),
        name="correlate_there",
    )(columns, panels, left, out)


def step_bits(count, core):
    bits = [1 << b for b in range(1, count.bit_length() - 1)]
    return bits if core else bits[::-1]


def source_masks(count, core):
    masks = [0]
    for bit in step_bits(count, core):
        masks += [m ^ bit for m in masks]
    return masks


def gathered(block, count):
    blocks = [block]
    orders = [step_bits(count, core) for core in (0, 1)]
    for step in range(len(orders[0])):
        pairs = [(i, i ^ orders[i % 2][step]) for i in range(count)]
        blocks += [lax.ppermute(b, "inp", pairs) for b in blocks]
    return blocks


def body(voltages, fir_taps):
    _, frames, chans, width = voltages.shape
    tap_count = fir_taps.shape[0]
    devices, count = lax.axis_size("chan"), lax.axis_size("inp")
    mine = chans // devices
    plane, place = lax.axis_index("chan"), lax.axis_index("inp")

    rim = voltages[:, frames - (tap_count - 1) :].astype(jnp.bfloat16)
    rim = lax.ppermute(rim, "chan", [(i, i + 1) for i in range(devices - 1)])
    table = transform_rows(chans, GROUP + tap_count - 1)
    table = lax.dynamic_slice_in_dim(jnp.asarray(table), plane * mine, chans, 0)
    taps = jnp.tile(fir_taps, (1, 2 * (GROUP + tap_count - 1)))
    sources = np.array(
        [
            [[i ^ m for m in source_masks(count, i % 2)], [i ^ 1 ^ m for m in source_masks(count, 1 - i % 2)]]
            for i in range(count)
        ],
        np.int32,
    )
    sources = lax.dynamic_index_in_dim(jnp.asarray(sources), place, 0, keepdims=False)

    near, turning = channelize(voltages, rim, table, taps, devices)
    nears = gathered(near, count)
    whole = struct((mine, 2, width, width * count), jnp.float32)
    other_core = [(i, i ^ 1) for i in range(count)]
    out = None
    waiting = []
    for k in range(mine):
        turned = [
            lax.ppermute(turning[k][d - 1], "chan", [(i, (i + d) % devices) for i in range(devices)])
            for d in range(1, devices)
        ]
        fars = gathered(pack(turned), count)
        out, packed, left = correlate_here(k, nears, fars, sources[0], out, whole)
        waiting.append((k, lax.ppermute(packed, "inp", other_core), left))
        if k:
            then, panels, left = waiting.pop(0)
            out = correlate_there(then, panels, left, sources[1], out)
    for then, panels, left in waiting:
        out = correlate_there(then, panels, left, sources[1], out)
    return out


def solution(mesh):
    placed = (P(None, "chan", None, "inp"), P())
    return jax.shard_map(body, mesh=mesh, in_specs=placed, out_specs=P("chan", None, "inp", None), check_vma=False)
```

time: 326 us -> 171 us (0.52)
  Pallas kernels: 0 us -> 61.8 us
  other arithmetic: 61 us -> 0.94 us
  waiting for transfers between devices: 95.7 us -> 39.8 us
  blocking collectives: 52.9 us -> 0 us
  starting transfers between devices: 4.94 us -> 54 us
  matrix products: 48.6 us -> 0 us
  local copies, waits for them, and re-layouts: 48.7 us -> 11.9 us
  between operations: 13.5 us -> 0.14 us
    all_gather x1 -> x0, waiting for transfers between devices: 92.4 us -> none  [body(): piece = lax.all_gather(turned, 'inp', axis=3, tiled=True)]
    pallas_call x0 -> x13, Pallas kernels: none -> 61.8 us  [the longest x4 24.7 us: correlate_there(): pl.pallas_call(functools.partial(correlate_there_step, 1.0 / (devices * f...]
    all_to_all x1 -> x0, blocking collectives: 52.9 us -> none  [body(): lax.all_to_all(spectra, 'chan', split_axis=0, concat_axis=2, tiled=True)]
    ppermute x1 -> x32, starting transfers between devices: 4.94 us -> 54 us  [the longest x12 32.4 us: body(): lax.ppermute(turning[k][d - 1], 'chan', [(i, (i + d) % devices) for i in...]
    dot_general x6 -> x0, matrix products: 48.6 us -> none  [the longest x1 21.1 us: body(): jnp.einsum('cpsi,cpsj->cij', turned, piece, preferred_element_type=jnp.fl...]
    mul x2 -> x0, local copies, waits for them, and re-layouts: 45 us -> none  [the longest x1 44.2 us: body(): return jnp.stack([real_part, imag_part], 1) * norm_factor]
    mul x1 -> x0, other arithmetic: 43.6 us -> none  [body(): return jnp.stack([real_part, imag_part], 1) * norm_factor]
    ppermute x1 -> x32, waiting for transfers between devices: 3.29 us -> 39.8 us  [the longest x15 24.2 us: gathered(): blocks += [lax.ppermute(b, 'inp', pairs) for b in blocks]]
  transfers between devices with their start and end apart: 2 -> 32, of which waited for: 2 -> 12; matrix products, arithmetic and copies ran while one was open for 0% -> 1% of each run, Pallas kernels for 0% -> 30%
where the time goes in v1:
time: 171 us; the launch traced here: 169 us
  Pallas kernels  61.8 us (36%)
  starting transfers between devices  54 us (32%)
  waiting for transfers between devices  39.8 us (23%)
  local copies, waits for them, and re-layouts  11.9 us (7%)
    ppermute x12, starting transfers between devices, body(): lax.ppermute(turning[k][d - 1], 'chan', [(i, (i + d) % devices) for i in...  32.4 us
    pallas_call x4, Pallas kernels, correlate_there(): pl.pallas_call(functools.partial(correlate_there_step, 1.0 / (devices * f...  24.7 us
    pallas_call x4, Pallas kernels, correlate_here(): pl.pallas_call(functools.partial(correlate_here_step, count, 1.0 / (devic...  24.5 us
    ppermute x15, waiting for transfers between devices, gathered(): blocks += [lax.ppermute(b, 'inp', pairs) for b in blocks]  24.2 us
    ppermute x15, starting transfers between devices, gathered(): blocks += [lax.ppermute(b, 'inp', pairs) for b in blocks]  15.9 us
    ppermute x12, waiting for transfers between devices, body(): lax.ppermute(turning[k][d - 1], 'chan', [(i, (i + d) % devices) for i in...  15.1 us
    unnamed x52, local copies, waits for them, and re-layouts  9.52 us
    pallas_call x4, Pallas kernels, pack(): pl.pallas_call(pack_step, out_shape=struct((len(pieces),) + pieces[0].sha...  7.23 us
  transfers between devices with their start and end apart: 32, of which 12 were waited for; matrix products, arithmetic and copies ran while one was open for 1% of the time, Pallas kernels for 30%

profile of v1, /device:TPU:0, one launch (start us, length us, event | category | flops | bytes accessed | tf_op | source)
XLA Modules:
  0.0 168.6 jit_solution(12451207725531122102)
XLA Ops:
  0.0 0.9 slice_convert_fusion
  0.9 4.9 %collective-permute-start = (bf16[2,3,16,512]{3,2,1,0:T(8,128)(2,1)S(1)}, bf16[2,3,16,512]{3,2,1,0:T(8,128)(2,1)S(1)}, u32[]{:S(2)}, u32[]{:S(2)}) collective-permute-start(bf16[2,3,16,512]{3,2,1,0:T(8,128)(2,1)S(1)} %slice_convert_fusion), channel_id=1, source_target_pairs={{0,8},{8,16},{16,24},{1,9},{9,17},{17,25},{2,10},{10,18},{18,26},{... | collective-permute-start | bytes 294920 | tf_op jit(solution)/shard_map/ppermute | solution.py:237
  6.7 0.9 constant_dynamic-slice_fusion.table
  8.1 2.2 %copy-done.8 = s32[2,64,16,512]{3,2,1,0:T(8,128)S(1)} copy-done((s32[2,64,16,512]{3,2,1,0:T(8,128)S(1)}, s32[2,64,16,512]{3,2,1,0:T(8,128)}, u32[]{:S(2)}) %copy-start.8) | copy-done | bytes 4194328
  10.3 5.4 %channelize.1 = (bf16[4,2,64,512]{3,2,1,0:T(8,128)(2,1)S(1)}, bf16[2,64,512]{2,1,0:T(8,128)(2,1)S(1)}, bf16[2,64,512]{2,1,0:T(8,128)(2,1)S(1)}, bf16[2,64,512]{2...) custom-call(s32[2,64,16,512]{3,2,1,0:T(8,128)S(1)} %copy-done.8, ...), custom_call_target="tpu_custom_call" | custom-call | flops 2550136832 | bytes 6291456 | tf_op jit(solution)/shard_map/channelize/pallas_call | solution.py:81
  16.3 1.6 collective-permute-start.1
  17.9 2.4 %collective-permute-start.16 = (bf16[2,64,512]{2,1,0:T(8,128)(2,1)S(1)}, bf16[2,64,512]{2,1,0:T(8,128)(2,1)S(1)}, u32[]{:S(2)}, u32[]{:S(2)}) collective-permute-start(bf16[2,64,512]{2,1,0:T(8,128)(2,1)S(1)} %get-tuple-element.37), channel_id=1, source_target_pairs={{0,8},{8,16},{16,24},{24,0},{1,9},{9,17},{17,25},{25,1},{2,10},{10... | collective-permute-start | bytes 393224 | tf_op jit(solution)/shard_map/ppermute | solution.py:258
  20.3 2.6 %collective-permute-start.17 = (bf16[2,64,512]{2,1,0:T(8,128)(2,1)S(1)}, bf16[2,64,512]{2,1,0:T(8,128)(2,1)S(1)}, u32[]{:S(2)}, u32[]{:S(2)}) collective-permute-start(bf16[2,64,512]{2,1,0:T(8,128)(2,1)S(1)} %get-tuple-element.38), channel_id=1, source_target_pairs={{0,16},{8,24},{16,0},{24,8},{1,17},{9,25},{17,1},{25,9},{2,18},{10... | collective-permute-start | bytes 393224 | tf_op jit(solution)/shard_map/ppermute | solution.py:258
  22.9 1.3 collective-permute-start.18
  24.2 2.6 %collective-permute-done.16.refs_0_ = bf16[2,64,512]{2,1,0:T(8,128)(2,1)S(1)} collective-permute-done((bf16[2,64,512]{2,1,0:T(8,128)(2,1)S(1)}, bf16[2,64,512]{2,1,0:T(8,128)(2,1)S(1)}, u32[]{:S(2)}, u32[]{:S(2)}) %collective-permute-start.16) | collective-permute-done | bytes 131104 | tf_op jit(solution)/shard_map/ppermute | solution.py:258
  26.8 3.4 %collective-permute-done.17.refs_1_ = bf16[2,64,512]{2,1,0:T(8,128)(2,1)S(1)} collective-permute-done((bf16[2,64,512]{2,1,0:T(8,128)(2,1)S(1)}, bf16[2,64,512]{2,1,0:T(8,128)(2,1)S(1)}, u32[]{:S(2)}, u32[]{:S(2)}) %collective-permute-start.17) | collective-permute-done | bytes 131104 | tf_op jit(solution)/shard_map/ppermute | solution.py:258
  31.5 1.8 %pack.6.refs_4_ = bf16[3,2,64,512]{3,2,1,0:T(8,128)(2,1)} custom-call(bf16[2,64,512]{2,1,0:T(8,128)(2,1)} %copy-done.22, bf16[2,64,512]{2,1,0:T(8,128)(2,1)} %copy-done.24, bf16[2,64,512]{2,1,0:T(8,128)(2,1)} %copy-done.25), custom_call_target="tpu_custom_call" | custom-call | bytes 786432 | tf_op jit(solution)/shard_map/pack/pallas_call | solution.py:111
  33.3 1.4 collective-permute-start.19
  34.7 2.6 %collective-permute-start.10 = (bf16[2,64,512]{2,1,0:T(8,128)(2,1)S(1)}, bf16[2,64,512]{2,1,0:T(8,128)(2,1)S(1)}, u32[]{:S(2)}, u32[]{:S(2)}) collective-permute-start(bf16[2,64,512]{2,1,0:T(8,128)(2,1)S(1)} %get-tuple-element.34), channel_id=1, source_target_pairs={{0,8},{8,16},{16,24},{24,0},{1,9},{9,17},{17,25},{25,1},{2,10},{10... | collective-permute-start | bytes 393224 | tf_op jit(solution)/shard_map/ppermute | solution.py:258
  37.4 2.3 %collective-permute-start.11 = (bf16[2,64,512]{2,1,0:T(8,128)(2,1)S(1)}, bf16[2,64,512]{2,1,0:T(8,128)(2,1)S(1)}, u32[]{:S(2)}, u32[]{:S(2)}) collective-permute-start(bf16[2,64,512]{2,1,0:T(8,128)(2,1)S(1)} %get-tuple-element.35), channel_id=1, source_target_pairs={{0,16},{8,24},{16,0},{24,8},{1,17},{9,25},{17,1},{25,9},{2,18},{10... | collective-permute-start | bytes 393224 | tf_op jit(solution)/shard_map/ppermute | solution.py:258
  39.8 3.5 %collective-permute-done.10.refs_0_ = bf16[2,64,512]{2,1,0:T(8,128)(2,1)S(1)} collective-permute-done((bf16[2,64,512]{2,1,0:T(8,128)(2,1)S(1)}, bf16[2,64,512]{2,1,0:T(8,128)(2,1)S(1)}, u32[]{:S(2)}, u32[]{:S(2)}) %collective-permute-start.10) | collective-permute-done | bytes 131104 | tf_op jit(solution)/shard_map/ppermute | solution.py:258
  44.1 1.2 collective-permute-start.3
  45.3 1.6 collective-permute-done.11.refs_1_
  46.9 0.9 collective-permute-start.20
  48.5 1.8 %pack.5.refs_4_ = bf16[3,2,64,512]{3,2,1,0:T(8,128)(2,1)} custom-call(bf16[2,64,512]{2,1,0:T(8,128)(2,1)} %copy-done.17, bf16[2,64,512]{2,1,0:T(8,128)(2,1)} %copy-done.18, bf16[2,64,512]{2,1,0:T(8,128)(2,1)} %copy-done.19), custom_call_target="tpu_custom_call" | custom-call | bytes 786432 | tf_op jit(solution)/shard_map/pack/pallas_call | solution.py:111
  50.3 1.4 collective-permute-start.13
  53.1 13.5 %collective-permute-done.20.refs_6_ = bf16[3,2,64,512]{3,2,1,0:T(8,128)(2,1)} collective-permute-done((bf16[3,2,64,512]{3,2,1,0:T(8,128)(2,1)}, bf16[3,2,64,512]{3,2,1,0:T(8,128)(2,1)}, u32[]{:S(2)}, u32[]{:S(2)}) %collective-permute-start.20) | collective-permute-done | bytes 393248 | tf_op jit(solution)/shard_map/ppermute | solution.py:225
  67.4 1.2 collective-permute-start.15
  68.6 2.2 %collective-permute-done.21.refs_7_ = bf16[3,2,64,512]{3,2,1,0:T(8,128)(2,1)} collective-permute-done((bf16[3,2,64,512]{3,2,1,0:T(8,128)(2,1)S(1)}, bf16[3,2,64,512]{3,2,1,0:T(8,128)(2,1)}, u32[]{:S(2)}, u32[]{:S(2)}) %collective-permute-start.21) | collective-permute-done | bytes 393248 | tf_op jit(solution)/shard_map/ppermute | solution.py:225
  70.8 1.0 copy-done.7
  71.8 7.2 %correlate_here.4 = (f32[4,2,512,4096]{3,2,1,0:T(8,128)}, bf16[4,4,2,64,512]{4,3,2,1,0:T(8,128)(2,1)}, bf16[1024,512]{1,0:T(8,128)(2,1)S(1)}) custom-call(s32[4]{0:T(128)S(1)} %get-tuple-element.55.columns, bf16[4,2,64,512]{3,2,1,0:T(8,128)(2,1)S(1)} %get-tuple-element.30.refs_0_, bf16[4,2,64,512]{3,2,1,0:T(8,128)(2,1)S(1)} %collective-permute-done.1.refs_1_, ...), custom_call_target="tpu_custom_call" | custom-call | flops 2147483648 | bytes 12582912 | tf_op jit(solution)/shard_map/correlate_here/pallas_call | solution.py:161
  79.1 1.3 copy-done.6
  80.4 6.1 %correlate_here.5 = (f32[4,2,512,4096]{3,2,1,0:T(8,128)}, bf16[4,4,2,64,512]{4,3,2,1,0:T(8,128)(2,1)}, bf16[1024,512]{1,0:T(8,128)(2,1)S(1)}) custom-call(s32[4]{0:T(128)S(1)} %get-tuple-element.55.columns, bf16[4,2,64,512]{3,2,1,0:T(8,128)(2,1)S(1)} %get-tuple-element.30.refs_0_, ...), custom_call_target="tpu_custom_call", output_to_operand_aliasing={{0}: (9, {})} | custom-call | flops 2147483648 | bytes 12582912 | tf_op jit(solution)/shard_map/correlate_here/pallas_call | solution.py:161
  87.2 4.3 %collective-permute-start.24 = (bf16[2,64,512]{2,1,0:T(8,128)(2,1)S(1)}, bf16[2,64,512]{2,1,0:T(8,128)(2,1)S(1)}, u32[]{:S(2)}, u32[]{:S(2)}) collective-permute-start(bf16[2,64,512]{2,1,0:T(8,128)(2,1)S(1)} %copy-done.14), channel_id=1, source_target_pairs={{0,16},{8,24},{16,0},{24,8},{1,17},{9,25},{17,1},{25,9},{2,18},{10... | collective-permute-start | bytes 393224 | tf_op jit(solution)/shard_map/ppermute | solution.py:258
  91.5 2.9 %collective-permute-start.25 = (bf16[2,64,512]{2,1,0:T(8,128)(2,1)S(1)}, bf16[2,64,512]{2,1,0:T(8,128)(2,1)S(1)}, u32[]{:S(2)}, u32[]{:S(2)}) collective-permute-start(bf16[2,64,512]{2,1,0:T(8,128)(2,1)S(1)} %copy-done.12), channel_id=1, source_target_pairs={{0,24},{8,0},{16,8},{24,16},{1,25},{9,1},{17,9},{25,17},{2,26},{10... | collective-permute-start | bytes 393224 | tf_op jit(solution)/shard_map/ppermute | solution.py:258
  94.4 7.1 %collective-permute-start.4 = (bf16[2,64,512]{2,1,0:T(8,128)(2,1)}, bf16[2,64,512]{2,1,0:T(8,128)(2,1)}, u32[]{:S(2)}, u32[]{:S(2)}) collective-permute-start(bf16[2,64,512]{2,1,0:T(8,128)(2,1)} %get-tuple-element.31), channel_id=1, source_target_pairs={{0,8},{8,16},{16,24},{24,0},{1,9},{9,17},{17,25},{25,1},{2,10},{10... | collective-permute-start | bytes 393224 | tf_op jit(solution)/shard_map/ppermute | solution.py:258
  102.8 1.8 %pack.7.refs_4_ = bf16[3,2,64,512]{3,2,1,0:T(8,128)(2,1)} custom-call(bf16[2,64,512]{2,1,0:T(8,128)(2,1)} %copy-done.20, bf16[2,64,512]{2,1,0:T(8,128)(2,1)} %copy-done.21, bf16[2,64,512]{2,1,0:T(8,128)(2,1)} %copy-done.23), custom_call_target="tpu_custom_call" | custom-call | bytes 786432 | tf_op jit(solution)/shard_map/pack/pallas_call | solution.py:111
  104.6 2.8 %collective-permute-start.5 = (bf16[2,64,512]{2,1,0:T(8,128)(2,1)}, bf16[2,64,512]{2,1,0:T(8,128)(2,1)}, u32[]{:S(2)}, u32[]{:S(2)}) collective-permute-start(bf16[2,64,512]{2,1,0:T(8,128)(2,1)} %copy-done.10), channel_id=1, source_target_pairs={{0,16},{8,24},{16,0},{24,8},{1,17},{9,25},{17,1},{25,9},{2,18},{10... | collective-permute-start | bytes 393224 | tf_op jit(solution)/shard_map/ppermute | solution.py:258
  107.5 3.4 %collective-permute-start.6 = (bf16[2,64,512]{2,1,0:T(8,128)(2,1)}, bf16[2,64,512]{2,1,0:T(8,128)(2,1)}, u32[]{:S(2)}, u32[]{:S(2)}) collective-permute-start(bf16[2,64,512]{2,1,0:T(8,128)(2,1)} %copy-done.9), channel_id=1, source_target_pairs={{0,24},{8,0},{16,8},{24,16},{1,25},{9,1},{17,9},{25,17},{2,26},{10... | collective-permute-start | bytes 393224 | tf_op jit(solution)/shard_map/ppermute | solution.py:258
  110.8 1.4 collective-permute-done.5.refs_1_
  112.2 2.7 %collective-permute-done.6.refs_2_ = bf16[2,64,512]{2,1,0:T(8,128)(2,1)} collective-permute-done((bf16[2,64,512]{2,1,0:T(8,128)(2,1)}, bf16[2,64,512]{2,1,0:T(8,128)(2,1)}, u32[]{:S(2)}, u32[]{:S(2)}) %collective-permute-start.6) | collective-permute-done | bytes 131104 | tf_op jit(solution)/shard_map/ppermute | solution.py:258
  114.9 1.8 %pack.4.refs_4_ = bf16[3,2,64,512]{3,2,1,0:T(8,128)(2,1)} custom-call(bf16[2,64,512]{2,1,0:T(8,128)(2,1)} %collective-permute-done.4.refs_0_, bf16[2,64,512]{2,1,0:T(8,128)(2,1)} %collective-permute-done.5.refs_1_, bf16[2,64,512]{2,1,0:T(8,128)(2,1)} %collective-permute-done.6.refs_2_), custom_call_target="tpu_custom_call" | custom-call | bytes 786432 | tf_op jit(solution)/shard_map/pack/pallas_call | solution.py:111
  116.7 1.7 %collective-permute-start.7 = (bf16[3,2,64,512]{3,2,1,0:T(8,128)(2,1)}, bf16[3,2,64,512]{3,2,1,0:T(8,128)(2,1)S(1)}, u32[]{:S(2)}, u32[]{:S(2)}) collective-permute-start(bf16[3,2,64,512]{3,2,1,0:T(8,128)(2,1)} %pack.4.refs_4_), channel_id=1, source_target_pairs={{0,4},{1,3},{2,6},{3,1},{4,0},{5,7},{6,2},{7,5},{8,12},{9,11},{10,... | collective-permute-start | bytes 1179656 | tf_op jit(solution)/shard_map/ppermute | solution.py:225
  119.3 1.2 collective-permute-start.28
  120.5 8.4 %collective-permute-done.7.refs_5_ = bf16[3,2,64,512]{3,2,1,0:T(8,128)(2,1)S(1)} collective-permute-done((bf16[3,2,64,512]{3,2,1,0:T(8,128)(2,1)}, bf16[3,2,64,512]{3,2,1,0:T(8,128)(2,1)S(1)}, u32[]{:S(2)}, u32[]{:S(2)}) %collective-permute-start.7) | collective-permute-done | bytes 393248 | tf_op jit(solution)/shard_map/ppermute | solution.py:225
  129.8 1.1 collective-permute-start.9
  130.9 1.2 copy-done.4
  132.1 7.0 %correlate_there.4.refs_8_ = f32[4,2,512,4096]{3,2,1,0:T(8,128)} custom-call(s32[4]{0:T(128)S(1)} %get-tuple-element.56.columns, bf16[4,4,2,64,512]{4,3,2,1,0:T(8,128)(2,1)} %collective-permute-done.29.panels, bf16[1024,512]{1,0:T(8,128)(2,1)S(1)} %copy-done.4, f32[4,2,512,4096]{3,2,1,0:T(8,128)} %get-tuple-element.48._), custom_call_target="tpu_custom_call", output_to_operand_aliasing={{}: (3, {})} | custom-call | flops 2147483648 | bytes 10485760 | tf_op jit(solution)/shard_map/correlate_there/pallas_call | solution.py:188
  139.2 5.6 %correlate_here.6 = (f32[4,2,512,4096]{3,2,1,0:T(8,128)}, bf16[4,4,2,64,512]{4,3,2,1,0:T(8,128)(2,1)S(1)}, bf16[1024,512]{1,0:T(8,128)(2,1)S(1)}) custom-call(s32[4]{0:T(128)S(1)} %get-tuple-element.55.columns, bf16[4,2,64,512]{3,2,1,0:T(8,128)(2,1)S(1)} %get-tuple-element.30.refs_0_, ...), custom_call_target="tpu_custom_call", output_to_operand_aliasing={{0}: (9, {})} | custom-call | flops 2147483648 | bytes 12582912 | tf_op jit(solution)/shard_map/correlate_here/pallas_call | solution.py:161
  144.8 7.0 %correlate_there.5.refs_8_ = f32[4,2,512,4096]{3,2,1,0:T(8,128)} custom-call(s32[4]{0:T(128)S(1)} %get-tuple-element.56.columns, bf16[4,4,2,64,512]{4,3,2,1,0:T(8,128)(2,1)} %collective-permute-done.22.panels, bf16[1024,512]{1,0:T(8,128)(2,1)S(1)} %get-tuple-element.42.left, f32[4,2,512,4096]{3,2,1,0:T(8,128)} %get-tuple-element.49._), custom_call_target="tpu_custom_call", output_to_operand_aliasing={{}: (3, {})} | custom-call | flops 2147483648 | bytes 10485760 | tf_op jit(solution)/shard_map/correlate_there/pallas_call | solution.py:188
  151.8 5.6 %correlate_here.7 = (f32[4,2,512,4096]{3,2,1,0:T(8,128)}, bf16[4,4,2,64,512]{4,3,2,1,0:T(8,128)(2,1)S(1)}, bf16[1024,512]{1,0:T(8,128)(2,1)S(1)}) custom-call(s32[4]{0:T(128)S(1)} %get-tuple-element.55.columns, bf16[4,2,64,512]{3,2,1,0:T(8,128)(2,1)S(1)} %get-tuple-element.30.refs_0_, ...), custom_call_target="tpu_custom_call", output_to_operand_aliasing={{0}: (9, {})} | custom-call | flops 2147483648 | bytes 12582912 | tf_op jit(solution)/shard_map/correlate_here/pallas_call | solution.py:161
  157.9 5.3 %correlate_there.6._ = f32[4,2,512,4096]{3,2,1,0:T(8,128)} custom-call(s32[4]{0:T(128)S(1)} %get-tuple-element.56.columns, bf16[4,4,2,64,512]{4,3,2,1,0:T(8,128)(2,1)S(1)} %collective-permute-done.31.panels, bf16[1024,512]{1,0:T(8,128)(2,1)S(1)} %get-tuple-element.53.left, f32[4,2,512,4096]{3,2,1,0:T(8,128)} %get-tuple-element.54._), custom_call_target="tpu_custom_call", output_to_operand_aliasing={{}: (3, {})} | custom-call | flops 2147483648 | bytes 10485760 | tf_op jit(solution)/shard_map/correlate_there/pallas_call | solution.py:188
  163.3 5.3 %correlate_there.7 = f32[4,2,512,4096]{3,2,1,0:T(8,128)} custom-call(s32[4]{0:T(128)S(1)} %get-tuple-element.56.columns, bf16[4,4,2,64,512]{4,3,2,1,0:T(8,128)(2,1)S(1)} %collective-permute-done.30.panels, bf16[1024,512]{1,0:T(8,128)(2,1)S(1)} %get-tuple-element.51.left, f32[4,2,512,4096]{3,2,1,0:T(8,128)} %correlate_there.6._), custom_call_target="tpu_custom_call", output_to_operand_aliasing={{}: (3, {})} | custom-call | flops 2147483648 | bytes 10485760 | tf_op jit(solution)/shard_map/correlate_there/pallas_call | solution.py:188
  (87 shorter events, 11.5 us)
Async XLA Ops:
  0.9 7.1 %collective-permute-start = (bf16[2,3,16,512]{3,2,1,0:T(8,128)(2,1)S(1)}, bf16[2,3,16,512]{3,2,1,0:T(8,128)(2,1)S(1)}, u32[]{:S(2)}, u32[]{:S(2)}) collective-permute-start(bf16[2,3,16,512]{3,2,1,0:T(8,128)(2,1)S(1)} %slice_convert_fusion), channel_id=1, source_target_pairs={{0,8},{8,16},{16,24},{1,9},{9,17},{17,25},{2,10},{10,18},{18,26},{... | collective-permute-start | bytes 294920 | tf_op jit(solution)/shard_map/ppermute | solution.py:237
  8.1 2.2 %copy-start.8 = (s32[2,64,16,512]{3,2,1,0:T(8,128)S(1)}, s32[2,64,16,512]{3,2,1,0:T(8,128)}, u32[]{:S(2)}) copy-start(s32[2,64,16,512]{3,2,1,0:T(8,128)} %volts.1) | copy-start | bytes 12582916
  16.3 23.4 %copy-start.10 = (bf16[2,64,512]{2,1,0:T(8,128)(2,1)}, bf16[2,64,512]{2,1,0:T(8,128)(2,1)S(1)}, u32[]{:S(2)}) copy-start(bf16[2,64,512]{2,1,0:T(8,128)(2,1)S(1)} %get-tuple-element.32) | copy-start | bytes 393220
  16.3 23.4 %copy-start.13 = (bf16[2,64,512]{2,1,0:T(8,128)(2,1)}, bf16[2,64,512]{2,1,0:T(8,128)(2,1)S(1)}, u32[]{:S(2)}) copy-start(bf16[2,64,512]{2,1,0:T(8,128)(2,1)S(1)} %get-tuple-element.44) | copy-start | bytes 393220
  16.3 27.8 %copy-start.9 = (bf16[2,64,512]{2,1,0:T(8,128)(2,1)}, bf16[2,64,512]{2,1,0:T(8,128)(2,1)S(1)}, u32[]{:S(2)}) copy-start(bf16[2,64,512]{2,1,0:T(8,128)(2,1)S(1)} %get-tuple-element.33) | copy-start | bytes 393220
  16.3 27.8 %copy-start.11 = (bf16[2,64,512]{2,1,0:T(8,128)(2,1)}, bf16[2,64,512]{2,1,0:T(8,128)(2,1)S(1)}, u32[]{:S(2)}) copy-start(bf16[2,64,512]{2,1,0:T(8,128)(2,1)S(1)} %get-tuple-element.45) | copy-start | bytes 393220
  16.3 27.8 %collective-permute-start.1 = (bf16[4,2,64,512]{3,2,1,0:T(8,128)(2,1)S(1)}, bf16[4,2,64,512]{3,2,1,0:T(8,128)(2,1)S(1)}, u32[]{:S(2)}, u32[]{:S(2)}) collective-permute-start(bf16[4,2,64,512]{3,2,1,0:T(8,128)(2,1)S(1)} %get-tuple-element.30.refs_0_), channel_id=1, source_target_pairs={{0,4},{1,3},{2,6},{3,1},{4,0},{5,7},{6,2},{7,5},{8,12},{9,11},{10,... | collective-permute-start | bytes 1572872 | tf_op jit(solution)/shard_map/ppermute | solution.py:225
  17.9 8.9 %collective-permute-start.16 = (bf16[2,64,512]{2,1,0:T(8,128)(2,1)S(1)}, bf16[2,64,512]{2,1,0:T(8,128)(2,1)S(1)}, u32[]{:S(2)}, u32[]{:S(2)}) collective-permute-start(bf16[2,64,512]{2,1,0:T(8,128)(2,1)S(1)} %get-tuple-element.37), channel_id=1, source_target_pairs={{0,8},{8,16},{16,24},{24,0},{1,9},{9,17},{17,25},{25,1},{2,10},{10... | collective-permute-start | bytes 393224 | tf_op jit(solution)/shard_map/ppermute | solution.py:258
  20.3 9.9 %collective-permute-start.17 = (bf16[2,64,512]{2,1,0:T(8,128)(2,1)S(1)}, bf16[2,64,512]{2,1,0:T(8,128)(2,1)S(1)}, u32[]{:S(2)}, u32[]{:S(2)}) collective-permute-start(bf16[2,64,512]{2,1,0:T(8,128)(2,1)S(1)} %get-tuple-element.38), channel_id=1, source_target_pairs={{0,16},{8,24},{16,0},{24,8},{1,17},{9,25},{17,1},{25,9},{2,18},{10... | collective-permute-start | bytes 393224 | tf_op jit(solution)/shard_map/ppermute | solution.py:258
  22.9 7.3 %collective-permute-start.18 = (bf16[2,64,512]{2,1,0:T(8,128)(2,1)S(1)}, bf16[2,64,512]{2,1,0:T(8,128)(2,1)S(1)}, u32[]{:S(2)}, u32[]{:S(2)}) collective-permute-start(bf16[2,64,512]{2,1,0:T(8,128)(2,1)S(1)} %get-tuple-element.39), channel_id=1, source_target_pairs={{0,24},{8,0},{16,8},{24,16},{1,25},{9,1},{17,9},{25,17},{2,26},{10... | collective-permute-start | bytes 393224 | tf_op jit(solution)/shard_map/ppermute | solution.py:258
  26.8 3.4 %copy-start.22 = (bf16[2,64,512]{2,1,0:T(8,128)(2,1)}, bf16[2,64,512]{2,1,0:T(8,128)(2,1)S(1)}, u32[]{:S(2)}) copy-start(bf16[2,64,512]{2,1,0:T(8,128)(2,1)S(1)} %collective-permute-done.16.refs_0_) | copy-start | bytes 393220
  33.3 18.5 %collective-permute-start.19 = (bf16[3,2,64,512]{3,2,1,0:T(8,128)(2,1)}, bf16[3,2,64,512]{3,2,1,0:T(8,128)(2,1)S(1)}, u32[]{:S(2)}, u32[]{:S(2)}) collective-permute-start(bf16[3,2,64,512]{3,2,1,0:T(8,128)(2,1)} %pack.6.refs_4_), channel_id=1, source_target_pairs={{0,4},{1,3},{2,6},{3,1},{4,0},{5,7},{6,2},{7,5},{8,12},{9,11},{10,... | collective-permute-start | bytes 1179656 | tf_op jit(solution)/shard_map/ppermute | solution.py:225
  34.7 8.5 %collective-permute-start.10 = (bf16[2,64,512]{2,1,0:T(8,128)(2,1)S(1)}, bf16[2,64,512]{2,1,0:T(8,128)(2,1)S(1)}, u32[]{:S(2)}, u32[]{:S(2)}) collective-permute-start(bf16[2,64,512]{2,1,0:T(8,128)(2,1)S(1)} %get-tuple-element.34), channel_id=1, source_target_pairs={{0,8},{8,16},{16,24},{24,0},{1,9},{9,17},{17,25},{25,1},{2,10},{10... | collective-permute-start | bytes 393224 | tf_op jit(solution)/shard_map/ppermute | solution.py:258
  37.4 9.6 %collective-permute-start.11 = (bf16[2,64,512]{2,1,0:T(8,128)(2,1)S(1)}, bf16[2,64,512]{2,1,0:T(8,128)(2,1)S(1)}, u32[]{:S(2)}, u32[]{:S(2)}) collective-permute-start(bf16[2,64,512]{2,1,0:T(8,128)(2,1)S(1)} %get-tuple-element.35), channel_id=1, source_target_pairs={{0,16},{8,24},{16,0},{24,8},{1,17},{9,25},{17,1},{25,9},{2,18},{10... | collective-permute-start | bytes 393224 | tf_op jit(solution)/shard_map/ppermute | solution.py:258
  39.6 8.2 %collective-permute-start.12 = (bf16[2,64,512]{2,1,0:T(8,128)(2,1)S(1)}, bf16[2,64,512]{2,1,0:T(8,128)(2,1)S(1)}, u32[]{:S(2)}, u32[]{:S(2)}) collective-permute-start(bf16[2,64,512]{2,1,0:T(8,128)(2,1)S(1)} %get-tuple-element.36), channel_id=1, source_target_pairs={{0,24},{8,0},{16,8},{24,16},{1,25},{9,1},{17,9},{25,17},{2,26},{10... | collective-permute-start | bytes 393224 | tf_op jit(solution)/shard_map/ppermute | solution.py:258
  43.2 4.7 %copy-start.17 = (bf16[2,64,512]{2,1,0:T(8,128)(2,1)}, bf16[2,64,512]{2,1,0:T(8,128)(2,1)S(1)}, u32[]{:S(2)}) copy-start(bf16[2,64,512]{2,1,0:T(8,128)(2,1)S(1)} %collective-permute-done.10.refs_0_) | copy-start | bytes 393220
  43.2 25.4 %collective-permute-start.2 = (bf16[4,2,64,512]{3,2,1,0:T(8,128)(2,1)S(1)}, bf16[4,2,64,512]{3,2,1,0:T(8,128)(2,1)S(1)}, u32[]{:S(2)}, u32[]{:S(2)}) collective-permute-start(bf16[4,2,64,512]{3,2,1,0:T(8,128)(2,1)S(1)} %get-tuple-element.30.refs_0_), channel_id=1, source_target_pairs={{0,2},{1,5},{2,0},{3,7},{4,6},{5,1},{6,4},{7,3},{8,10},{9,13},{10,... | collective-permute-start | bytes 1572872 | tf_op jit(solution)/shard_map/ppermute | solution.py:225
  44.1 26.7 %collective-permute-start.3 = (bf16[4,2,64,512]{3,2,1,0:T(8,128)(2,1)S(1)}, bf16[4,2,64,512]{3,2,1,0:T(8,128)(2,1)S(1)}, u32[]{:S(2)}, u32[]{:S(2)}) collective-permute-start(bf16[4,2,64,512]{3,2,1,0:T(8,128)(2,1)S(1)} %collective-permute-done.1.refs_1_), channel_id=1, source_target_pairs={{0,2},{1,5},{2,0},{3,7},{4,6},{5,1},{6,4},{7,3},{8,10},{9,13},{10,... | collective-permute-start | bytes 1572872 | tf_op jit(solution)/shard_map/ppermute | solution.py:225
  46.9 19.6 %collective-permute-start.20 = (bf16[3,2,64,512]{3,2,1,0:T(8,128)(2,1)}, bf16[3,2,64,512]{3,2,1,0:T(8,128)(2,1)}, u32[]{:S(2)}, u32[]{:S(2)}) collective-permute-start(bf16[3,2,64,512]{3,2,1,0:T(8,128)(2,1)} %pack.6.refs_4_), channel_id=1, source_target_pairs={{0,2},{1,5},{2,0},{3,7},{4,6},{5,1},{6,4},{7,3},{8,10},{9,13},{10,... | collective-permute-start | bytes 1179656 | tf_op jit(solution)/shard_map/ppermute | solution.py:225
  50.3 28.8 %copy-start.1 = (bf16[3,2,64,512]{3,2,1,0:T(8,128)(2,1)S(1)}, bf16[3,2,64,512]{3,2,1,0:T(8,128)(2,1)}, u32[]{:S(2)}) copy-start(bf16[3,2,64,512]{3,2,1,0:T(8,128)(2,1)} %pack.5.refs_4_) | copy-start | bytes 1179652
  50.3 17.1 %collective-permute-start.13 = (bf16[3,2,64,512]{3,2,1,0:T(8,128)(2,1)}, bf16[3,2,64,512]{3,2,1,0:T(8,128)(2,1)S(1)}, u32[]{:S(2)}, u32[]{:S(2)}) collective-permute-start(bf16[3,2,64,512]{3,2,1,0:T(8,128)(2,1)} %pack.5.refs_4_), channel_id=1, source_target_pairs={{0,4},{1,3},{2,6},{3,1},{4,0},{5,7},{6,2},{7,5},{8,12},{9,11},{10,... | collective-permute-start | bytes 1179656 | tf_op jit(solution)/shard_map/ppermute | solution.py:225
  51.8 19.0 %collective-permute-start.21 = (bf16[3,2,64,512]{3,2,1,0:T(8,128)(2,1)S(1)}, bf16[3,2,64,512]{3,2,1,0:T(8,128)(2,1)}, u32[]{:S(2)}, u32[]{:S(2)}) collective-permute-start(bf16[3,2,64,512]{3,2,1,0:T(8,128)(2,1)S(1)} %collective-permute-done.19.refs_5_), channel_id=1, source_target_pairs={{0,2},{1,5},{2,0},{3,7},{4,6},{5,1},{6,4},{7,3},{8,10},{9,13},{10,... | collective-permute-start | bytes 1179656 | tf_op jit(solution)/shard_map/ppermute | solution.py:225
  66.6 12.4 %collective-permute-start.14 = (bf16[3,2,64,512]{3,2,1,0:T(8,128)(2,1)}, bf16[3,2,64,512]{3,2,1,0:T(8,128)(2,1)S(1)}, u32[]{:S(2)}, u32[]{:S(2)}) collective-permute-start(bf16[3,2,64,512]{3,2,1,0:T(8,128)(2,1)} %pack.5.refs_4_), channel_id=1, source_target_pairs={{0,2},{1,5},{2,0},{3,7},{4,6},{5,1},{6,4},{7,3},{8,10},{9,13},{10,... | collective-permute-start | bytes 1179656 | tf_op jit(solution)/shard_map/ppermute | solution.py:225
  67.4 11.7 %copy-start.5 = (bf16[3,2,64,512]{3,2,1,0:T(8,128)(2,1)}, bf16[3,2,64,512]{3,2,1,0:T(8,128)(2,1)S(1)}, u32[]{:S(2)}) copy-start(bf16[3,2,64,512]{3,2,1,0:T(8,128)(2,1)S(1)} %collective-permute-done.13.refs_5_) | copy-start | bytes 1179652
  67.4 11.7 %collective-permute-start.15 = (bf16[3,2,64,512]{3,2,1,0:T(8,128)(2,1)S(1)}, bf16[3,2,64,512]{3,2,1,0:T(8,128)(2,1)S(1)}, u32[]{:S(2)}, u32[]{:S(2)}) collective-permute-start(bf16[3,2,64,512]{3,2,1,0:T(8,128)(2,1)S(1)} %collective-permute-done.13.refs_5_), channel_id=1, source_target_pairs={{0,2},{1,5},{2,0},{3,7},{4,6},{5,1},{6,4},{7,3},{8,10},{9,13},{10,... | collective-permute-start | bytes 1179656 | tf_op jit(solution)/shard_map/ppermute | solution.py:225
  79.0 7.5 %copy-start.3 = (bf16[1024,512]{1,0:T(8,128)(2,1)}, bf16[1024,512]{1,0:T(8,128)(2,1)S(1)}, u32[]{:S(2)}) copy-start(bf16[1024,512]{1,0:T(8,128)(2,1)S(1)} %get-tuple-element.47.left) | copy-start | bytes 3145732
  79.0 50.8 %collective-permute-start.29 = (bf16[4,4,2,64,512]{4,3,2,1,0:T(8,128)(2,1)}, bf16[4,4,2,64,512]{4,3,2,1,0:T(8,128)(2,1)}, u32[]{:S(2)}, u32[]{:S(2)}) collective-permute-start(bf16[4,4,2,64,512]{4,3,2,1,0:T(8,128)(2,1)} %get-tuple-element.46), channel_id=1, source_target_pairs={{0,1},{1,0},{2,3},{3,2},{4,5},{5,4},{6,7},{7,6},{8,9},{9,8},{10,11... | collective-permute-start | bytes 6291464 | tf_op jit(solution)/shard_map/ppermute | solution.py:263
  80.4 6.2 %copy-start.16 = (bf16[2,64,512]{2,1,0:T(8,128)(2,1)S(1)}, bf16[2,64,512]{2,1,0:T(8,128)(2,1)}, u32[]{:S(2)}) copy-start(bf16[2,64,512]{2,1,0:T(8,128)(2,1)} %copy-done.15) | copy-start | bytes 393220
  80.4 6.8 %copy-start.14 = (bf16[2,64,512]{2,1,0:T(8,128)(2,1)S(1)}, bf16[2,64,512]{2,1,0:T(8,128)(2,1)}, u32[]{:S(2)}) copy-start(bf16[2,64,512]{2,1,0:T(8,128)(2,1)} %copy-done.13) | copy-start | bytes 393220
  80.4 11.2 %copy-start.12 = (bf16[2,64,512]{2,1,0:T(8,128)(2,1)S(1)}, bf16[2,64,512]{2,1,0:T(8,128)(2,1)}, u32[]{:S(2)}) copy-start(bf16[2,64,512]{2,1,0:T(8,128)(2,1)} %copy-done.11) | copy-start | bytes 393220
  86.4 58.3 %collective-permute-start.22 = (bf16[4,4,2,64,512]{4,3,2,1,0:T(8,128)(2,1)}, bf16[4,4,2,64,512]{4,3,2,1,0:T(8,128)(2,1)}, u32[]{:S(2)}, u32[]{:S(2)}) collective-permute-start(bf16[4,4,2,64,512]{4,3,2,1,0:T(8,128)(2,1)} %get-tuple-element.41), channel_id=1, source_target_pairs={{0,1},{1,0},{2,3},{3,2},{4,5},{5,4},{6,7},{7,6},{8,9},{9,8},{10,11... | collective-permute-start | bytes 6291464 | tf_op jit(solution)/shard_map/ppermute | solution.py:263
  86.6 7.8 %collective-permute-start.23 = (bf16[2,64,512]{2,1,0:T(8,128)(2,1)S(1)}, bf16[2,64,512]{2,1,0:T(8,128)(2,1)S(1)}, u32[]{:S(2)}, u32[]{:S(2)}) collective-permute-start(bf16[2,64,512]{2,1,0:T(8,128)(2,1)S(1)} %copy-done.16), channel_id=1, source_target_pairs={{0,8},{8,16},{16,24},{24,0},{1,9},{9,17},{17,25},{25,1},{2,10},{10... | collective-permute-start | bytes 393224 | tf_op jit(solution)/shard_map/ppermute | solution.py:258
  87.2 14.3 %collective-permute-start.24 = (bf16[2,64,512]{2,1,0:T(8,128)(2,1)S(1)}, bf16[2,64,512]{2,1,0:T(8,128)(2,1)S(1)}, u32[]{:S(2)}, u32[]{:S(2)}) collective-permute-start(bf16[2,64,512]{2,1,0:T(8,128)(2,1)S(1)} %copy-done.14), channel_id=1, source_target_pairs={{0,16},{8,24},{16,0},{24,8},{1,17},{9,25},{17,1},{25,9},{2,18},{10... | collective-permute-start | bytes 393224 | tf_op jit(solution)/shard_map/ppermute | solution.py:258
  91.5 10.0 %collective-permute-start.25 = (bf16[2,64,512]{2,1,0:T(8,128)(2,1)S(1)}, bf16[2,64,512]{2,1,0:T(8,128)(2,1)S(1)}, u32[]{:S(2)}, u32[]{:S(2)}) collective-permute-start(bf16[2,64,512]{2,1,0:T(8,128)(2,1)S(1)} %copy-done.12), channel_id=1, source_target_pairs={{0,24},{8,0},{16,8},{24,16},{1,25},{9,1},{17,9},{25,17},{2,26},{10... | collective-permute-start | bytes 393224 | tf_op jit(solution)/shard_map/ppermute | solution.py:258
  94.4 7.1 %copy-start.20 = (bf16[2,64,512]{2,1,0:T(8,128)(2,1)}, bf16[2,64,512]{2,1,0:T(8,128)(2,1)S(1)}, u32[]{:S(2)}) copy-start(bf16[2,64,512]{2,1,0:T(8,128)(2,1)S(1)} %collective-permute-done.23.refs_0_) | copy-start | bytes 393220
  94.4 13.1 %collective-permute-start.4 = (bf16[2,64,512]{2,1,0:T(8,128)(2,1)}, bf16[2,64,512]{2,1,0:T(8,128)(2,1)}, u32[]{:S(2)}, u32[]{:S(2)}) collective-permute-start(bf16[2,64,512]{2,1,0:T(8,128)(2,1)} %get-tuple-element.31), channel_id=1, source_target_pairs={{0,8},{8,16},{16,24},{24,0},{1,9},{9,17},{17,25},{25,1},{2,10},{10... | collective-permute-start | bytes 393224 | tf_op jit(solution)/shard_map/ppermute | solution.py:258
  104.6 14.7 %collective-permute-start.26 = (bf16[3,2,64,512]{3,2,1,0:T(8,128)(2,1)}, bf16[3,2,64,512]{3,2,1,0:T(8,128)(2,1)S(1)}, u32[]{:S(2)}, u32[]{:S(2)}) collective-permute-start(bf16[3,2,64,512]{3,2,1,0:T(8,128)(2,1)} %pack.7.refs_4_), channel_id=1, source_target_pairs={{0,4},{1,3},{2,6},{3,1},{4,0},{5,7},{6,2},{7,5},{8,12},{9,11},{10,... | collective-permute-start | bytes 1179656 | tf_op jit(solution)/shard_map/ppermute | solution.py:225
  104.6 7.6 %collective-permute-start.5 = (bf16[2,64,512]{2,1,0:T(8,128)(2,1)}, bf16[2,64,512]{2,1,0:T(8,128)(2,1)}, u32[]{:S(2)}, u32[]{:S(2)}) collective-permute-start(bf16[2,64,512]{2,1,0:T(8,128)(2,1)} %copy-done.10), channel_id=1, source_target_pairs={{0,16},{8,24},{16,0},{24,8},{1,17},{9,25},{17,1},{25,9},{2,18},{10... | collective-permute-start | bytes 393224 | tf_op jit(solution)/shard_map/ppermute | solution.py:258
  107.5 7.4 %collective-permute-start.6 = (bf16[2,64,512]{2,1,0:T(8,128)(2,1)}, bf16[2,64,512]{2,1,0:T(8,128)(2,1)}, u32[]{:S(2)}, u32[]{:S(2)}) collective-permute-start(bf16[2,64,512]{2,1,0:T(8,128)(2,1)} %copy-done.9), channel_id=1, source_target_pairs={{0,24},{8,0},{16,8},{24,16},{1,25},{9,1},{17,9},{25,17},{2,26},{10... | collective-permute-start | bytes 393224 | tf_op jit(solution)/shard_map/ppermute | solution.py:258
  116.7 12.2 %collective-permute-start.7 = (bf16[3,2,64,512]{3,2,1,0:T(8,128)(2,1)}, bf16[3,2,64,512]{3,2,1,0:T(8,128)(2,1)S(1)}, u32[]{:S(2)}, u32[]{:S(2)}) collective-permute-start(bf16[3,2,64,512]{3,2,1,0:T(8,128)(2,1)} %pack.4.refs_4_), channel_id=1, source_target_pairs={{0,4},{1,3},{2,6},{3,1},{4,0},{5,7},{6,2},{7,5},{8,12},{9,11},{10,... | collective-permute-start | bytes 1179656 | tf_op jit(solution)/shard_map/ppermute | solution.py:225
  118.4 20.7 %collective-permute-start.27 = (bf16[3,2,64,512]{3,2,1,0:T(8,128)(2,1)}, bf16[3,2,64,512]{3,2,1,0:T(8,128)(2,1)S(1)}, u32[]{:S(2)}, u32[]{:S(2)}) collective-permute-start(bf16[3,2,64,512]{3,2,1,0:T(8,128)(2,1)} %pack.7.refs_4_), channel_id=1, source_target_pairs={{0,2},{1,5},{2,0},{3,7},{4,6},{5,1},{6,4},{7,3},{8,10},{9,13},{10,... | collective-permute-start | bytes 1179656 | tf_op jit(solution)/shard_map/ppermute | solution.py:225
  119.3 19.9 %collective-permute-start.28 = (bf16[3,2,64,512]{3,2,1,0:T(8,128)(2,1)S(1)}, bf16[3,2,64,512]{3,2,1,0:T(8,128)(2,1)S(1)}, u32[]{:S(2)}, u32[]{:S(2)}) collective-permute-start(bf16[3,2,64,512]{3,2,1,0:T(8,128)(2,1)S(1)} %collective-permute-done.26.refs_5_), channel_id=1, source_target_pairs={{0,2},{1,5},{2,0},{3,7},{4,6},{5,1},{6,4},{7,3},{8,10},{9,13},{10,... | collective-permute-start | bytes 1179656 | tf_op jit(solution)/shard_map/ppermute | solution.py:225
  128.9 22.9 %collective-permute-start.8 = (bf16[3,2,64,512]{3,2,1,0:T(8,128)(2,1)}, bf16[3,2,64,512]{3,2,1,0:T(8,128)(2,1)S(1)}, u32[]{:S(2)}, u32[]{:S(2)}) collective-permute-start(bf16[3,2,64,512]{3,2,1,0:T(8,128)(2,1)} %pack.4.refs_4_), channel_id=1, source_target_pairs={{0,2},{1,5},{2,0},{3,7},{4,6},{5,1},{6,4},{7,3},{8,10},{9,13},{10,... | collective-permute-start | bytes 1179656 | tf_op jit(solution)/shard_map/ppermute | solution.py:225
  129.8 22.0 %collective-permute-start.9 = (bf16[3,2,64,512]{3,2,1,0:T(8,128)(2,1)S(1)}, bf16[3,2,64,512]{3,2,1,0:T(8,128)(2,1)S(1)}, u32[]{:S(2)}, u32[]{:S(2)}) collective-permute-start(bf16[3,2,64,512]{3,2,1,0:T(8,128)(2,1)S(1)} %collective-permute-done.7.refs_5_), channel_id=1, source_target_pairs={{0,2},{1,5},{2,0},{3,7},{4,6},{5,1},{6,4},{7,3},{8,10},{9,13},{10,... | collective-permute-start | bytes 1179656 | tf_op jit(solution)/shard_map/ppermute | solution.py:225
  132.1 7.0 %copy-start.2 = (bf16[3,2,64,512]{3,2,1,0:T(8,128)(2,1)S(1)}, bf16[3,2,64,512]{3,2,1,0:T(8,128)(2,1)}, u32[]{:S(2)}) copy-start(bf16[3,2,64,512]{3,2,1,0:T(8,128)(2,1)} %pack.7.refs_4_) | copy-start | bytes 1179652
  144.8 13.2 %collective-permute-start.31 = (bf16[4,4,2,64,512]{4,3,2,1,0:T(8,128)(2,1)S(1)}, bf16[4,4,2,64,512]{4,3,2,1,0:T(8,128)(2,1)S(1)}, u32[]{:S(2)}, u32[]{:S(2)}) collective-permute-start(bf16[4,4,2,64,512]{4,3,2,1,0:T(8,128)(2,1)S(1)} %get-tuple-element.52), channel_id=1, source_target_pairs={{0,1},{1,0},{2,3},{3,2},{4,5},{5,4},{6,7},{7,6},{8,9},{9,8},{10,11... | collective-permute-start | bytes 6291464 | tf_op jit(solution)/shard_map/ppermute | solution.py:263
  144.8 7.0 %copy-start = (bf16[3,2,64,512]{3,2,1,0:T(8,128)(2,1)S(1)}, bf16[3,2,64,512]{3,2,1,0:T(8,128)(2,1)}, u32[]{:S(2)}) copy-start(bf16[3,2,64,512]{3,2,1,0:T(8,128)(2,1)} %pack.4.refs_4_) | copy-start | bytes 1179652
  157.4 5.8 %collective-permute-start.30 = (bf16[4,4,2,64,512]{4,3,2,1,0:T(8,128)(2,1)S(1)}, bf16[4,4,2,64,512]{4,3,2,1,0:T(8,128)(2,1)S(1)}, u32[]{:S(2)}, u32[]{:S(2)}) collective-permute-start(bf16[4,4,2,64,512]{4,3,2,1,0:T(8,128)(2,1)S(1)} %get-tuple-element.50), channel_id=1, source_target_pairs={{0,1},{1,0},{2,3},{3,2},{4,5},{5,4},{6,7},{7,6},{8,9},{9,8},{10,11... | collective-permute-start | bytes 6291464 | tf_op jit(solution)/shard_map/ppermute | solution.py:263
  (10 other events, 8.3 us)

commit v2 on v0

v2 whole, which is shorter than its diff:
```python
import functools
import math

import jax
import jax.numpy as jnp
import numpy as np
from jax import lax
from jax.experimental import pallas as pl
from jax.experimental.pallas import tpu as pltpu
from jax.sharding import PartitionSpec as P

VOLT_SCALE = 1.0 / 256.0
GROUP = 16
MIB = 1 << 20
CORRELATE_VMEM = 16 * MIB
ANY = pl.BlockSpec(memory_space=pl.ANY)
HBM = pl.BlockSpec(memory_space=pltpu.HBM)
TOKEN = jax.ShapeDtypeStruct((8, 128), jnp.float32)


def struct(shape, dtype=jnp.bfloat16):
    return jax.ShapeDtypeStruct(shape, dtype)


def transform_rows(chans, span):
    index = np.arange(chans)
    angle = (index[:, None] * index[None, :] % chans) * (2.0 * math.pi / chans)
    cosine, sine = np.cos(angle), np.sin(angle)
    rows = np.stack([np.stack([cosine, sine], 1), np.stack([-sine, cosine], 1)], 1) * VOLT_SCALE
    rows = np.broadcast_to(rows[:, :, :, None], (chans, 2, 2, span, chans))
    return np.tile(rows.reshape(chans, 2, -1), (2, 1, 1)).astype(np.float32)


def channelize_group(volts, held, weights, outs, layout):
    group, chans, width = volts.shape[1:]
    span = held.shape[0] // 2
    ahead = span - group * chans
    for q in range(2):
        held[q * span + ahead : (q + 1) * span, :] = (
            volts[q].astype(jnp.float32).astype(jnp.bfloat16).reshape(group * chans, width)
        )
    frames = held[...]
    result = jnp.dot(weights[0], frames, preferred_element_type=jnp.float32)
    result = result + jnp.dot(weights[1], frames, preferred_element_type=jnp.float32)
    devices = max(d for d, _ in layout) + 1
    result = result.astype(jnp.bfloat16).reshape(devices, -1, 2, group, width)
    for (d, channels), out in zip(layout, outs, strict=True):
        out[...] = result[d, channels[0] : channels[-1] + 1]


def channelize_inner(layout, tap_count, voltages, table, taps, *rest):
    outs, (weights, held, volts, last, sems) = rest[:-5], rest[-5:]
    slots, _, group, chans, width = volts.shape
    ahead = (tap_count - 1) * chans
    span = ahead + group * chans
    g = pl.program_id(0)

    def arrival(g):
        return pltpu.make_async_copy(voltages.at[:, pl.ds((g + 1) * group, group)], volts.at[g], sems.at[g])

    @pl.when(g == 0)
    def _():
        early = pltpu.make_async_copy(voltages.at[:, pl.ds(group - (tap_count - 1), tap_count - 1)], last, sems.at[slots])
        early.start()
        for slot in range(slots):
            arrival(slot).start()
        column = lax.broadcasted_iota(jnp.int32, (group, 2 * span), 1)
        column = jnp.where(column >= span, column - span, column) // chans
        row = lax.broadcasted_iota(jnp.int32, (group, 2 * span), 0)
        band = jnp.zeros((group, 2 * span), jnp.float32)
        for k in range(tap_count):
            band = band + jnp.where(column == row + (tap_count - 1 - k), taps[k : k + 1, :], 0.0)
        for c in range(table.shape[0]):
            for p in range(2):
                exact = table[c, p : p + 1, :] * band
                high = exact.astype(jnp.bfloat16)
                at = (2 * c + p) * group
                weights[0, at : at + group, :] = high
                weights[1, at : at + group, :] = (exact - high.astype(jnp.float32)).astype(jnp.bfloat16)
        early.wait()
        for q in range(2):
            frames = last[q].astype(jnp.float32).astype(jnp.bfloat16)
            held[q * span : q * span + ahead, :] = frames.reshape(ahead, width)

    @pl.when(g > 0)
    def _():
        for q in range(2):
            held[q * span : q * span + ahead, :] = held[(q + 1) * span - ahead : (q + 1) * span, :]

    arrival(g).wait()
    channelize_group(volts.at[g], held, weights, outs, layout)


def channelize_first(layout, voltages, rim, weights, *rest):
    outs, (held, volts, sem) = rest[len(layout) : -3], rest[-3:]
    span = held.shape[0] // 2
    ahead = span - volts.shape[1] * volts.shape[2]
    arrival = pltpu.make_async_copy(voltages.at[:, pl.ds(0, volts.shape[1])], volts, sem)
    arrival.start()
    for q in range(2):
        held[q * span : q * span + ahead, :] = rim[q].reshape(ahead, rim.shape[-1])
    arrival.wait()
    channelize_group(volts, held, weights, outs, layout)


def channelize(voltages, rim, table, taps, layout):
    _, frames, chans, width = voltages.shape
    tap_count = taps.shape[0]
    span = (GROUP + tap_count - 1) * chans
    groups = frames // GROUP
    shapes = [struct((len(channels), 2, frames, width)) for _, channels in layout]
    blocks = [(len(channels), 2, GROUP, width) for _, channels in layout]
    weight_shape = (2, chans * 2 * GROUP, 2 * span)
    cost = 2 * 2 * GROUP * (chans * 2) * (2 * span) * width
    held = pltpu.VMEM((2 * span, width), jnp.bfloat16)
    block = (2, GROUP, chans, width)
    params = pltpu.CompilerParams(vmem_limit_bytes=32 * MIB)
    *outs, weights = pl.pallas_call(
        functools.partial(channelize_inner, layout, tap_count),
        grid=(groups - 1,),
        in_specs=[
            HBM,
            pl.BlockSpec(table.shape, lambda g: (0, 0, 0)),
            pl.BlockSpec(taps.shape, lambda g: (0, 0)),
        ],
        out_specs=[pl.BlockSpec(b, lambda g: (0, 0, g + 1, 0)) for b in blocks]
        + [pl.BlockSpec(weight_shape, lambda g: (0, 0, 0))],
        out_shape=shapes + [struct(weight_shape)],
        scratch_shapes=[
            held,
            pltpu.VMEM((groups - 1,) + block, jnp.int32),
            pltpu.VMEM((2, tap_count - 1, chans, width), jnp.int32),
            pltpu.SemaphoreType.DMA((groups,)),
        ],
        compiler_params=params,
        cost_estimate=pl.CostEstimate(
            flops=cost * (groups - 1), bytes_accessed=6 * voltages.size, transcendentals=0
        ),
        name="channelize_inner",
    )(voltages, table, taps)
    return pl.pallas_call(
        functools.partial(channelize_first, layout),
        grid=(1,),
        in_specs=[
            HBM,
            pl.BlockSpec(rim.shape, lambda g: (0, 0, 0, 0)),
            pl.BlockSpec(weight_shape, lambda g: (0, 0, 0)),
        ]
        + [ANY] * len(layout),
        out_specs=[pl.BlockSpec(b, lambda g: (0, 0, 0, 0)) for b in blocks],
        out_shape=shapes,
        input_output_aliases={3 + i: i for i in range(len(layout))},
        scratch_shapes=[held, pltpu.VMEM(block, jnp.int32), pltpu.SemaphoreType.DMA],
        compiler_params=params,
        cost_estimate=pl.CostEstimate(flops=cost, bytes_accessed=6 * voltages.size // groups, transcendentals=0),
        name="channelize_first",
    )(voltages, rim, weights, *outs)


def correlate_step(shape, where, token, *refs):
    works, frames, has_out, scale = shape
    refs = list(refs)
    take = lambda number: [refs.pop(0) for _ in range(number)]
    operands = {(w, job): (take(2), take(2)) for w, (_, jobs, _) in enumerate(works) for job in jobs}
    stored = [take(1)[0] if has_left else None for _, _, has_left in works]
    take(has_out)
    out, _ = take(2)
    made = [None if has_left else take(1)[0] for _, _, has_left in works]
    panel, left, results, sems, left_sems, out_sems = refs
    slots, depth, width = panel.shape
    rows = 2 * frames
    units = [(w, job, c, half) for w, (channels, jobs, _) in enumerate(works) for job in jobs for c in range(len(channels)) for half in (0, 1)]

    def arrivals(u):
        w, job, c, half = units[u]
        at = 0
        for ref in operands[w, job][half]:
            first = works[w][0][0] if ref.shape[1] > len(works[w][0]) else 0
            for d in range(ref.shape[0]):
                yield pltpu.make_async_copy(
                    ref.at[d, first + c], panel.at[u % slots, pl.ds(at * rows, rows)], sems.at[u % slots, at]
                )
                at += 1

    def departures(u):
        w, job, c, half = units[u]
        columns = pl.ds(pl.multiple_of(where[job, half] * width, width), width)
        for p in range(2):
            slot = (2 * u + p) % results.shape[0]
            yield pltpu.make_async_copy(results.at[slot], out.at[works[w][0][0] + c, p, :, columns], out_sems.at[slot])

    def stored_rows(w, c):
        return pltpu.make_async_copy(stored[w].at[c], left.at[w, c], left_sems.at[w, c])

    def made_rows(w, c):
        return pltpu.make_async_copy(left.at[w, c], made[w].at[c], left_sems.at[w, c])

    seen = set()
    behind = results.shape[0] // 2
    for u in range(min(slots, len(units))):
        w, _, c, _ = units[u]
        if stored[w] is not None and (w, c) not in seen:
            stored_rows(w, c).start()
            seen.add((w, c))
        for copy in arrivals(u):
            copy.start()
    ready = set()
    for u, (w, job, c, half) in enumerate(units):
        for copy in arrivals(u):
            copy.wait()
        if (w, c) not in ready:
            ready.add((w, c))
            if stored[w] is not None:
                stored_rows(w, c).wait()
            else:
                for at in range(0, depth, rows):
                    real = panel[u % slots, at : at + frames].T
                    imag = panel[u % slots, at + frames : at + rows].T
                    left[w, c, :width, at : at + rows] = jnp.concatenate([real, imag], 1)
                    left[w, c, width:, at : at + rows] = jnp.concatenate([imag, -real], 1)
                made_rows(w, c).start()
        if u >= behind:
            for copy in departures(u - behind):
                copy.wait()
        for p, copy in enumerate(departures(u)):
            lines = left[w, c, p * width : (p + 1) * width]
            result = jnp.dot(lines, panel[u % slots], preferred_element_type=jnp.float32) * scale
            results[(2 * u + p) % results.shape[0]] = result
            copy.start()
        later = u + slots
        if later < len(units):
            w, _, c, _ = units[later]
            if stored[w] is not None and (w, c) not in seen:
                stored_rows(w, c).start()
                seen.add((w, c))
            for copy in arrivals(later):
                copy.start()
    for u in range(max(0, len(units) - behind), len(units)):
        for copy in departures(u):
            copy.wait()
    for w, (channels, _, has_left) in enumerate(works):
        if not has_left:
            for c in range(len(channels)):
                made_rows(w, c).wait()


def correlate(works, where, token, out, whole):
    frames, width = next(iter(works[0][2].values()))[0][0].shape[-2:]
    operands = [
        p.reshape(-1, p.shape[-4], 2 * frames, width) for _, _, jobs in works for job in jobs.values() for half in job for p in half
    ]
    depth = 2 * frames * (operands[0].shape[0] + operands[1].shape[0])
    lefts = [left for _, left, _ in works if left is not None]
    has_out = out is not None
    channels = max(len(channels) for channels, _, _ in works)
    made = [struct((len(c), 2 * width, depth)) for c, left, _ in works if left is None]
    shape = ([(tuple(c), tuple(jobs), left is not None) for c, left, jobs in works], frames, has_out, 2.0 / depth)
    slots, results = 4, 4
    out, token, *made = pl.pallas_call(
        functools.partial(correlate_step, shape),
        in_specs=[pl.BlockSpec(memory_space=pltpu.SMEM), ANY] + [HBM] * (len(operands) + len(lefts) + has_out),
        out_specs=[HBM, ANY] + [HBM] * len(made),
        out_shape=[whole, TOKEN] + made,
        input_output_aliases={1: 1, **({2 + len(operands) + len(lefts): 0} if has_out else {})},
        scratch_shapes=[
            pltpu.VMEM((slots, depth, width), jnp.bfloat16),
            pltpu.VMEM((len(works), channels, 2 * width, depth), jnp.bfloat16),
            pltpu.VMEM((results, width, width), jnp.float32),
            pltpu.SemaphoreType.DMA((slots, depth // (2 * frames))),
            pltpu.SemaphoreType.DMA((len(works), channels)),
            pltpu.SemaphoreType.DMA((results,)),
        ],
        compiler_params=pltpu.CompilerParams(vmem_limit_bytes=CORRELATE_VMEM),
        cost_estimate=pl.CostEstimate(flops=0, bytes_accessed=0, transcendentals=0),
        name="correlate",
    )(where, token, *operands, *lefts, *([out] if has_out else []))
    made = iter(made)
    return out, token, [left if left is not None else next(made) for _, left, _ in works]


def step_bits(count, core):
    bits = [1 << b for b in range(1, count.bit_length() - 1)]
    return bits if core else bits[::-1]


def source_masks(count, core):
    masks = [0]
    for bit in step_bits(count, core):
        masks += [m ^ bit for m in masks]
    return masks


def moves(count):
    order = []
    for step in range(len(step_bits(count, 0))):
        order += [(block, step) for block in range(1 << step)]
    return order


def body(voltages, fir_taps):
    _, frames, chans, width = voltages.shape
    tap_count = fir_taps.shape[0]
    devices, count = lax.axis_size("chan"), lax.axis_size("inp")
    mine = chans // devices
    plane, place = lax.axis_index("chan"), lax.axis_index("inp")

    rim = voltages[:, frames - (tap_count - 1) :].astype(jnp.bfloat16)
    rim = lax.ppermute(rim, "chan", [(i, i + 1) for i in range(devices - 1)])
    table = transform_rows(chans, GROUP + tap_count - 1)
    table = lax.dynamic_slice_in_dim(jnp.asarray(table), plane * mine, chans, 0)
    taps = jnp.tile(fir_taps, (1, 2 * (GROUP + tap_count - 1)))
    sources = np.array([[i ^ m for m in source_masks(count, i % 2)] for i in range(count)], np.int32)
    sources = np.stack([sources, sources[np.arange(count) ^ 1]], 2)
    sources = lax.dynamic_index_in_dim(jnp.asarray(sources), place, 0, keepdims=False)

    halves = [range(mine)] if mine < 2 else [range(mine // 2), range(mine // 2, mine)]
    layout = [(0, range(mine))] + [(d, half) for half in halves for d in range(1, devices)]
    firsts = channelize(voltages, rim, table, taps, layout)

    def turned(piece, d):
        return lax.ppermute(piece, "chan", [(i, (i + d) % devices) for i in range(devices)])

    def swapped(block):
        return lax.ppermute(block, "inp", [(i, i ^ 1) for i in range(count)])

    orders = [step_bits(count, core) for core in (0, 1)]
    steps = moves(count)
    chips = len(steps) + 1
    whole = struct((mine, 2, width, width * count), jnp.float32)

    groups = range(1 + len(halves))
    turning = [firsts[1 + h * (devices - 1) :][: devices - 1] for h in range(len(halves))]
    here = [[] for _ in groups]
    there = [[] for _ in groups]
    jobs = [(h, m) for h in range(len(halves)) for m in range(chips)]
    lefts = {}
    state = {"out": None, "token": jnp.zeros(TOKEN.shape, TOKEN.dtype)}

    def gated(arrays):
        *arrays, state["token"] = lax.optimization_barrier((*arrays, state["token"]))
        return arrays

    def work():
        works = {}
        while jobs:
            h, m = jobs[0]
            held = (0, 1 + h)
            if any(len(there[g]) <= m for g in held):
                break
            jobs.pop(0)
            works.setdefault(h, {})[m] = [[side[g][m] for g in held] for side in (here, there)]
        if works:
            state["out"], state["token"], rows = correlate(
                [(halves[h], lefts.get(h), pairs) for h, pairs in works.items()], sources, state["token"], state["out"], whole
            )
            lefts.update(zip(works, rows))

    def one_round(sends, turns, swaps):
        sent = gated([here[g][source] for g, source, _ in sends] + [piece for _, piece in turns] + [here[g][m] for g, m in swaps])
        moved = [
            lax.ppermute(block, "inp", [(i, i ^ orders[i % 2][step]) for i in range(count)])
            for block, (_, _, step) in zip(sent, sends)
        ]
        arrived = [turned(block, d) for block, (d, _) in zip(sent[len(sends) :], turns)]
        for block, (g, _) in zip(sent[len(sends) + len(turns) :], swaps):
            there[g].append(swapped(block))
        work()
        moved = gated(moved + arrived)
        for block, (g, _, _) in zip(moved, sends):
            here[g].append(block)
        return moved[len(sends) :]

    here[0].append(firsts[0])
    swaps = [(0, 0)]
    for g in groups:
        rest = list(enumerate(turning[g], 1)) if g < len(halves) else []
        arrived = []
        pending = list(steps)
        rounds = []
        landed = 1
        while pending:
            now = [move for move in pending[:2] if move[0] < landed]
            pending = pending[len(now) :]
            landed += len(now)
            rounds.append(now)
        share = -(-len(rest) // len(rounds))
        for now in rounds:
            arrived += one_round([(g, source, step) for source, step in now], rest[:share], swaps)
            rest = rest[share:]
            swaps = [(g, len(here[g]) - len(now) + i) for i in range(len(now))]
        if arrived:
            here[g + 1] += gated([jnp.stack(arrived)])
            swaps.append((g + 1, 0))
    one_round([], [], swaps)
    return state["out"]


def solution(mesh):
    placed = (P(None, "chan", None, "inp"), P())
    return jax.shard_map(body, mesh=mesh, in_specs=placed, out_specs=P("chan", None, "inp", None), check_vma=False)
```

time: 326 us -> 137 us (0.42)
  Pallas kernels: 0 us -> 61.2 us
  other arithmetic: 61 us -> 2.15 us
  blocking collectives: 52.9 us -> 0 us
  waiting for transfers between devices: 95.7 us -> 43.1 us
  matrix products: 48.6 us -> 0 us
  local copies, waits for them, and re-layouts: 48.7 us -> 5.36 us
  starting transfers between devices: 4.94 us -> 24.1 us
  between operations: 13.5 us -> 0.35 us
    all_gather x1 -> x0, waiting for transfers between devices: 92.4 us -> none  [body(): piece = lax.all_gather(turned, 'inp', axis=3, tiled=True)]
    pallas_call x0 -> x7, Pallas kernels: none -> 61.2 us  [the longest x5 55 us: correlate(): pl.pallas_call(functools.partial(correlate_step, shape), in_specs=[pl.Blo...]
    all_to_all x1 -> x0, blocking collectives: 52.9 us -> none  [body(): lax.all_to_all(spectra, 'chan', split_axis=0, concat_axis=2, tiled=True)]
    dot_general x6 -> x0, matrix products: 48.6 us -> none  [the longest x1 21.1 us: body(): jnp.einsum('cpsi,cpsj->cij', turned, piece, preferred_element_type=jnp.fl...]
    mul x2 -> x0, local copies, waits for them, and re-layouts: 45 us -> none  [the longest x1 44.2 us: body(): return jnp.stack([real_part, imag_part], 1) * norm_factor]
    mul x1 -> x0, other arithmetic: 43.6 us -> none  [body(): return jnp.stack([real_part, imag_part], 1) * norm_factor]
    ppermute x1 -> x28, waiting for transfers between devices: 3.29 us -> 43.1 us  [the longest x6 32.3 us: turned(): lax.ppermute(piece, 'chan', [(i, (i + d) % devices) for i in range(device...]
    ppermute x1 -> x28, starting transfers between devices: 4.94 us -> 24.1 us  [the longest x9 9.9 us: one_round(): lax.ppermute(block, 'inp', [(i, i ^ orders[i % 2][step]) for i in range(c...]
  transfers between devices with their start and end apart: 2 -> 28, of which waited for: 2 -> 13; matrix products, arithmetic and copies ran while one was open for 0% -> 2% of each run, Pallas kernels for 0% -> 38%
where the time goes in v2:
time: 137 us; the launch traced here: 136 us
  Pallas kernels  61.2 us (45%)
  waiting for transfers between devices  43.1 us (31%)
  starting transfers between devices  24.1 us (18%)
  local copies, waits for them, and re-layouts  5.36 us (4%)
  other arithmetic  2.15 us (2%)
    pallas_call x5, Pallas kernels, correlate(): pl.pallas_call(functools.partial(correlate_step, shape), in_specs=[pl.Blo...  55 us
    ppermute x6, waiting for transfers between devices, turned(): lax.ppermute(piece, 'chan', [(i, (i + d) % devices) for i in range(device...  32.3 us
    ppermute x9, starting transfers between devices, one_round(): lax.ppermute(block, 'inp', [(i, i ^ orders[i % 2][step]) for i in range(c...  9.9 us
    ppermute x12, waiting for transfers between devices, swapped(): return lax.ppermute(block, 'inp', [(i, i ^ 1) for i in range(count)])  8.74 us
    ppermute x6, starting transfers between devices, turned(): lax.ppermute(piece, 'chan', [(i, (i + d) % devices) for i in range(device...  6.78 us
    ppermute x1, starting transfers between devices, body(): rim = lax.ppermute(rim, 'chan', [(i, i + 1) for i in range(devices - 1)])  4.93 us
    pallas_call x1, Pallas kernels, channelize(): pl.pallas_call(functools.partial(channelize_inner, layout, tap_count), gr...  4.4 us
    unnamed x4, local copies, waits for them, and re-layouts  2.9 us
  transfers between devices with their start and end apart: 28, of which 13 were waited for; matrix products, arithmetic and copies ran while one was open for 2% of the time, Pallas kernels for 38%

profile of v2, /device:TPU:0, one launch (start us, length us, event | category | flops | bytes accessed | tf_op | source)
XLA Modules:
  0.0 136.3 jit_solution(8740283161107268769)
XLA Ops:
  0.0 0.9 slice_convert_fusion
  0.9 4.9 %collective-permute-start = (bf16[2,3,16,512]{3,2,1,0:T(8,128)(2,1)S(1)}, bf16[2,3,16,512]{3,2,1,0:T(8,128)(2,1)S(1)}, u32[]{:S(2)}, u32[]{:S(2)}) collective-permute-start(bf16[2,3,16,512]{3,2,1,0:T(8,128)(2,1)S(1)} %slice_convert_fusion), channel_id=1, source_target_pairs={{0,8},{8,16},{16,24},{1,9},{9,17},{17,25},{2,10},{10,18},{18,26},{... | collective-permute-start | bytes 294920 | tf_op jit(solution)/shard_map/ppermute | solution.py:308
  5.9 0.7 tile.4
  6.7 0.9 constant_dynamic-slice_fusion.table
  7.6 2.2 %copy-done = s32[2,64,16,512]{3,2,1,0:T(8,128)S(1)} copy-done((s32[2,64,16,512]{3,2,1,0:T(8,128)S(1)}, s32[2,64,16,512]{3,2,1,0:T(8,128)}, u32[]{:S(2)}) %copy-start) | copy-done | bytes 4194328
  9.8 4.4 %channelize_inner.1 = (bf16[4,2,64,512]{3,2,1,0:T(8,128)(2,1)S(1)}, bf16[2,2,64,512]{3,2,1,0:T(8,128)(2,1)S(1)}, bf16[2,2,64,512]{3,2,1,0:T(8,128)(2,1)S(1)}, bf...) custom-call(s32[2,64,16,512]{3,2,1,0:T(8,128)S(1)} %copy-done, ...), custom_call_target="tpu_custom_call" | custom-call | flops 1912602624 | bytes 6291456 | tf_op jit(solution)/shard_map/channelize_inner/pallas_call | solution.py:118
  14.2 1.8 %channelize_first.1 = (bf16[4,2,64,512]{3,2,1,0:T(8,128)(2,1)S(1)}, bf16[2,2,64,512]{3,2,1,0:T(8,128)(2,1)S(1)}, bf16[2,2,64,512]{3,2,1,0:T(8,128)(2,1)S(1)}, bf...) custom-call(s32[2,64,16,512]{3,2,1,0:T(8,128)S(1)} %copy-done, ...), custom_call_target="tpu_custom_call", output_to_operand_aliasing={{0}: (3, {}), {1}: (4, {}), {2}: (5, {}), {3}: (6, {}), {4}... | custom-call | flops 637534208 | bytes 1572864 | tf_op jit(solution)/shard_map/channelize_first/pallas_call | solution.py:141
  16.0 0.7 copy-done.1
  16.7 1.5 %collective-permute-start.1 = (bf16[4,2,64,512]{3,2,1,0:T(8,128)(2,1)S(1)}, bf16[4,2,64,512]{3,2,1,0:T(8,128)(2,1)S(1)}, u32[]{:S(2)}, u32[]{:S(2)}) collective-permute-start(bf16[4,2,64,512]{3,2,1,0:T(8,128)(2,1)S(1)} %get-tuple-element.126), channel_id=1, source_target_pairs={{0,4},{1,3},{2,6},{3,1},{4,0},{5,7},{6,2},{7,5},{8,12},{9,11},{10,... | collective-permute-start | bytes 1572872 | tf_op jit(solution)/shard_map/ppermute | solution.py:361
  18.2 1.5 %collective-permute-start.2 = (bf16[4,2,64,512]{3,2,1,0:T(8,128)(2,1)S(1)}, bf16[4,2,64,512]{3,2,1,0:T(8,128)(2,1)S(1)}, u32[]{:S(2)}, u32[]{:S(2)}) collective-permute-start(bf16[4,2,64,512]{3,2,1,0:T(8,128)(2,1)S(1)} %get-tuple-element.126), channel_id=1, source_target_pairs={{0,2},{1,5},{2,0},{3,7},{4,6},{5,1},{6,4},{7,3},{8,10},{9,13},{10,... | collective-permute-start | bytes 1572872 | tf_op jit(solution)/shard_map/ppermute | solution.py:361
  19.7 1.6 %collective-permute-start.3 = (bf16[2,2,64,512]{3,2,1,0:T(8,128)(2,1)S(1)}, bf16[2,2,64,512]{3,2,1,0:T(8,128)(2,1)S(1)}, u32[]{:S(2)}, u32[]{:S(2)}) collective-permute-start(bf16[2,2,64,512]{3,2,1,0:T(8,128)(2,1)S(1)} %get-tuple-element.102), channel_id=1, source_target_pairs={{0,8},{8,16},{16,24},{24,0},{1,9},{9,17},{17,25},{25,1},{2,10},{10... | collective-permute-start | bytes 786440 | tf_op jit(solution)/shard_map/ppermute | solution.py:321
  21.3 1.0 collective-permute-start.4
  22.3 8.5 %collective-permute-done.3 = bf16[2,2,64,512]{3,2,1,0:T(8,128)(2,1)S(1)} collective-permute-done((bf16[2,2,64,512]{3,2,1,0:T(8,128)(2,1)S(1)}, bf16[2,2,64,512]{3,2,1,0:T(8,128)(2,1)S(1)}, u32[]{:S(2)}, u32[]{:S(2)}) %collective-permute-start.3) | collective-permute-done | bytes 262176 | tf_op jit(solution)/shard_map/ppermute | solution.py:321
  30.8 9.1 %collective-permute-done.4 = bf16[2,2,64,512]{3,2,1,0:T(8,128)(2,1)S(1)} collective-permute-done((bf16[2,2,64,512]{3,2,1,0:T(8,128)(2,1)S(1)}, bf16[2,2,64,512]{3,2,1,0:T(8,128)(2,1)S(1)}, u32[]{:S(2)}, u32[]{:S(2)}) %collective-permute-start.4) | collective-permute-done | bytes 262176 | tf_op jit(solution)/shard_map/ppermute | solution.py:321
  39.9 0.5 collective-permute-start.5
  40.5 1.7 %collective-permute-start.6 = (bf16[2,2,64,512]{3,2,1,0:T(8,128)(2,1)S(1)}, bf16[2,2,64,512]{3,2,1,0:T(8,128)(2,1)S(1)}, u32[]{:S(2)}, u32[]{:S(2)}) collective-permute-start(bf16[2,2,64,512]{3,2,1,0:T(8,128)(2,1)S(1)} %get-tuple-element.112), channel_id=1, source_target_pairs={{0,24},{8,0},{16,8},{24,16},{1,25},{9,1},{17,9},{25,17},{2,26},{10... | collective-permute-start | bytes 786440 | tf_op jit(solution)/shard_map/ppermute | solution.py:321
  42.2 6.2 %collective-permute-done.6 = bf16[2,2,64,512]{3,2,1,0:T(8,128)(2,1)S(1)} collective-permute-done((bf16[2,2,64,512]{3,2,1,0:T(8,128)(2,1)S(1)}, bf16[2,2,64,512]{3,2,1,0:T(8,128)(2,1)S(1)}, u32[]{:S(2)}, u32[]{:S(2)}) %collective-permute-start.6) | collective-permute-done | bytes 262176 | tf_op jit(solution)/shard_map/ppermute | solution.py:321
  48.4 0.7 collective-permute-done.5
  49.3 0.5 collective-permute-start.11
  49.8 0.8 collective-permute-start.7
  50.6 0.5 collective-permute-start.8
  51.1 1.2 collective-permute-done.11
  52.3 1.5 %collective-permute-start.9 = (bf16[2,2,64,512]{3,2,1,0:T(8,128)(2,1)}, bf16[2,2,64,512]{3,2,1,0:T(8,128)(2,1)}, u32[]{:S(2)}, u32[]{:S(2)}) collective-permute-start(bf16[2,2,64,512]{3,2,1,0:T(8,128)(2,1)} %get-tuple-element.123), channel_id=1, source_target_pairs={{0,8},{8,16},{16,24},{24,0},{1,9},{9,17},{17,25},{25,1},{2,10},{10... | collective-permute-start | bytes 786440 | tf_op jit(solution)/shard_map/ppermute | solution.py:321
  53.8 0.7 dynamic-slice_bitcast_fusion
  54.5 7.8 %correlate.5 = (f32[4,2,512,4096]{3,2,1,0:T(8,128)}, f32[8,128]{1,0:T(8,128)S(1)}, bf16[2,1024,512]{2,1,0:T(8,128)(2,1)S(1)}) custom-call(s32[4,2]{1,0:T(4,128)S(1)} %copy.30.where, f32[8,128]{1,0:T(8,128)S(1)} %broadcast_in_dim.3.token, bf16[1,4,128,512]{3,2,1,0:T(8,128)(2,1)S(1)} %bitcast.32, ...), custom_call_target="tpu_custom_call", output_to_operand_aliasing={{1}: (1, {})} | custom-call | tf_op jit(solution)/shard_map/correlate/pallas_call | solution.py:259
  62.3 8.4 %collective-permute-done.10 = bf16[2,2,64,512]{3,2,1,0:T(8,128)(2,1)} collective-permute-done((bf16[2,2,64,512]{3,2,1,0:T(8,128)(2,1)}, bf16[2,2,64,512]{3,2,1,0:T(8,128)(2,1)}, u32[]{:S(2)}, u32[]{:S(2)}) %collective-permute-start.10) | collective-permute-done | bytes 262176 | tf_op jit(solution)/shard_map/ppermute | solution.py:321
  70.8 0.5 collective-permute-start.18
  71.4 1.5 %collective-permute-start.13 = (bf16[3,2,2,64,512]{4,3,2,1,0:T(8,128)(2,1)}, bf16[3,2,2,64,512]{4,3,2,1,0:T(8,128)(2,1)S(1)}, u32[]{:S(2)}, u32[]{:S(2)}) collective-permute-start(bf16[3,2,2,64,512]{4,3,2,1,0:T(8,128)(2,1)} %collective-permute-done.7), channel_id=1, source_target_pairs={{0,2},{1,5},{2,0},{3,7},{4,6},{5,1},{6,4},{7,3},{8,10},{9,13},{10,... | collective-permute-start | bytes 2359304 | tf_op jit(solution)/shard_map/ppermute | solution.py:361
  72.9 1.7 %collective-permute-done.15 = bf16[4,2,64,512]{3,2,1,0:T(8,128)(2,1)S(1)} collective-permute-done((bf16[4,2,64,512]{3,2,1,0:T(8,128)(2,1)S(1)}, bf16[4,2,64,512]{3,2,1,0:T(8,128)(2,1)S(1)}, u32[]{:S(2)}, u32[]{:S(2)}) %collective-permute-start.15) | collective-permute-done | bytes 524320 | tf_op jit(solution)/shard_map/ppermute | solution.py:324
  74.6 1.0 collective-permute-start.14
  75.7 11.4 %correlate.6 = (f32[4,2,512,4096]{3,2,1,0:T(8,128)}, f32[8,128]{1,0:T(8,128)S(1)}) custom-call(s32[4,2]{1,0:T(4,128)S(1)} %copy.30.where, f32[8,128]{1,0:T(8,128)S(1)} %get-tuple-element.137.token, bf16[1,4,128,512]{3,2,1,0:T(8,128)(2,1)S(1)} %bitcast.36, bf16[3,2,128,512]{3,2,1,0:T(8,128)(2,1)} %bitcast.11.refs_1_, ...), custom_call_target="tpu_custom_call", output_to_operand_aliasing={{1}: (1, {}), {0}: (11, {})} | custom-call | tf_op jit(solution)/shard_map/correlate/pallas_call | solution.py:259
  87.1 1.1 pad_maximum_fusion.1
  88.2 0.2 collective-permute-start.22
  88.4 0.4 collective-permute-start.23
  88.8 1.3 collective-permute-start.19
  90.1 1.0 collective-permute-start.20
  91.1 1.9 %collective-permute-done.21 = bf16[4,2,64,512]{3,2,1,0:T(8,128)(2,1)S(1)} collective-permute-done((bf16[4,2,64,512]{3,2,1,0:T(8,128)(2,1)S(1)}, bf16[4,2,64,512]{3,2,1,0:T(8,128)(2,1)S(1)}, u32[]{:S(2)}, u32[]{:S(2)}) %collective-permute-start.21) | collective-permute-done | bytes 524320 | tf_op jit(solution)/shard_map/ppermute | solution.py:324
  93.0 14.5 %correlate.7 = (f32[4,2,512,4096]{3,2,1,0:T(8,128)}, f32[8,128]{1,0:T(8,128)S(1)}, bf16[2,1024,512]{2,1,0:T(8,128)(2,1)S(1)}) custom-call(s32[4,2]{1,0:T(4,128)S(1)} %copy.30.where, f32[8,128]{1,0:T(8,128)S(1)} %get-tuple-element.152.token, bf16[1,4,128,512]{3,2,1,0:T(8,128)(2,1)S(1)} %bitcast.40, ...), custom_call_target="tpu_custom_call", output_to_operand_aliasing={{1}: (1, {}), {0}: (11, {})} | custom-call | tf_op jit(solution)/shard_map/correlate/pallas_call | solution.py:259
  107.6 1.4 %collective-permute-done.19 = bf16[3,2,2,64,512]{4,3,2,1,0:T(8,128)(2,1)S(1)} collective-permute-done((bf16[3,2,2,64,512]{4,3,2,1,0:T(8,128)(2,1)S(1)}, bf16[3,2,2,64,512]{4,3,2,1,0:T(8,128)(2,1)S(1)}, u32[]{:S(2)}, u32[]{:S(2)}) %collective-permute-start.19) | collective-permute-done | bytes 786464 | tf_op jit(solution)/shard_map/ppermute | solution.py:361
  108.9 0.1 collective-permute-start.25
  109.0 0.4 collective-permute-start.26
  109.4 1.2 collective-permute-start.24
  110.6 0.6 collective-permute-done.25
  111.2 1.1 collective-permute-done.26
  112.3 13.6 %correlate.8 = (f32[4,2,512,4096]{3,2,1,0:T(8,128)}, f32[8,128]{1,0:T(8,128)S(1)}) custom-call(s32[4,2]{1,0:T(4,128)S(1)} %copy.30.where, f32[8,128]{1,0:T(8,128)S(1)} %get-tuple-element.162.token, bf16[1,4,128,512]{3,2,1,0:T(8,128)(2,1)S(1)} %bitcast.37, bf16[3,2,128,512]{3,2,1,0:T(8,128)(2,1)S(1)} %bitcast.51, ...), custom_call_target="tpu_custom_call", output_to_operand_aliasing={{1}: (1, {}), {0}: (11, {})} | custom-call | tf_op jit(solution)/shard_map/correlate/pallas_call | solution.py:259
  125.9 0.2 collective-permute-start.27
  126.1 2.1 %collective-permute-done.27 = bf16[3,2,2,64,512]{4,3,2,1,0:T(8,128)(2,1)S(1)} collective-permute-done((bf16[3,2,2,64,512]{4,3,2,1,0:T(8,128)(2,1)S(1)}, bf16[3,2,2,64,512]{4,3,2,1,0:T(8,128)(2,1)S(1)}, u32[]{:S(2)}, u32[]{:S(2)}) %collective-permute-start.27) | collective-permute-done | bytes 786464 | tf_op jit(solution)/shard_map/ppermute | solution.py:324
  128.3 7.8 %correlate.9 = (f32[4,2,512,4096]{3,2,1,0:T(8,128)}, f32[8,128]{1,0:T(8,128)S(1)}) custom-call(s32[4,2]{1,0:T(4,128)S(1)} %copy.30.where, f32[8,128]{1,0:T(8,128)S(1)} %get-tuple-element.168.token, bf16[1,4,128,512]{3,2,1,0:T(8,128)(2,1)S(1)} %bitcast.41, bf16[3,2,128,512]{3,2,1,0:T(8,128)(2,1)S(1)} %bitcast.54, ...), custom_call_target="tpu_custom_call", output_to_operand_aliasing={{1}: (1, {}), {0}: (7, {})} | custom-call | tf_op jit(solution)/shard_map/correlate/pallas_call | solution.py:259
  (28 shorter events, 0.7 us)
Async XLA Ops:
  0.9 13.2 %collective-permute-start = (bf16[2,3,16,512]{3,2,1,0:T(8,128)(2,1)S(1)}, bf16[2,3,16,512]{3,2,1,0:T(8,128)(2,1)S(1)}, u32[]{:S(2)}, u32[]{:S(2)}) collective-permute-start(bf16[2,3,16,512]{3,2,1,0:T(8,128)(2,1)S(1)} %slice_convert_fusion), channel_id=1, source_target_pairs={{0,8},{8,16},{16,24},{1,9},{9,17},{17,25},{2,10},{10,18},{18,26},{... | collective-permute-start | bytes 294920 | tf_op jit(solution)/shard_map/ppermute | solution.py:308
  7.6 2.2 %copy-start = (s32[2,64,16,512]{3,2,1,0:T(8,128)S(1)}, s32[2,64,16,512]{3,2,1,0:T(8,128)}, u32[]{:S(2)}) copy-start(s32[2,64,16,512]{3,2,1,0:T(8,128)} %voltages.3) | copy-start | bytes 12582916
  16.0 0.7 copy-start.1
  16.7 23.3 %collective-permute-start.1 = (bf16[4,2,64,512]{3,2,1,0:T(8,128)(2,1)S(1)}, bf16[4,2,64,512]{3,2,1,0:T(8,128)(2,1)S(1)}, u32[]{:S(2)}, u32[]{:S(2)}) collective-permute-start(bf16[4,2,64,512]{3,2,1,0:T(8,128)(2,1)S(1)} %get-tuple-element.126), channel_id=1, source_target_pairs={{0,4},{1,3},{2,6},{3,1},{4,0},{5,7},{6,2},{7,5},{8,12},{9,11},{10,... | collective-permute-start | bytes 1572872 | tf_op jit(solution)/shard_map/ppermute | solution.py:361
  18.2 21.7 %collective-permute-start.2 = (bf16[4,2,64,512]{3,2,1,0:T(8,128)(2,1)S(1)}, bf16[4,2,64,512]{3,2,1,0:T(8,128)(2,1)S(1)}, u32[]{:S(2)}, u32[]{:S(2)}) collective-permute-start(bf16[4,2,64,512]{3,2,1,0:T(8,128)(2,1)S(1)} %get-tuple-element.126), channel_id=1, source_target_pairs={{0,2},{1,5},{2,0},{3,7},{4,6},{5,1},{6,4},{7,3},{8,10},{9,13},{10,... | collective-permute-start | bytes 1572872 | tf_op jit(solution)/shard_map/ppermute | solution.py:361
  19.7 11.1 %collective-permute-start.3 = (bf16[2,2,64,512]{3,2,1,0:T(8,128)(2,1)S(1)}, bf16[2,2,64,512]{3,2,1,0:T(8,128)(2,1)S(1)}, u32[]{:S(2)}, u32[]{:S(2)}) collective-permute-start(bf16[2,2,64,512]{3,2,1,0:T(8,128)(2,1)S(1)} %get-tuple-element.102), channel_id=1, source_target_pairs={{0,8},{8,16},{16,24},{24,0},{1,9},{9,17},{17,25},{25,1},{2,10},{10... | collective-permute-start | bytes 786440 | tf_op jit(solution)/shard_map/ppermute | solution.py:321
  21.3 18.7 %collective-permute-start.4 = (bf16[2,2,64,512]{3,2,1,0:T(8,128)(2,1)S(1)}, bf16[2,2,64,512]{3,2,1,0:T(8,128)(2,1)S(1)}, u32[]{:S(2)}, u32[]{:S(2)}) collective-permute-start(bf16[2,2,64,512]{3,2,1,0:T(8,128)(2,1)S(1)} %get-tuple-element.103), channel_id=1, source_target_pairs={{0,16},{8,24},{16,0},{24,8},{1,17},{9,25},{17,1},{25,9},{2,18},{10... | collective-permute-start | bytes 786440 | tf_op jit(solution)/shard_map/ppermute | solution.py:321
  39.9 9.2 %collective-permute-start.5 = (bf16[4,2,64,512]{3,2,1,0:T(8,128)(2,1)S(1)}, bf16[4,2,64,512]{3,2,1,0:T(8,128)(2,1)S(1)}, u32[]{:S(2)}, u32[]{:S(2)}) collective-permute-start(bf16[4,2,64,512]{3,2,1,0:T(8,128)(2,1)S(1)} %collective-permute-done.1), channel_id=1, source_target_pairs={{0,2},{1,5},{2,0},{3,7},{4,6},{5,1},{6,4},{7,3},{8,10},{9,13},{10,... | collective-permute-start | bytes 1572872 | tf_op jit(solution)/shard_map/ppermute | solution.py:361
  40.5 7.9 %collective-permute-start.6 = (bf16[2,2,64,512]{3,2,1,0:T(8,128)(2,1)S(1)}, bf16[2,2,64,512]{3,2,1,0:T(8,128)(2,1)S(1)}, u32[]{:S(2)}, u32[]{:S(2)}) collective-permute-start(bf16[2,2,64,512]{3,2,1,0:T(8,128)(2,1)S(1)} %get-tuple-element.112), channel_id=1, source_target_pairs={{0,24},{8,0},{16,8},{24,16},{1,25},{9,1},{17,9},{25,17},{2,26},{10... | collective-permute-start | bytes 786440 | tf_op jit(solution)/shard_map/ppermute | solution.py:321
  49.2 5.3 %collective-permute-start.12 = (bf16[3,2,2,64,512]{4,3,2,1,0:T(8,128)(2,1)S(1)}, bf16[3,2,2,64,512]{4,3,2,1,0:T(8,128)(2,1)}, u32[]{:S(2)}, u32[]{:S(2)}) collective-permute-start(bf16[3,2,2,64,512]{4,3,2,1,0:T(8,128)(2,1)S(1)} %pad_maximum_fusion), channel_id=1, source_target_pairs={{0,1},{1,0},{2,3},{3,2},{4,5},{5,4},{6,7},{7,6},{8,9},{9,8},{10,11... | collective-permute-start | bytes 2359304 | tf_op jit(solution)/shard_map/ppermute | solution.py:324
  49.3 3.0 %collective-permute-start.11 = (bf16[4,2,64,512]{3,2,1,0:T(8,128)(2,1)S(1)}, bf16[4,2,64,512]{3,2,1,0:T(8,128)(2,1)S(1)}, u32[]{:S(2)}, u32[]{:S(2)}) collective-permute-start(bf16[4,2,64,512]{3,2,1,0:T(8,128)(2,1)S(1)} %get-tuple-element.126), channel_id=1, source_target_pairs={{0,1},{1,0},{2,3},{3,2},{4,5},{5,4},{6,7},{7,6},{8,9},{9,8},{10,11... | collective-permute-start | bytes 1572872 | tf_op jit(solution)/shard_map/ppermute | solution.py:324
  49.8 21.0 %collective-permute-start.7 = (bf16[3,2,2,64,512]{4,3,2,1,0:T(8,128)(2,1)S(1)}, bf16[3,2,2,64,512]{4,3,2,1,0:T(8,128)(2,1)}, u32[]{:S(2)}, u32[]{:S(2)}) collective-permute-start(bf16[3,2,2,64,512]{4,3,2,1,0:T(8,128)(2,1)S(1)} %pad_maximum_fusion), channel_id=1, source_target_pairs={{0,4},{1,3},{2,6},{3,1},{4,0},{5,7},{6,2},{7,5},{8,12},{9,11},{10,... | collective-permute-start | bytes 2359304 | tf_op jit(solution)/shard_map/ppermute | solution.py:361
  50.6 20.2 %collective-permute-start.8 = (bf16[3,2,2,64,512]{4,3,2,1,0:T(8,128)(2,1)S(1)}, bf16[3,2,2,64,512]{4,3,2,1,0:T(8,128)(2,1)}, u32[]{:S(2)}, u32[]{:S(2)}) collective-permute-start(bf16[3,2,2,64,512]{4,3,2,1,0:T(8,128)(2,1)S(1)} %pad_maximum_fusion), channel_id=1, source_target_pairs={{0,2},{1,5},{2,0},{3,7},{4,6},{5,1},{6,4},{7,3},{8,10},{9,13},{10,... | collective-permute-start | bytes 2359304 | tf_op jit(solution)/shard_map/ppermute | solution.py:361
  51.1 19.6 %collective-permute-start.10 = (bf16[2,2,64,512]{3,2,1,0:T(8,128)(2,1)}, bf16[2,2,64,512]{3,2,1,0:T(8,128)(2,1)}, u32[]{:S(2)}, u32[]{:S(2)}) collective-permute-start(bf16[2,2,64,512]{3,2,1,0:T(8,128)(2,1)} %get-tuple-element.124), channel_id=1, source_target_pairs={{0,16},{8,24},{16,0},{24,8},{1,17},{9,25},{17,1},{25,9},{2,18},{10... | collective-permute-start | bytes 786440 | tf_op jit(solution)/shard_map/ppermute | solution.py:321
  52.3 18.4 %collective-permute-start.9 = (bf16[2,2,64,512]{3,2,1,0:T(8,128)(2,1)}, bf16[2,2,64,512]{3,2,1,0:T(8,128)(2,1)}, u32[]{:S(2)}, u32[]{:S(2)}) collective-permute-start(bf16[2,2,64,512]{3,2,1,0:T(8,128)(2,1)} %get-tuple-element.123), channel_id=1, source_target_pairs={{0,8},{8,16},{16,24},{24,0},{1,9},{9,17},{17,25},{25,1},{2,10},{10... | collective-permute-start | bytes 786440 | tf_op jit(solution)/shard_map/ppermute | solution.py:321
  70.7 5.0 %collective-permute-start.16 = (bf16[3,2,2,64,512]{4,3,2,1,0:T(8,128)(2,1)}, bf16[3,2,2,64,512]{4,3,2,1,0:T(8,128)(2,1)S(1)}, u32[]{:S(2)}, u32[]{:S(2)}) collective-permute-start(bf16[3,2,2,64,512]{4,3,2,1,0:T(8,128)(2,1)} %collective-permute-done.7), channel_id=1, source_target_pairs={{0,1},{1,0},{2,3},{3,2},{4,5},{5,4},{6,7},{7,6},{8,9},{9,8},{10,11... | collective-permute-start | bytes 2359304 | tf_op jit(solution)/shard_map/ppermute | solution.py:324
  70.8 4.9 %collective-permute-start.18 = (bf16[3,2,2,64,512]{4,3,2,1,0:T(8,128)(2,1)}, bf16[3,2,2,64,512]{4,3,2,1,0:T(8,128)(2,1)S(1)}, u32[]{:S(2)}, u32[]{:S(2)}) collective-permute-start(bf16[3,2,2,64,512]{4,3,2,1,0:T(8,128)(2,1)} %collective-permute-done.8), channel_id=1, source_target_pairs={{0,1},{1,0},{2,3},{3,2},{4,5},{5,4},{6,7},{7,6},{8,9},{9,8},{10,11... | collective-permute-start | bytes 2359304 | tf_op jit(solution)/shard_map/ppermute | solution.py:324
  71.3 3.3 %collective-permute-start.15 = (bf16[4,2,64,512]{3,2,1,0:T(8,128)(2,1)S(1)}, bf16[4,2,64,512]{3,2,1,0:T(8,128)(2,1)S(1)}, u32[]{:S(2)}, u32[]{:S(2)}) collective-permute-start(bf16[4,2,64,512]{3,2,1,0:T(8,128)(2,1)S(1)} %collective-permute-done.1), channel_id=1, source_target_pairs={{0,1},{1,0},{2,3},{3,2},{4,5},{5,4},{6,7},{7,6},{8,9},{9,8},{10,11... | collective-permute-start | bytes 1572872 | tf_op jit(solution)/shard_map/ppermute | solution.py:324
  71.4 15.7 %collective-permute-start.13 = (bf16[3,2,2,64,512]{4,3,2,1,0:T(8,128)(2,1)}, bf16[3,2,2,64,512]{4,3,2,1,0:T(8,128)(2,1)S(1)}, u32[]{:S(2)}, u32[]{:S(2)}) collective-permute-start(bf16[3,2,2,64,512]{4,3,2,1,0:T(8,128)(2,1)} %collective-permute-done.7), channel_id=1, source_target_pairs={{0,2},{1,5},{2,0},{3,7},{4,6},{5,1},{6,4},{7,3},{8,10},{9,13},{10,... | collective-permute-start | bytes 2359304 | tf_op jit(solution)/shard_map/ppermute | solution.py:361
  72.9 2.8 %collective-permute-start.17 = (bf16[4,2,64,512]{3,2,1,0:T(8,128)(2,1)S(1)}, bf16[4,2,64,512]{3,2,1,0:T(8,128)(2,1)S(1)}, u32[]{:S(2)}, u32[]{:S(2)}) collective-permute-start(bf16[4,2,64,512]{3,2,1,0:T(8,128)(2,1)S(1)} %collective-permute-done.2), channel_id=1, source_target_pairs={{0,1},{1,0},{2,3},{3,2},{4,5},{5,4},{6,7},{7,6},{8,9},{9,8},{10,11... | collective-permute-start | bytes 1572872 | tf_op jit(solution)/shard_map/ppermute | solution.py:324
  74.6 12.5 %collective-permute-start.14 = (bf16[2,2,64,512]{3,2,1,0:T(8,128)(2,1)}, bf16[2,2,64,512]{3,2,1,0:T(8,128)(2,1)S(1)}, u32[]{:S(2)}, u32[]{:S(2)}) collective-permute-start(bf16[2,2,64,512]{3,2,1,0:T(8,128)(2,1)} %copy-done.1), channel_id=1, source_target_pairs={{0,24},{8,0},{16,8},{24,16},{1,25},{9,1},{17,9},{25,17},{2,26},{10... | collective-permute-start | bytes 786440 | tf_op jit(solution)/shard_map/ppermute | solution.py:321
  88.2 4.8 %collective-permute-start.22 = (bf16[3,2,2,64,512]{4,3,2,1,0:T(8,128)(2,1)S(1)}, bf16[3,2,2,64,512]{4,3,2,1,0:T(8,128)(2,1)S(1)}, u32[]{:S(2)}, u32[]{:S(2)}) collective-permute-start(bf16[3,2,2,64,512]{4,3,2,1,0:T(8,128)(2,1)S(1)} %collective-permute-done.13), channel_id=1, source_target_pairs={{0,1},{1,0},{2,3},{3,2},{4,5},{5,4},{6,7},{7,6},{8,9},{9,8},{10,11... | collective-permute-start | bytes 2359304 | tf_op jit(solution)/shard_map/ppermute | solution.py:324
  88.4 4.6 %collective-permute-start.23 = (bf16[3,2,2,64,512]{4,3,2,1,0:T(8,128)(2,1)S(1)}, bf16[3,2,2,64,512]{4,3,2,1,0:T(8,128)(2,1)S(1)}, u32[]{:S(2)}, u32[]{:S(2)}) collective-permute-start(bf16[3,2,2,64,512]{4,3,2,1,0:T(8,128)(2,1)S(1)} %pad_maximum_fusion.1), channel_id=1, source_target_pairs={{0,1},{1,0},{2,3},{3,2},{4,5},{5,4},{6,7},{7,6},{8,9},{9,8},{10,11... | collective-permute-start | bytes 2359304 | tf_op jit(solution)/shard_map/ppermute | solution.py:324
  88.8 20.1 %collective-permute-start.19 = (bf16[3,2,2,64,512]{4,3,2,1,0:T(8,128)(2,1)S(1)}, bf16[3,2,2,64,512]{4,3,2,1,0:T(8,128)(2,1)S(1)}, u32[]{:S(2)}, u32[]{:S(2)}) collective-permute-start(bf16[3,2,2,64,512]{4,3,2,1,0:T(8,128)(2,1)S(1)} %pad_maximum_fusion.1), channel_id=1, source_target_pairs={{0,4},{1,3},{2,6},{3,1},{4,0},{5,7},{6,2},{7,5},{8,12},{9,11},{10,... | collective-permute-start | bytes 2359304 | tf_op jit(solution)/shard_map/ppermute | solution.py:361
  90.1 18.8 %collective-permute-start.20 = (bf16[3,2,2,64,512]{4,3,2,1,0:T(8,128)(2,1)S(1)}, bf16[3,2,2,64,512]{4,3,2,1,0:T(8,128)(2,1)S(1)}, u32[]{:S(2)}, u32[]{:S(2)}) collective-permute-start(bf16[3,2,2,64,512]{4,3,2,1,0:T(8,128)(2,1)S(1)} %pad_maximum_fusion.1), channel_id=1, source_target_pairs={{0,2},{1,5},{2,0},{3,7},{4,6},{5,1},{6,4},{7,3},{8,10},{9,13},{10,... | collective-permute-start | bytes 2359304 | tf_op jit(solution)/shard_map/ppermute | solution.py:361
  91.1 1.9 %collective-permute-start.21 = (bf16[4,2,64,512]{3,2,1,0:T(8,128)(2,1)S(1)}, bf16[4,2,64,512]{3,2,1,0:T(8,128)(2,1)S(1)}, u32[]{:S(2)}, u32[]{:S(2)}) collective-permute-start(bf16[4,2,64,512]{3,2,1,0:T(8,128)(2,1)S(1)} %collective-permute-done.5), channel_id=1, source_target_pairs={{0,1},{1,0},{2,3},{3,2},{4,5},{5,4},{6,7},{7,6},{8,9},{9,8},{10,11... | collective-permute-start | bytes 1572872 | tf_op jit(solution)/shard_map/ppermute | solution.py:324
  108.9 2.3 %collective-permute-start.25 = (bf16[3,2,2,64,512]{4,3,2,1,0:T(8,128)(2,1)S(1)}, bf16[3,2,2,64,512]{4,3,2,1,0:T(8,128)(2,1)S(1)}, u32[]{:S(2)}, u32[]{:S(2)}) collective-permute-start(bf16[3,2,2,64,512]{4,3,2,1,0:T(8,128)(2,1)S(1)} %collective-permute-done.19), channel_id=1, source_target_pairs={{0,1},{1,0},{2,3},{3,2},{4,5},{5,4},{6,7},{7,6},{8,9},{9,8},{10,11... | collective-permute-start | bytes 2359304 | tf_op jit(solution)/shard_map/ppermute | solution.py:324
  109.0 3.3 %collective-permute-start.26 = (bf16[3,2,2,64,512]{4,3,2,1,0:T(8,128)(2,1)S(1)}, bf16[3,2,2,64,512]{4,3,2,1,0:T(8,128)(2,1)S(1)}, u32[]{:S(2)}, u32[]{:S(2)}) collective-permute-start(bf16[3,2,2,64,512]{4,3,2,1,0:T(8,128)(2,1)S(1)} %collective-permute-done.20), channel_id=1, source_target_pairs={{0,1},{1,0},{2,3},{3,2},{4,5},{5,4},{6,7},{7,6},{8,9},{9,8},{10,11... | collective-permute-start | bytes 2359304 | tf_op jit(solution)/shard_map/ppermute | solution.py:324
  109.4 16.5 %collective-permute-start.24 = (bf16[3,2,2,64,512]{4,3,2,1,0:T(8,128)(2,1)S(1)}, bf16[3,2,2,64,512]{4,3,2,1,0:T(8,128)(2,1)S(1)}, u32[]{:S(2)}, u32[]{:S(2)}) collective-permute-start(bf16[3,2,2,64,512]{4,3,2,1,0:T(8,128)(2,1)S(1)} %collective-permute-done.19), channel_id=1, source_target_pairs={{0,2},{1,5},{2,0},{3,7},{4,6},{5,1},{6,4},{7,3},{8,10},{9,13},{10,... | collective-permute-start | bytes 2359304 | tf_op jit(solution)/shard_map/ppermute | solution.py:361
  125.9 2.4 %collective-permute-start.27 = (bf16[3,2,2,64,512]{4,3,2,1,0:T(8,128)(2,1)S(1)}, bf16[3,2,2,64,512]{4,3,2,1,0:T(8,128)(2,1)S(1)}, u32[]{:S(2)}, u32[]{:S(2)}) collective-permute-start(bf16[3,2,2,64,512]{4,3,2,1,0:T(8,128)(2,1)S(1)} %collective-permute-done.24), channel_id=1, source_target_pairs={{0,1},{1,0},{2,3},{3,2},{4,5},{5,4},{6,7},{7,6},{8,9},{9,8},{10,11... | collective-permute-start | bytes 2359304 | tf_op jit(solution)/shard_map/ppermute | solution.py:324

commit v3 on v2

--- a/solution.py
+++ b/solution.py
@@ -12,7 +12,8 @@
 VOLT_SCALE = 1.0 / 256.0
 GROUP = 16
 MIB = 1 << 20
-CORRELATE_VMEM = 16 * MIB
+CHANNELIZE_VMEM = 32 * MIB
+CORRELATE_VMEM = 18 * MIB
 ANY = pl.BlockSpec(memory_space=pl.ANY)
 HBM = pl.BlockSpec(memory_space=pltpu.HBM)
 TOKEN = jax.ShapeDtypeStruct((8, 128), jnp.float32)
@@ -67,12 +68,16 @@
         column = lax.broadcasted_iota(jnp.int32, (group, 2 * span), 1)
         column = jnp.where(column >= span, column - span, column) // chans
         row = lax.broadcasted_iota(jnp.int32, (group, 2 * span), 0)
+        sample = lax.broadcasted_iota(jnp.int32, (chans, 2 * span), 1) % chans
+        spread = (sample == lax.broadcasted_iota(jnp.int32, (chans, 2 * span), 0)).astype(jnp.float32)
+        spread_taps = jnp.dot(taps[...], spread, precision=lax.Precision.HIGHEST, preferred_element_type=jnp.float32)
+        first = lax.axis_index("chan") * (chans // lax.axis_size("chan"))
         band = jnp.zeros((group, 2 * span), jnp.float32)
         for k in range(tap_count):
-            band = band + jnp.where(column == row + (tap_count - 1 - k), taps[k : k + 1, :], 0.0)
-        for c in range(table.shape[0]):
+            band = band + jnp.where(column == row + (tap_count - 1 - k), spread_taps[k : k + 1, :], 0.0)
+        for c in range(chans):
             for p in range(2):
-                exact = table[c, p : p + 1, :] * band
+                exact = table[first + c, p : p + 1, :] * band
                 high = exact.astype(jnp.bfloat16)
                 at = (2 * c + p) * group
                 weights[0, at : at + group, :] = high
@@ -114,7 +119,7 @@
     cost = 2 * 2 * GROUP * (chans * 2) * (2 * span) * width
     held = pltpu.VMEM((2 * span, width), jnp.bfloat16)
     block = (2, GROUP, chans, width)
-    params = pltpu.CompilerParams(vmem_limit_bytes=32 * MIB)
+    params = pltpu.CompilerParams(vmem_limit_bytes=CHANNELIZE_VMEM)
     *outs, weights = pl.pallas_call(
         functools.partial(channelize_inner, layout, tap_count),
         grid=(groups - 1,),
@@ -167,20 +172,19 @@
     out, _ = take(2)
     made = [None if has_left else take(1)[0] for _, _, has_left in works]
     panel, left, results, sems, left_sems, out_sems = refs
-    slots, depth, width = panel.shape
-    rows = 2 * frames
+    slots, distances, rows, width = panel.shape
+    depth = distances * rows
     units = [(w, job, c, half) for w, (channels, jobs, _) in enumerate(works) for job in jobs for c in range(len(channels)) for half in (0, 1)]
 
     def arrivals(u):
         w, job, c, half = units[u]
         at = 0
-        for ref in operands[w, job][half]:
+        for i, ref in enumerate(operands[w, job][half]):
             first = works[w][0][0] if ref.shape[1] > len(works[w][0]) else 0
-            for d in range(ref.shape[0]):
-                yield pltpu.make_async_copy(
-                    ref.at[d, first + c], panel.at[u % slots, pl.ds(at * rows, rows)], sems.at[u % slots, at]
-                )
-                at += 1
+            yield pltpu.make_async_copy(
+                ref.at[:, first + c], panel.at[u % slots, pl.ds(at, ref.shape[0])], sems.at[u % slots, i]
+            )
+            at += ref.shape[0]
 
     def departures(u):
         w, job, c, half = units[u]
@@ -213,9 +217,10 @@
             if stored[w] is not None:
                 stored_rows(w, c).wait()
             else:
-                for at in range(0, depth, rows):
-                    real = panel[u % slots, at : at + frames].T
-                    imag = panel[u % slots, at + frames : at + rows].T
+                for d in range(distances):
+                    at = d * rows
+                    real = panel[u % slots, d, :frames].T
+                    imag = panel[u % slots, d, frames:].T
                     left[w, c, :width, at : at + rows] = jnp.concatenate([real, imag], 1)
                     left[w, c, width:, at : at + rows] = jnp.concatenate([imag, -real], 1)
                 made_rows(w, c).start()
@@ -224,7 +229,7 @@
                 copy.wait()
         for p, copy in enumerate(departures(u)):
             lines = left[w, c, p * width : (p + 1) * width]
-            result = jnp.dot(lines, panel[u % slots], preferred_element_type=jnp.float32) * scale
+            result = jnp.dot(lines, panel[u % slots].reshape(depth, width), preferred_element_type=jnp.float32) * scale
             results[(2 * u + p) % results.shape[0]] = result
             copy.start()
         later = u + slots
@@ -255,7 +260,7 @@
     channels = max(len(channels) for channels, _, _ in works)
     made = [struct((len(c), 2 * width, depth)) for c, left, _ in works if left is None]
     shape = ([(tuple(c), tuple(jobs), left is not None) for c, left, jobs in works], frames, has_out, 2.0 / depth)
-    slots, results = 4, 4
+    slots, results = 4, 8
     out, token, *made = pl.pallas_call(
         functools.partial(correlate_step, shape),
         in_specs=[pl.BlockSpec(memory_space=pltpu.SMEM), ANY] + [HBM] * (len(operands) + len(lefts) + has_out),
@@ -263,10 +268,10 @@
         out_shape=[whole, TOKEN] + made,
         input_output_aliases={1: 1, **({2 + len(operands) + len(lefts): 0} if has_out else {})},
         scratch_shapes=[
-            pltpu.VMEM((slots, depth, width), jnp.bfloat16),
+            pltpu.VMEM((slots, depth // (2 * frames), 2 * frames, width), jnp.bfloat16),
             pltpu.VMEM((len(works), channels, 2 * width, depth), jnp.bfloat16),
             pltpu.VMEM((results, width, width), jnp.float32),
-            pltpu.SemaphoreType.DMA((slots, depth // (2 * frames))),
+            pltpu.SemaphoreType.DMA((slots, 2)),
             pltpu.SemaphoreType.DMA((len(works), channels)),
             pltpu.SemaphoreType.DMA((results,)),
         ],
@@ -302,20 +307,18 @@
     tap_count = fir_taps.shape[0]
     devices, count = lax.axis_size("chan"), lax.axis_size("inp")
     mine = chans // devices
-    plane, place = lax.axis_index("chan"), lax.axis_index("inp")
+    place = lax.axis_index("inp")
 
     rim = voltages[:, frames - (tap_count - 1) :].astype(jnp.bfloat16)
     rim = lax.ppermute(rim, "chan", [(i, i + 1) for i in range(devices - 1)])
     table = transform_rows(chans, GROUP + tap_count - 1)
-    table = lax.dynamic_slice_in_dim(jnp.asarray(table), plane * mine, chans, 0)
-    taps = jnp.tile(fir_taps, (1, 2 * (GROUP + tap_count - 1)))
     sources = np.array([[i ^ m for m in source_masks(count, i % 2)] for i in range(count)], np.int32)
     sources = np.stack([sources, sources[np.arange(count) ^ 1]], 2)
     sources = lax.dynamic_index_in_dim(jnp.asarray(sources), place, 0, keepdims=False)
 
     halves = [range(mine)] if mine < 2 else [range(mine // 2), range(mine // 2, mine)]
     layout = [(0, range(mine))] + [(d, half) for half in halves for d in range(1, devices)]
-    firsts = channelize(voltages, rim, table, taps, layout)
+    firsts = channelize(voltages, rim, jnp.asarray(table), fir_taps, layout)
 
     def turned(piece, d):
         return lax.ppermute(piece, "chan", [(i, (i + d) % devices) for i in range(devices)])

time: 137 us -> 129 us (0.942)
  Pallas kernels: 61.2 us -> 48.8 us
  waiting for transfers between devices: 43.1 us -> 47.7 us
    pallas_call x5, Pallas kernels: 55 us -> 42.5 us  [correlate(): pl.pallas_call(functools.partial(correlate_step, shape), in_specs=[pl.Blo...]
    ppermute x9, waiting for transfers between devices: 2.12 us -> 5.73 us  [one_round(): lax.ppermute(block, 'inp', [(i, i ^ orders[i % 2][step]) for i in range(c...]
    unnamed x4 -> x8, local copies, waits for them, and re-layouts: 2.9 us -> 4.5 us
  transfers between devices with their start and end apart: 28 -> 28, of which waited for: 13 -> 13; matrix products, arithmetic and copies ran while one was open for 2% -> 1% of each run, Pallas kernels for 38% -> 32%
where the time goes in v3:
time: 129 us; the launch traced here: 128 us
  Pallas kernels  48.8 us (38%)
  waiting for transfers between devices  47.7 us (37%)
  starting transfers between devices  24.1 us (19%)
  local copies, waits for them, and re-layouts  5.27 us (4%)
  other arithmetic  2.15 us (2%)
    pallas_call x5, Pallas kernels, correlate(): pl.pallas_call(functools.partial(correlate_step, shape), in_specs=[pl.Blo...  42.5 us
    ppermute x6, waiting for transfers between devices, turned(): lax.ppermute(piece, 'chan', [(i, (i + d) % devices) for i in range(device...  33.2 us
    ppermute x9, starting transfers between devices, one_round(): lax.ppermute(block, 'inp', [(i, i ^ orders[i % 2][step]) for i in range(c...  9.89 us
    ppermute x12, waiting for transfers between devices, swapped(): return lax.ppermute(block, 'inp', [(i, i ^ 1) for i in range(count)])  8.72 us
    ppermute x6, starting transfers between devices, turned(): lax.ppermute(piece, 'chan', [(i, (i + d) % devices) for i in range(device...  6.79 us
    ppermute x9, waiting for transfers between devices, one_round(): lax.ppermute(block, 'inp', [(i, i ^ orders[i % 2][step]) for i in range(c...  5.73 us
    ppermute x1, starting transfers between devices, body(): rim = lax.ppermute(rim, 'chan', [(i, i + 1) for i in range(devices - 1)])  4.93 us
    pallas_call x1, Pallas kernels, channelize(): pl.pallas_call(functools.partial(channelize_inner, layout, tap_count), gr...  4.58 us
  transfers between devices with their start and end apart: 28, of which 13 were waited for; matrix products, arithmetic and copies ran while one was open for 1% of the time, Pallas kernels for 32%

profile of v3, /device:TPU:0, one launch (start us, length us, event | category | flops | bytes accessed | tf_op | source)
XLA Modules:
  0.0 128.4 jit_solution(12064178151693312010)
XLA Ops:
  0.0 0.9 slice_convert_fusion
  0.9 4.9 %collective-permute-start = (bf16[2,3,16,512]{3,2,1,0:T(8,128)(2,1)S(1)}, bf16[2,3,16,512]{3,2,1,0:T(8,128)(2,1)S(1)}, u32[]{:S(2)}, u32[]{:S(2)}) collective-permute-start(bf16[2,3,16,512]{3,2,1,0:T(8,128)(2,1)S(1)} %slice_convert_fusion), channel_id=1, source_target_pairs={{0,8},{8,16},{16,24},{1,9},{9,17},{17,25},{2,10},{10,18},{18,26},{... | collective-permute-start | bytes 294920 | tf_op jit(solution)/shard_map/ppermute | solution.py:313
  5.9 2.2 %copy-done = s32[2,64,16,512]{3,2,1,0:T(8,128)S(1)} copy-done((s32[2,64,16,512]{3,2,1,0:T(8,128)S(1)}, s32[2,64,16,512]{3,2,1,0:T(8,128)}, u32[]{:S(2)}) %copy-start) | copy-done | bytes 4194328
  8.1 0.7 copy-done.2
  8.8 0.9 copy-done.3
  9.7 4.6 %channelize_inner.1 = (bf16[4,2,64,512]{3,2,1,0:T(8,128)(2,1)S(1)}, bf16[2,2,64,512]{3,2,1,0:T(8,128)(2,1)S(1)}, bf16[2,2,64,512]{3,2,1,0:T(8,128)(2,1)S(1)}, bf...) custom-call(s32[2,64,16,512]{3,2,1,0:T(8,128)S(1)} %copy-done, ...), custom_call_target="tpu_custom_call" | custom-call | flops 1912602624 | bytes 6291456 | tf_op jit(solution)/shard_map/channelize_inner/pallas_call | solution.py:123
  14.3 1.7 %channelize_first.1 = (bf16[4,2,64,512]{3,2,1,0:T(8,128)(2,1)S(1)}, bf16[2,2,64,512]{3,2,1,0:T(8,128)(2,1)S(1)}, bf16[2,2,64,512]{3,2,1,0:T(8,128)(2,1)S(1)}, bf...) custom-call(s32[2,64,16,512]{3,2,1,0:T(8,128)S(1)} %copy-done, ...), custom_call_target="tpu_custom_call", output_to_operand_aliasing={{0}: (3, {}), {1}: (4, {}), {2}: (5, {}), {3}: (6, {}), {4}... | custom-call | flops 637534208 | bytes 1572864 | tf_op jit(solution)/shard_map/channelize_first/pallas_call | solution.py:146
  16.0 0.7 copy-done.1
  16.8 1.5 %collective-permute-start.1 = (bf16[4,2,64,512]{3,2,1,0:T(8,128)(2,1)S(1)}, bf16[4,2,64,512]{3,2,1,0:T(8,128)(2,1)S(1)}, u32[]{:S(2)}, u32[]{:S(2)}) collective-permute-start(bf16[4,2,64,512]{3,2,1,0:T(8,128)(2,1)S(1)} %get-tuple-element.126), channel_id=1, source_target_pairs={{0,4},{1,3},{2,6},{3,1},{4,0},{5,7},{6,2},{7,5},{8,12},{9,11},{10,... | collective-permute-start | bytes 1572872 | tf_op jit(solution)/shard_map/ppermute | solution.py:364
  18.2 1.5 %collective-permute-start.2 = (bf16[4,2,64,512]{3,2,1,0:T(8,128)(2,1)S(1)}, bf16[4,2,64,512]{3,2,1,0:T(8,128)(2,1)S(1)}, u32[]{:S(2)}, u32[]{:S(2)}) collective-permute-start(bf16[4,2,64,512]{3,2,1,0:T(8,128)(2,1)S(1)} %get-tuple-element.126), channel_id=1, source_target_pairs={{0,2},{1,5},{2,0},{3,7},{4,6},{5,1},{6,4},{7,3},{8,10},{9,13},{10,... | collective-permute-start | bytes 1572872 | tf_op jit(solution)/shard_map/ppermute | solution.py:364
  19.7 1.6 %collective-permute-start.3 = (bf16[2,2,64,512]{3,2,1,0:T(8,128)(2,1)S(1)}, bf16[2,2,64,512]{3,2,1,0:T(8,128)(2,1)S(1)}, u32[]{:S(2)}, u32[]{:S(2)}) collective-permute-start(bf16[2,2,64,512]{3,2,1,0:T(8,128)(2,1)S(1)} %get-tuple-element.102), channel_id=1, source_target_pairs={{0,8},{8,16},{16,24},{24,0},{1,9},{9,17},{17,25},{25,1},{2,10},{10... | collective-permute-start | bytes 786440 | tf_op jit(solution)/shard_map/ppermute | solution.py:324
  21.3 1.0 collective-permute-start.4
  22.3 8.5 %collective-permute-done.3 = bf16[2,2,64,512]{3,2,1,0:T(8,128)(2,1)S(1)} collective-permute-done((bf16[2,2,64,512]{3,2,1,0:T(8,128)(2,1)S(1)}, bf16[2,2,64,512]{3,2,1,0:T(8,128)(2,1)S(1)}, u32[]{:S(2)}, u32[]{:S(2)}) %collective-permute-start.3) | collective-permute-done | bytes 262176 | tf_op jit(solution)/shard_map/ppermute | solution.py:324
  30.9 9.1 %collective-permute-done.4 = bf16[2,2,64,512]{3,2,1,0:T(8,128)(2,1)S(1)} collective-permute-done((bf16[2,2,64,512]{3,2,1,0:T(8,128)(2,1)S(1)}, bf16[2,2,64,512]{3,2,1,0:T(8,128)(2,1)S(1)}, u32[]{:S(2)}, u32[]{:S(2)}) %collective-permute-start.4) | collective-permute-done | bytes 262176 | tf_op jit(solution)/shard_map/ppermute | solution.py:324
  40.0 0.5 collective-permute-start.5
  40.5 1.7 %collective-permute-start.6 = (bf16[2,2,64,512]{3,2,1,0:T(8,128)(2,1)S(1)}, bf16[2,2,64,512]{3,2,1,0:T(8,128)(2,1)S(1)}, u32[]{:S(2)}, u32[]{:S(2)}) collective-permute-start(bf16[2,2,64,512]{3,2,1,0:T(8,128)(2,1)S(1)} %get-tuple-element.112), channel_id=1, source_target_pairs={{0,24},{8,0},{16,8},{24,16},{1,25},{9,1},{17,9},{25,17},{2,26},{10... | collective-permute-start | bytes 786440 | tf_op jit(solution)/shard_map/ppermute | solution.py:324
  42.2 6.2 %collective-permute-done.6 = bf16[2,2,64,512]{3,2,1,0:T(8,128)(2,1)S(1)} collective-permute-done((bf16[2,2,64,512]{3,2,1,0:T(8,128)(2,1)S(1)}, bf16[2,2,64,512]{3,2,1,0:T(8,128)(2,1)S(1)}, u32[]{:S(2)}, u32[]{:S(2)}) %collective-permute-start.6) | collective-permute-done | bytes 262176 | tf_op jit(solution)/shard_map/ppermute | solution.py:324
  48.4 0.7 collective-permute-done.5
  49.3 0.5 collective-permute-start.11
  49.8 0.8 collective-permute-start.7
  50.6 0.5 collective-permute-start.8
  51.2 1.2 collective-permute-done.11
  52.4 1.4 %collective-permute-start.9 = (bf16[2,2,64,512]{3,2,1,0:T(8,128)(2,1)}, bf16[2,2,64,512]{3,2,1,0:T(8,128)(2,1)}, u32[]{:S(2)}, u32[]{:S(2)}) collective-permute-start(bf16[2,2,64,512]{3,2,1,0:T(8,128)(2,1)} %get-tuple-element.123), channel_id=1, source_target_pairs={{0,8},{8,16},{16,24},{24,0},{1,9},{9,17},{17,25},{25,1},{2,10},{10... | collective-permute-start | bytes 786440 | tf_op jit(solution)/shard_map/ppermute | solution.py:324
  53.8 0.7 dynamic-slice_bitcast_fusion
  54.6 6.8 %correlate.5 = (f32[4,2,512,4096]{3,2,1,0:T(8,128)}, f32[8,128]{1,0:T(8,128)S(1)}, bf16[2,1024,512]{2,1,0:T(8,128)(2,1)S(1)}) custom-call(s32[4,2]{1,0:T(4,128)S(1)} %copy.25.where, f32[8,128]{1,0:T(8,128)S(1)} %broadcast_in_dim.3.token, bf16[1,4,128,512]{3,2,1,0:T(8,128)(2,1)S(1)} %bitcast.32, ...), custom_call_target="tpu_custom_call", output_to_operand_aliasing={{1}: (1, {})} | custom-call | tf_op jit(solution)/shard_map/correlate/pallas_call | solution.py:264
  61.4 9.4 %collective-permute-done.10 = bf16[2,2,64,512]{3,2,1,0:T(8,128)(2,1)} collective-permute-done((bf16[2,2,64,512]{3,2,1,0:T(8,128)(2,1)}, bf16[2,2,64,512]{3,2,1,0:T(8,128)(2,1)}, u32[]{:S(2)}, u32[]{:S(2)}) %collective-permute-start.10) | collective-permute-done | bytes 262176 | tf_op jit(solution)/shard_map/ppermute | solution.py:324
  70.9 0.5 collective-permute-start.18
  71.5 1.5 %collective-permute-start.13 = (bf16[3,2,2,64,512]{4,3,2,1,0:T(8,128)(2,1)}, bf16[3,2,2,64,512]{4,3,2,1,0:T(8,128)(2,1)S(1)}, u32[]{:S(2)}, u32[]{:S(2)}) collective-permute-start(bf16[3,2,2,64,512]{4,3,2,1,0:T(8,128)(2,1)} %collective-permute-done.7), channel_id=1, source_target_pairs={{0,2},{1,5},{2,0},{3,7},{4,6},{5,1},{6,4},{7,3},{8,10},{9,13},{10,... | collective-permute-start | bytes 2359304 | tf_op jit(solution)/shard_map/ppermute | solution.py:364
  73.0 1.7 %collective-permute-done.15 = bf16[4,2,64,512]{3,2,1,0:T(8,128)(2,1)S(1)} collective-permute-done((bf16[4,2,64,512]{3,2,1,0:T(8,128)(2,1)S(1)}, bf16[4,2,64,512]{3,2,1,0:T(8,128)(2,1)S(1)}, u32[]{:S(2)}, u32[]{:S(2)}) %collective-permute-start.15) | collective-permute-done | bytes 524320 | tf_op jit(solution)/shard_map/ppermute | solution.py:327
  74.6 1.0 collective-permute-start.14
  75.8 9.5 %correlate.6 = (f32[4,2,512,4096]{3,2,1,0:T(8,128)}, f32[8,128]{1,0:T(8,128)S(1)}) custom-call(s32[4,2]{1,0:T(4,128)S(1)} %copy.25.where, f32[8,128]{1,0:T(8,128)S(1)} %get-tuple-element.137.token, bf16[1,4,128,512]{3,2,1,0:T(8,128)(2,1)S(1)} %bitcast.36, bf16[3,2,128,512]{3,2,1,0:T(8,128)(2,1)} %bitcast.11.refs_1_, ...), custom_call_target="tpu_custom_call", output_to_operand_aliasing={{1}: (1, {}), {0}: (11, {})} | custom-call | tf_op jit(solution)/shard_map/correlate/pallas_call | solution.py:264
  85.3 1.1 pad_maximum_fusion.1
  86.4 0.2 collective-permute-start.22
  86.6 0.4 collective-permute-start.23
  87.0 1.3 %collective-permute-start.19 = (bf16[3,2,2,64,512]{4,3,2,1,0:T(8,128)(2,1)S(1)}, bf16[3,2,2,64,512]{4,3,2,1,0:T(8,128)(2,1)S(1)}, u32[]{:S(2)}, u32[]{:S(2)}) collective-permute-start(bf16[3,2,2,64,512]{4,3,2,1,0:T(8,128)(2,1)S(1)} %pad_maximum_fusion.1), channel_id=1, source_target_pairs={{0,4},{1,3},{2,6},{3,1},{4,0},{5,7},{6,2},{7,5},{8,12},{9,11},{10,... | collective-permute-start | bytes 2359304 | tf_op jit(solution)/shard_map/ppermute | solution.py:364
  88.3 1.0 collective-permute-start.20
  89.3 1.9 %collective-permute-done.21 = bf16[4,2,64,512]{3,2,1,0:T(8,128)(2,1)S(1)} collective-permute-done((bf16[4,2,64,512]{3,2,1,0:T(8,128)(2,1)S(1)}, bf16[4,2,64,512]{3,2,1,0:T(8,128)(2,1)S(1)}, u32[]{:S(2)}, u32[]{:S(2)}) %collective-permute-start.21) | collective-permute-done | bytes 524320 | tf_op jit(solution)/shard_map/ppermute | solution.py:327
  91.2 10.9 %correlate.7 = (f32[4,2,512,4096]{3,2,1,0:T(8,128)}, f32[8,128]{1,0:T(8,128)S(1)}, bf16[2,1024,512]{2,1,0:T(8,128)(2,1)S(1)}) custom-call(s32[4,2]{1,0:T(4,128)S(1)} %copy.25.where, f32[8,128]{1,0:T(8,128)S(1)} %get-tuple-element.152.token, bf16[1,4,128,512]{3,2,1,0:T(8,128)(2,1)S(1)} %bitcast.40, ...), custom_call_target="tpu_custom_call", output_to_operand_aliasing={{1}: (1, {}), {0}: (11, {})} | custom-call | tf_op jit(solution)/shard_map/correlate/pallas_call | solution.py:264
  102.1 5.0 %collective-permute-done.19 = bf16[3,2,2,64,512]{4,3,2,1,0:T(8,128)(2,1)S(1)} collective-permute-done((bf16[3,2,2,64,512]{4,3,2,1,0:T(8,128)(2,1)S(1)}, bf16[3,2,2,64,512]{4,3,2,1,0:T(8,128)(2,1)S(1)}, u32[]{:S(2)}, u32[]{:S(2)}) %collective-permute-start.19) | collective-permute-done | bytes 786464 | tf_op jit(solution)/shard_map/ppermute | solution.py:364
  107.1 0.1 collective-permute-start.25
  107.2 0.4 collective-permute-start.26
  107.6 1.2 collective-permute-start.24
  108.8 0.6 collective-permute-done.25
  109.4 1.1 collective-permute-done.26
  110.5 9.7 %correlate.8 = (f32[4,2,512,4096]{3,2,1,0:T(8,128)}, f32[8,128]{1,0:T(8,128)S(1)}) custom-call(s32[4,2]{1,0:T(4,128)S(1)} %copy.25.where, f32[8,128]{1,0:T(8,128)S(1)} %get-tuple-element.162.token, bf16[1,4,128,512]{3,2,1,0:T(8,128)(2,1)S(1)} %bitcast.37, bf16[3,2,128,512]{3,2,1,0:T(8,128)(2,1)S(1)} %bitcast.51, ...), custom_call_target="tpu_custom_call", output_to_operand_aliasing={{1}: (1, {}), {0}: (11, {})} | custom-call | tf_op jit(solution)/shard_map/correlate/pallas_call | solution.py:264
  120.2 0.2 collective-permute-start.27
  120.4 2.1 %collective-permute-done.27 = bf16[3,2,2,64,512]{4,3,2,1,0:T(8,128)(2,1)S(1)} collective-permute-done((bf16[3,2,2,64,512]{4,3,2,1,0:T(8,128)(2,1)S(1)}, bf16[3,2,2,64,512]{4,3,2,1,0:T(8,128)(2,1)S(1)}, u32[]{:S(2)}, u32[]{:S(2)}) %collective-permute-start.27) | collective-permute-done | bytes 786464 | tf_op jit(solution)/shard_map/ppermute | solution.py:327
  122.5 5.7 %correlate.9 = (f32[4,2,512,4096]{3,2,1,0:T(8,128)}, f32[8,128]{1,0:T(8,128)S(1)}) custom-call(s32[4,2]{1,0:T(4,128)S(1)} %copy.25.where, f32[8,128]{1,0:T(8,128)S(1)} %get-tuple-element.168.token, bf16[1,4,128,512]{3,2,1,0:T(8,128)(2,1)S(1)} %bitcast.41, bf16[3,2,128,512]{3,2,1,0:T(8,128)(2,1)S(1)} %bitcast.54, ...), custom_call_target="tpu_custom_call", output_to_operand_aliasing={{1}: (1, {}), {0}: (7, {})} | custom-call | tf_op jit(solution)/shard_map/correlate/pallas_call | solution.py:264
  (29 shorter events, 0.6 us)
Async XLA Ops:
  0.9 13.3 %collective-permute-start = (bf16[2,3,16,512]{3,2,1,0:T(8,128)(2,1)S(1)}, bf16[2,3,16,512]{3,2,1,0:T(8,128)(2,1)S(1)}, u32[]{:S(2)}, u32[]{:S(2)}) collective-permute-start(bf16[2,3,16,512]{3,2,1,0:T(8,128)(2,1)S(1)} %slice_convert_fusion), channel_id=1, source_target_pairs={{0,8},{8,16},{16,24},{1,9},{9,17},{17,25},{2,10},{10,18},{18,26},{... | collective-permute-start | bytes 294920 | tf_op jit(solution)/shard_map/ppermute | solution.py:313
  5.9 2.2 %copy-start = (s32[2,64,16,512]{3,2,1,0:T(8,128)S(1)}, s32[2,64,16,512]{3,2,1,0:T(8,128)}, u32[]{:S(2)}) copy-start(s32[2,64,16,512]{3,2,1,0:T(8,128)} %voltages.3) | copy-start | bytes 12582916
  8.1 0.7 copy-start.2
  8.8 0.9 copy-start.3
  16.0 0.7 copy-start.1
  16.8 23.2 %collective-permute-start.1 = (bf16[4,2,64,512]{3,2,1,0:T(8,128)(2,1)S(1)}, bf16[4,2,64,512]{3,2,1,0:T(8,128)(2,1)S(1)}, u32[]{:S(2)}, u32[]{:S(2)}) collective-permute-start(bf16[4,2,64,512]{3,2,1,0:T(8,128)(2,1)S(1)} %get-tuple-element.126), channel_id=1, source_target_pairs={{0,4},{1,3},{2,6},{3,1},{4,0},{5,7},{6,2},{7,5},{8,12},{9,11},{10,... | collective-permute-start | bytes 1572872 | tf_op jit(solution)/shard_map/ppermute | solution.py:364
  18.2 21.7 %collective-permute-start.2 = (bf16[4,2,64,512]{3,2,1,0:T(8,128)(2,1)S(1)}, bf16[4,2,64,512]{3,2,1,0:T(8,128)(2,1)S(1)}, u32[]{:S(2)}, u32[]{:S(2)}) collective-permute-start(bf16[4,2,64,512]{3,2,1,0:T(8,128)(2,1)S(1)} %get-tuple-element.126), channel_id=1, source_target_pairs={{0,2},{1,5},{2,0},{3,7},{4,6},{5,1},{6,4},{7,3},{8,10},{9,13},{10,... | collective-permute-start | bytes 1572872 | tf_op jit(solution)/shard_map/ppermute | solution.py:364
  19.7 11.1 %collective-permute-start.3 = (bf16[2,2,64,512]{3,2,1,0:T(8,128)(2,1)S(1)}, bf16[2,2,64,512]{3,2,1,0:T(8,128)(2,1)S(1)}, u32[]{:S(2)}, u32[]{:S(2)}) collective-permute-start(bf16[2,2,64,512]{3,2,1,0:T(8,128)(2,1)S(1)} %get-tuple-element.102), channel_id=1, source_target_pairs={{0,8},{8,16},{16,24},{24,0},{1,9},{9,17},{17,25},{25,1},{2,10},{10... | collective-permute-start | bytes 786440 | tf_op jit(solution)/shard_map/ppermute | solution.py:324
  21.3 18.7 %collective-permute-start.4 = (bf16[2,2,64,512]{3,2,1,0:T(8,128)(2,1)S(1)}, bf16[2,2,64,512]{3,2,1,0:T(8,128)(2,1)S(1)}, u32[]{:S(2)}, u32[]{:S(2)}) collective-permute-start(bf16[2,2,64,512]{3,2,1,0:T(8,128)(2,1)S(1)} %get-tuple-element.103), channel_id=1, source_target_pairs={{0,16},{8,24},{16,0},{24,8},{1,17},{9,25},{17,1},{25,9},{2,18},{10... | collective-permute-start | bytes 786440 | tf_op jit(solution)/shard_map/ppermute | solution.py:324
  40.0 9.2 %collective-permute-start.5 = (bf16[4,2,64,512]{3,2,1,0:T(8,128)(2,1)S(1)}, bf16[4,2,64,512]{3,2,1,0:T(8,128)(2,1)S(1)}, u32[]{:S(2)}, u32[]{:S(2)}) collective-permute-start(bf16[4,2,64,512]{3,2,1,0:T(8,128)(2,1)S(1)} %collective-permute-done.1), channel_id=1, source_target_pairs={{0,2},{1,5},{2,0},{3,7},{4,6},{5,1},{6,4},{7,3},{8,10},{9,13},{10,... | collective-permute-start | bytes 1572872 | tf_op jit(solution)/shard_map/ppermute | solution.py:364
  40.5 7.9 %collective-permute-start.6 = (bf16[2,2,64,512]{3,2,1,0:T(8,128)(2,1)S(1)}, bf16[2,2,64,512]{3,2,1,0:T(8,128)(2,1)S(1)}, u32[]{:S(2)}, u32[]{:S(2)}) collective-permute-start(bf16[2,2,64,512]{3,2,1,0:T(8,128)(2,1)S(1)} %get-tuple-element.112), channel_id=1, source_target_pairs={{0,24},{8,0},{16,8},{24,16},{1,25},{9,1},{17,9},{25,17},{2,26},{10... | collective-permute-start | bytes 786440 | tf_op jit(solution)/shard_map/ppermute | solution.py:324
  49.3 5.3 %collective-permute-start.12 = (bf16[3,2,2,64,512]{4,3,2,1,0:T(8,128)(2,1)S(1)}, bf16[3,2,2,64,512]{4,3,2,1,0:T(8,128)(2,1)}, u32[]{:S(2)}, u32[]{:S(2)}) collective-permute-start(bf16[3,2,2,64,512]{4,3,2,1,0:T(8,128)(2,1)S(1)} %pad_maximum_fusion), channel_id=1, source_target_pairs={{0,1},{1,0},{2,3},{3,2},{4,5},{5,4},{6,7},{7,6},{8,9},{9,8},{10,11... | collective-permute-start | bytes 2359304 | tf_op jit(solution)/shard_map/ppermute | solution.py:327
  49.3 3.0 %collective-permute-start.11 = (bf16[4,2,64,512]{3,2,1,0:T(8,128)(2,1)S(1)}, bf16[4,2,64,512]{3,2,1,0:T(8,128)(2,1)S(1)}, u32[]{:S(2)}, u32[]{:S(2)}) collective-permute-start(bf16[4,2,64,512]{3,2,1,0:T(8,128)(2,1)S(1)} %get-tuple-element.126), channel_id=1, source_target_pairs={{0,1},{1,0},{2,3},{3,2},{4,5},{5,4},{6,7},{7,6},{8,9},{9,8},{10,11... | collective-permute-start | bytes 1572872 | tf_op jit(solution)/shard_map/ppermute | solution.py:327
  49.8 20.9 %collective-permute-start.7 = (bf16[3,2,2,64,512]{4,3,2,1,0:T(8,128)(2,1)S(1)}, bf16[3,2,2,64,512]{4,3,2,1,0:T(8,128)(2,1)}, u32[]{:S(2)}, u32[]{:S(2)}) collective-permute-start(bf16[3,2,2,64,512]{4,3,2,1,0:T(8,128)(2,1)S(1)} %pad_maximum_fusion), channel_id=1, source_target_pairs={{0,4},{1,3},{2,6},{3,1},{4,0},{5,7},{6,2},{7,5},{8,12},{9,11},{10,... | collective-permute-start | bytes 2359304 | tf_op jit(solution)/shard_map/ppermute | solution.py:364
  50.6 20.2 %collective-permute-start.8 = (bf16[3,2,2,64,512]{4,3,2,1,0:T(8,128)(2,1)S(1)}, bf16[3,2,2,64,512]{4,3,2,1,0:T(8,128)(2,1)}, u32[]{:S(2)}, u32[]{:S(2)}) collective-permute-start(bf16[3,2,2,64,512]{4,3,2,1,0:T(8,128)(2,1)S(1)} %pad_maximum_fusion), channel_id=1, source_target_pairs={{0,2},{1,5},{2,0},{3,7},{4,6},{5,1},{6,4},{7,3},{8,10},{9,13},{10,... | collective-permute-start | bytes 2359304 | tf_op jit(solution)/shard_map/ppermute | solution.py:364
  51.2 19.6 %collective-permute-start.10 = (bf16[2,2,64,512]{3,2,1,0:T(8,128)(2,1)}, bf16[2,2,64,512]{3,2,1,0:T(8,128)(2,1)}, u32[]{:S(2)}, u32[]{:S(2)}) collective-permute-start(bf16[2,2,64,512]{3,2,1,0:T(8,128)(2,1)} %get-tuple-element.124), channel_id=1, source_target_pairs={{0,16},{8,24},{16,0},{24,8},{1,17},{9,25},{17,1},{25,9},{2,18},{10... | collective-permute-start | bytes 786440 | tf_op jit(solution)/shard_map/ppermute | solution.py:324
  52.4 18.4 %collective-permute-start.9 = (bf16[2,2,64,512]{3,2,1,0:T(8,128)(2,1)}, bf16[2,2,64,512]{3,2,1,0:T(8,128)(2,1)}, u32[]{:S(2)}, u32[]{:S(2)}) collective-permute-start(bf16[2,2,64,512]{3,2,1,0:T(8,128)(2,1)} %get-tuple-element.123), channel_id=1, source_target_pairs={{0,8},{8,16},{16,24},{24,0},{1,9},{9,17},{17,25},{25,1},{2,10},{10... | collective-permute-start | bytes 786440 | tf_op jit(solution)/shard_map/ppermute | solution.py:324
  70.8 5.0 %collective-permute-start.16 = (bf16[3,2,2,64,512]{4,3,2,1,0:T(8,128)(2,1)}, bf16[3,2,2,64,512]{4,3,2,1,0:T(8,128)(2,1)S(1)}, u32[]{:S(2)}, u32[]{:S(2)}) collective-permute-start(bf16[3,2,2,64,512]{4,3,2,1,0:T(8,128)(2,1)} %collective-permute-done.7), channel_id=1, source_target_pairs={{0,1},{1,0},{2,3},{3,2},{4,5},{5,4},{6,7},{7,6},{8,9},{9,8},{10,11... | collective-permute-start | bytes 2359304 | tf_op jit(solution)/shard_map/ppermute | solution.py:327
  70.9 4.9 %collective-permute-start.18 = (bf16[3,2,2,64,512]{4,3,2,1,0:T(8,128)(2,1)}, bf16[3,2,2,64,512]{4,3,2,1,0:T(8,128)(2,1)S(1)}, u32[]{:S(2)}, u32[]{:S(2)}) collective-permute-start(bf16[3,2,2,64,512]{4,3,2,1,0:T(8,128)(2,1)} %collective-permute-done.8), channel_id=1, source_target_pairs={{0,1},{1,0},{2,3},{3,2},{4,5},{5,4},{6,7},{7,6},{8,9},{9,8},{10,11... | collective-permute-start | bytes 2359304 | tf_op jit(solution)/shard_map/ppermute | solution.py:327
  71.4 3.3 %collective-permute-start.15 = (bf16[4,2,64,512]{3,2,1,0:T(8,128)(2,1)S(1)}, bf16[4,2,64,512]{3,2,1,0:T(8,128)(2,1)S(1)}, u32[]{:S(2)}, u32[]{:S(2)}) collective-permute-start(bf16[4,2,64,512]{3,2,1,0:T(8,128)(2,1)S(1)} %collective-permute-done.1), channel_id=1, source_target_pairs={{0,1},{1,0},{2,3},{3,2},{4,5},{5,4},{6,7},{7,6},{8,9},{9,8},{10,11... | collective-permute-start | bytes 1572872 | tf_op jit(solution)/shard_map/ppermute | solution.py:327
  71.5 13.8 %collective-permute-start.13 = (bf16[3,2,2,64,512]{4,3,2,1,0:T(8,128)(2,1)}, bf16[3,2,2,64,512]{4,3,2,1,0:T(8,128)(2,1)S(1)}, u32[]{:S(2)}, u32[]{:S(2)}) collective-permute-start(bf16[3,2,2,64,512]{4,3,2,1,0:T(8,128)(2,1)} %collective-permute-done.7), channel_id=1, source_target_pairs={{0,2},{1,5},{2,0},{3,7},{4,6},{5,1},{6,4},{7,3},{8,10},{9,13},{10,... | collective-permute-start | bytes 2359304 | tf_op jit(solution)/shard_map/ppermute | solution.py:364
  73.0 2.8 %collective-permute-start.17 = (bf16[4,2,64,512]{3,2,1,0:T(8,128)(2,1)S(1)}, bf16[4,2,64,512]{3,2,1,0:T(8,128)(2,1)S(1)}, u32[]{:S(2)}, u32[]{:S(2)}) collective-permute-start(bf16[4,2,64,512]{3,2,1,0:T(8,128)(2,1)S(1)} %collective-permute-done.2), channel_id=1, source_target_pairs={{0,1},{1,0},{2,3},{3,2},{4,5},{5,4},{6,7},{7,6},{8,9},{9,8},{10,11... | collective-permute-start | bytes 1572872 | tf_op jit(solution)/shard_map/ppermute | solution.py:327
  74.6 10.6 %collective-permute-start.14 = (bf16[2,2,64,512]{3,2,1,0:T(8,128)(2,1)}, bf16[2,2,64,512]{3,2,1,0:T(8,128)(2,1)S(1)}, u32[]{:S(2)}, u32[]{:S(2)}) collective-permute-start(bf16[2,2,64,512]{3,2,1,0:T(8,128)(2,1)} %copy-done.1), channel_id=1, source_target_pairs={{0,24},{8,0},{16,8},{24,16},{1,25},{9,1},{17,9},{25,17},{2,26},{10... | collective-permute-start | bytes 786440 | tf_op jit(solution)/shard_map/ppermute | solution.py:324
  86.4 4.8 %collective-permute-start.22 = (bf16[3,2,2,64,512]{4,3,2,1,0:T(8,128)(2,1)S(1)}, bf16[3,2,2,64,512]{4,3,2,1,0:T(8,128)(2,1)S(1)}, u32[]{:S(2)}, u32[]{:S(2)}) collective-permute-start(bf16[3,2,2,64,512]{4,3,2,1,0:T(8,128)(2,1)S(1)} %collective-permute-done.13), channel_id=1, source_target_pairs={{0,1},{1,0},{2,3},{3,2},{4,5},{5,4},{6,7},{7,6},{8,9},{9,8},{10,11... | collective-permute-start | bytes 2359304 | tf_op jit(solution)/shard_map/ppermute | solution.py:327
  86.6 4.6 %collective-permute-start.23 = (bf16[3,2,2,64,512]{4,3,2,1,0:T(8,128)(2,1)S(1)}, bf16[3,2,2,64,512]{4,3,2,1,0:T(8,128)(2,1)S(1)}, u32[]{:S(2)}, u32[]{:S(2)}) collective-permute-start(bf16[3,2,2,64,512]{4,3,2,1,0:T(8,128)(2,1)S(1)} %pad_maximum_fusion.1), channel_id=1, source_target_pairs={{0,1},{1,0},{2,3},{3,2},{4,5},{5,4},{6,7},{7,6},{8,9},{9,8},{10,11... | collective-permute-start | bytes 2359304 | tf_op jit(solution)/shard_map/ppermute | solution.py:327
  87.0 20.1 %collective-permute-start.19 = (bf16[3,2,2,64,512]{4,3,2,1,0:T(8,128)(2,1)S(1)}, bf16[3,2,2,64,512]{4,3,2,1,0:T(8,128)(2,1)S(1)}, u32[]{:S(2)}, u32[]{:S(2)}) collective-permute-start(bf16[3,2,2,64,512]{4,3,2,1,0:T(8,128)(2,1)S(1)} %pad_maximum_fusion.1), channel_id=1, source_target_pairs={{0,4},{1,3},{2,6},{3,1},{4,0},{5,7},{6,2},{7,5},{8,12},{9,11},{10,... | collective-permute-start | bytes 2359304 | tf_op jit(solution)/shard_map/ppermute | solution.py:364
  88.3 18.8 %collective-permute-start.20 = (bf16[3,2,2,64,512]{4,3,2,1,0:T(8,128)(2,1)S(1)}, bf16[3,2,2,64,512]{4,3,2,1,0:T(8,128)(2,1)S(1)}, u32[]{:S(2)}, u32[]{:S(2)}) collective-permute-start(bf16[3,2,2,64,512]{4,3,2,1,0:T(8,128)(2,1)S(1)} %pad_maximum_fusion.1), channel_id=1, source_target_pairs={{0,2},{1,5},{2,0},{3,7},{4,6},{5,1},{6,4},{7,3},{8,10},{9,13},{10,... | collective-permute-start | bytes 2359304 | tf_op jit(solution)/shard_map/ppermute | solution.py:364
  89.3 1.9 %collective-permute-start.21 = (bf16[4,2,64,512]{3,2,1,0:T(8,128)(2,1)S(1)}, bf16[4,2,64,512]{3,2,1,0:T(8,128)(2,1)S(1)}, u32[]{:S(2)}, u32[]{:S(2)}) collective-permute-start(bf16[4,2,64,512]{3,2,1,0:T(8,128)(2,1)S(1)} %collective-permute-done.5), channel_id=1, source_target_pairs={{0,1},{1,0},{2,3},{3,2},{4,5},{5,4},{6,7},{7,6},{8,9},{9,8},{10,11... | collective-permute-start | bytes 1572872 | tf_op jit(solution)/shard_map/ppermute | solution.py:327
  107.1 2.3 %collective-permute-start.25 = (bf16[3,2,2,64,512]{4,3,2,1,0:T(8,128)(2,1)S(1)}, bf16[3,2,2,64,512]{4,3,2,1,0:T(8,128)(2,1)S(1)}, u32[]{:S(2)}, u32[]{:S(2)}) collective-permute-start(bf16[3,2,2,64,512]{4,3,2,1,0:T(8,128)(2,1)S(1)} %collective-permute-done.19), channel_id=1, source_target_pairs={{0,1},{1,0},{2,3},{3,2},{4,5},{5,4},{6,7},{7,6},{8,9},{9,8},{10,11... | collective-permute-start | bytes 2359304 | tf_op jit(solution)/shard_map/ppermute | solution.py:327
  107.2 3.3 %collective-permute-start.26 = (bf16[3,2,2,64,512]{4,3,2,1,0:T(8,128)(2,1)S(1)}, bf16[3,2,2,64,512]{4,3,2,1,0:T(8,128)(2,1)S(1)}, u32[]{:S(2)}, u32[]{:S(2)}) collective-permute-start(bf16[3,2,2,64,512]{4,3,2,1,0:T(8,128)(2,1)S(1)} %collective-permute-done.20), channel_id=1, source_target_pairs={{0,1},{1,0},{2,3},{3,2},{4,5},{5,4},{6,7},{7,6},{8,9},{9,8},{10,11... | collective-permute-start | bytes 2359304 | tf_op jit(solution)/shard_map/ppermute | solution.py:327
  107.6 12.6 %collective-permute-start.24 = (bf16[3,2,2,64,512]{4,3,2,1,0:T(8,128)(2,1)S(1)}, bf16[3,2,2,64,512]{4,3,2,1,0:T(8,128)(2,1)S(1)}, u32[]{:S(2)}, u32[]{:S(2)}) collective-permute-start(bf16[3,2,2,64,512]{4,3,2,1,0:T(8,128)(2,1)S(1)} %collective-permute-done.19), channel_id=1, source_target_pairs={{0,2},{1,5},{2,0},{3,7},{4,6},{5,1},{6,4},{7,3},{8,10},{9,13},{10,... | collective-permute-start | bytes 2359304 | tf_op jit(solution)/shard_map/ppermute | solution.py:364
  120.2 2.4 %collective-permute-start.27 = (bf16[3,2,2,64,512]{4,3,2,1,0:T(8,128)(2,1)S(1)}, bf16[3,2,2,64,512]{4,3,2,1,0:T(8,128)(2,1)S(1)}, u32[]{:S(2)}, u32[]{:S(2)}) collective-permute-start(bf16[3,2,2,64,512]{4,3,2,1,0:T(8,128)(2,1)S(1)} %collective-permute-done.24), channel_id=1, source_target_pairs={{0,1},{1,0},{2,3},{3,2},{4,5},{5,4},{6,7},{7,6},{8,9},{9,8},{10,11... | collective-permute-start | bytes 2359304 | tf_op jit(solution)/shard_map/ppermute | solution.py:327

commit v4 on v3

--- a/solution.py
+++ b/solution.py
@@ -21,15 +21,6 @@
 
 def struct(shape, dtype=jnp.bfloat16):
     return jax.ShapeDtypeStruct(shape, dtype)
-
-
-def transform_rows(chans, span):
-    index = np.arange(chans)
-    angle = (index[:, None] * index[None, :] % chans) * (2.0 * math.pi / chans)
-    cosine, sine = np.cos(angle), np.sin(angle)
-    rows = np.stack([np.stack([cosine, sine], 1), np.stack([-sine, cosine], 1)], 1) * VOLT_SCALE
-    rows = np.broadcast_to(rows[:, :, :, None], (chans, 2, 2, span, chans))
-    return np.tile(rows.reshape(chans, 2, -1), (2, 1, 1)).astype(np.float32)
 
 
 def channelize_group(volts, held, weights, outs, layout):
@@ -49,7 +40,7 @@
         out[...] = result[d, channels[0] : channels[-1] + 1]
 
 
-def channelize_inner(layout, tap_count, voltages, table, taps, *rest):
+def channelize_inner(layout, tap_count, voltages, taps, *rest):
     outs, (weights, held, volts, last, sems) = rest[:-5], rest[-5:]
     slots, _, group, chans, width = volts.shape
     ahead = (tap_count - 1) * chans
@@ -75,9 +66,16 @@
         band = jnp.zeros((group, 2 * span), jnp.float32)
         for k in range(tap_count):
             band = band + jnp.where(column == row + (tap_count - 1 - k), spread_taps[k : k + 1, :], 0.0)
+        row = lax.broadcasted_iota(jnp.int32, (2 * chans, 2 * span), 0)
+        column = lax.broadcasted_iota(jnp.int32, (2 * chans, 2 * span), 1)
+        quarters = (row % 2) - (column >= span).astype(jnp.int32)
+        turn = ((first + row // 2) * (column % chans) + quarters * (chans // 4) + chans) % chans
+        basis = jnp.zeros((2 * chans, 2 * span), jnp.float32)
+        for m in range(chans):
+            basis = jnp.where(turn == m, math.cos(2.0 * math.pi * m / chans) * VOLT_SCALE, basis)
         for c in range(chans):
             for p in range(2):
-                exact = table[first + c, p : p + 1, :] * band
+                exact = basis[2 * c + p : 2 * c + p + 1, :] * band
                 high = exact.astype(jnp.bfloat16)
                 at = (2 * c + p) * group
                 weights[0, at : at + group, :] = high
@@ -108,7 +106,7 @@
     channelize_group(volts, held, weights, outs, layout)
 
 
-def channelize(voltages, rim, table, taps, layout):
+def channelize(voltages, rim, taps, layout):
     _, frames, chans, width = voltages.shape
     tap_count = taps.shape[0]
     span = (GROUP + tap_count - 1) * chans
@@ -125,7 +123,6 @@
         grid=(groups - 1,),
         in_specs=[
             HBM,
-            pl.BlockSpec(table.shape, lambda g: (0, 0, 0)),
             pl.BlockSpec(taps.shape, lambda g: (0, 0)),
         ],
         out_specs=[pl.BlockSpec(b, lambda g: (0, 0, g + 1, 0)) for b in blocks]
@@ -142,7 +139,7 @@
             flops=cost * (groups - 1), bytes_accessed=6 * voltages.size, transcendentals=0
         ),
         name="channelize_inner",
-    )(voltages, table, taps)
+    )(voltages, taps)
     return pl.pallas_call(
         functools.partial(channelize_first, layout),
         grid=(1,),
@@ -311,14 +308,13 @@
 
     rim = voltages[:, frames - (tap_count - 1) :].astype(jnp.bfloat16)
     rim = lax.ppermute(rim, "chan", [(i, i + 1) for i in range(devices - 1)])
-    table = transform_rows(chans, GROUP + tap_count - 1)
     sources = np.array([[i ^ m for m in source_masks(count, i % 2)] for i in range(count)], np.int32)
     sources = np.stack([sources, sources[np.arange(count) ^ 1]], 2)
     sources = lax.dynamic_index_in_dim(jnp.asarray(sources), place, 0, keepdims=False)
 
     halves = [range(mine)] if mine < 2 else [range(mine // 2), range(mine // 2, mine)]
     layout = [(0, range(mine))] + [(d, half) for half in halves for d in range(1, devices)]
-    firsts = channelize(voltages, rim, jnp.asarray(table), fir_taps, layout)
+    firsts = channelize(voltages, rim, fir_taps, layout)
 
     def turned(piece, d):
         return lax.ppermute(piece, "chan", [(i, (i + d) % devices) for i in range(devices)])

time: 129 us -> 128 us (level)
    unnamed x8 -> x6, local copies, waits for them, and re-layouts: 4.5 us -> 3.57 us
  transfers between devices with their start and end apart: 28 -> 28, of which waited for: 13 -> 13; matrix products, arithmetic and copies ran while one was open for 1% -> 1% of each run, Pallas kernels for 32% -> 33%
where the time goes in v4:
time: 128 us
  Pallas kernels  48.8 us (38%)
  waiting for transfers between devices  47.7 us (37%)
  starting transfers between devices  24.1 us (19%)
  local copies, waits for them, and re-layouts  4.34 us (3%)
  other arithmetic  2.15 us (2%)
    pallas_call x5, Pallas kernels, correlate(): pl.pallas_call(functools.partial(correlate_step, shape), in_specs=[pl.Blo...  42.5 us
    ppermute x6, waiting for transfers between devices, turned(): lax.ppermute(piece, 'chan', [(i, (i + d) % devices) for i in range(device...  33.3 us
    ppermute x9, starting transfers between devices, one_round(): lax.ppermute(block, 'inp', [(i, i ^ orders[i % 2][step]) for i in range(c...  9.91 us
    ppermute x12, waiting for transfers between devices, swapped(): return lax.ppermute(block, 'inp', [(i, i ^ 1) for i in range(count)])  8.74 us
    ppermute x6, starting transfers between devices, turned(): lax.ppermute(piece, 'chan', [(i, (i + d) % devices) for i in range(device...  6.77 us
    ppermute x9, waiting for transfers between devices, one_round(): lax.ppermute(block, 'inp', [(i, i ^ orders[i % 2][step]) for i in range(c...  5.73 us
    ppermute x1, starting transfers between devices, body(): rim = lax.ppermute(rim, 'chan', [(i, i + 1) for i in range(devices - 1)])  4.93 us
    pallas_call x1, Pallas kernels, channelize(): pl.pallas_call(functools.partial(channelize_inner, layout, tap_count), gr...  4.61 us
  transfers between devices with their start and end apart: 28, of which 13 were waited for; matrix products, arithmetic and copies ran while one was open for 1% of the time, Pallas kernels for 33%

profile of v4, /device:TPU:0, one launch (start us, length us, event | category | flops | bytes accessed | tf_op | source)
XLA Modules:
  0.0 127.5 jit_solution(4409344015134637409)
XLA Ops:
  0.0 0.9 slice_convert_fusion
  0.9 4.9 %collective-permute-start = (bf16[2,3,16,512]{3,2,1,0:T(8,128)(2,1)S(1)}, bf16[2,3,16,512]{3,2,1,0:T(8,128)(2,1)S(1)}, u32[]{:S(2)}, u32[]{:S(2)}) collective-permute-start(bf16[2,3,16,512]{3,2,1,0:T(8,128)(2,1)S(1)} %slice_convert_fusion), channel_id=1, source_target_pairs={{0,8},{8,16},{16,24},{1,9},{9,17},{17,25},{2,10},{10,18},{18,26},{... | collective-permute-start | bytes 294920 | tf_op jit(solution)/shard_map/ppermute | solution.py:310
  5.9 2.2 %copy-done = s32[2,64,16,512]{3,2,1,0:T(8,128)S(1)} copy-done((s32[2,64,16,512]{3,2,1,0:T(8,128)S(1)}, s32[2,64,16,512]{3,2,1,0:T(8,128)}, u32[]{:S(2)}) %copy-start) | copy-done | bytes 4194328
  8.1 0.7 copy-done.2
  8.8 4.6 %channelize_inner.1 = (bf16[4,2,64,512]{3,2,1,0:T(8,128)(2,1)S(1)}, bf16[2,2,64,512]{3,2,1,0:T(8,128)(2,1)S(1)}, bf16[2,2,64,512]{3,2,1,0:T(8,128)(2,1)S(1)}, bf...) custom-call(s32[2,64,16,512]{3,2,1,0:T(8,128)S(1)} %copy-done, ...), custom_call_target="tpu_custom_call" | custom-call | flops 1912602624 | bytes 6291456 | tf_op jit(solution)/shard_map/channelize_inner/pallas_call | solution.py:121
  13.4 1.7 %channelize_first.1 = (bf16[4,2,64,512]{3,2,1,0:T(8,128)(2,1)S(1)}, bf16[2,2,64,512]{3,2,1,0:T(8,128)(2,1)S(1)}, bf16[2,2,64,512]{3,2,1,0:T(8,128)(2,1)S(1)}, bf...) custom-call(s32[2,64,16,512]{3,2,1,0:T(8,128)S(1)} %copy-done, ...), custom_call_target="tpu_custom_call", output_to_operand_aliasing={{0}: (3, {}), {1}: (4, {}), {2}: (5, {}), {3}: (6, {}), {4}... | custom-call | flops 637534208 | bytes 1572864 | tf_op jit(solution)/shard_map/channelize_first/pallas_call | solution.py:143
  15.1 0.7 copy-done.1
  15.8 1.5 %collective-permute-start.1 = (bf16[4,2,64,512]{3,2,1,0:T(8,128)(2,1)S(1)}, bf16[4,2,64,512]{3,2,1,0:T(8,128)(2,1)S(1)}, u32[]{:S(2)}, u32[]{:S(2)}) collective-permute-start(bf16[4,2,64,512]{3,2,1,0:T(8,128)(2,1)S(1)} %get-tuple-element.126), channel_id=1, source_target_pairs={{0,4},{1,3},{2,6},{3,1},{4,0},{5,7},{6,2},{7,5},{8,12},{9,11},{10,... | collective-permute-start | bytes 1572872 | tf_op jit(solution)/shard_map/ppermute | solution.py:360
  17.4 1.5 %collective-permute-start.2 = (bf16[4,2,64,512]{3,2,1,0:T(8,128)(2,1)S(1)}, bf16[4,2,64,512]{3,2,1,0:T(8,128)(2,1)S(1)}, u32[]{:S(2)}, u32[]{:S(2)}) collective-permute-start(bf16[4,2,64,512]{3,2,1,0:T(8,128)(2,1)S(1)} %get-tuple-element.126), channel_id=1, source_target_pairs={{0,2},{1,5},{2,0},{3,7},{4,6},{5,1},{6,4},{7,3},{8,10},{9,13},{10,... | collective-permute-start | bytes 1572872 | tf_op jit(solution)/shard_map/ppermute | solution.py:360
  18.9 1.6 %collective-permute-start.3 = (bf16[2,2,64,512]{3,2,1,0:T(8,128)(2,1)S(1)}, bf16[2,2,64,512]{3,2,1,0:T(8,128)(2,1)S(1)}, u32[]{:S(2)}, u32[]{:S(2)}) collective-permute-start(bf16[2,2,64,512]{3,2,1,0:T(8,128)(2,1)S(1)} %get-tuple-element.102), channel_id=1, source_target_pairs={{0,8},{8,16},{16,24},{24,0},{1,9},{9,17},{17,25},{25,1},{2,10},{10... | collective-permute-start | bytes 786440 | tf_op jit(solution)/shard_map/ppermute | solution.py:320
  20.4 1.0 collective-permute-start.4
  21.4 8.5 %collective-permute-done.3 = bf16[2,2,64,512]{3,2,1,0:T(8,128)(2,1)S(1)} collective-permute-done((bf16[2,2,64,512]{3,2,1,0:T(8,128)(2,1)S(1)}, bf16[2,2,64,512]{3,2,1,0:T(8,128)(2,1)S(1)}, u32[]{:S(2)}, u32[]{:S(2)}) %collective-permute-start.3) | collective-permute-done | bytes 262176 | tf_op jit(solution)/shard_map/ppermute | solution.py:320
  30.0 9.1 %collective-permute-done.4 = bf16[2,2,64,512]{3,2,1,0:T(8,128)(2,1)S(1)} collective-permute-done((bf16[2,2,64,512]{3,2,1,0:T(8,128)(2,1)S(1)}, bf16[2,2,64,512]{3,2,1,0:T(8,128)(2,1)S(1)}, u32[]{:S(2)}, u32[]{:S(2)}) %collective-permute-start.4) | collective-permute-done | bytes 262176 | tf_op jit(solution)/shard_map/ppermute | solution.py:320
  39.1 0.5 collective-permute-start.5
  39.6 1.7 %collective-permute-start.6 = (bf16[2,2,64,512]{3,2,1,0:T(8,128)(2,1)S(1)}, bf16[2,2,64,512]{3,2,1,0:T(8,128)(2,1)S(1)}, u32[]{:S(2)}, u32[]{:S(2)}) collective-permute-start(bf16[2,2,64,512]{3,2,1,0:T(8,128)(2,1)S(1)} %get-tuple-element.112), channel_id=1, source_target_pairs={{0,24},{8,0},{16,8},{24,16},{1,25},{9,1},{17,9},{25,17},{2,26},{10... | collective-permute-start | bytes 786440 | tf_op jit(solution)/shard_map/ppermute | solution.py:320
  41.3 6.2 %collective-permute-done.6 = bf16[2,2,64,512]{3,2,1,0:T(8,128)(2,1)S(1)} collective-permute-done((bf16[2,2,64,512]{3,2,1,0:T(8,128)(2,1)S(1)}, bf16[2,2,64,512]{3,2,1,0:T(8,128)(2,1)S(1)}, u32[]{:S(2)}, u32[]{:S(2)}) %collective-permute-start.6) | collective-permute-done | bytes 262176 | tf_op jit(solution)/shard_map/ppermute | solution.py:320
  47.6 0.7 collective-permute-done.5
  48.5 0.5 collective-permute-start.11
  49.0 0.8 collective-permute-start.7
  49.8 0.5 collective-permute-start.8
  50.3 1.2 collective-permute-done.11
  51.5 1.5 %collective-permute-start.9 = (bf16[2,2,64,512]{3,2,1,0:T(8,128)(2,1)}, bf16[2,2,64,512]{3,2,1,0:T(8,128)(2,1)}, u32[]{:S(2)}, u32[]{:S(2)}) collective-permute-start(bf16[2,2,64,512]{3,2,1,0:T(8,128)(2,1)} %get-tuple-element.123), channel_id=1, source_target_pairs={{0,8},{8,16},{16,24},{24,0},{1,9},{9,17},{17,25},{25,1},{2,10},{10... | collective-permute-start | bytes 786440 | tf_op jit(solution)/shard_map/ppermute | solution.py:320
  52.9 0.7 dynamic-slice_bitcast_fusion
  53.6 0.1 copy.24.where
  53.7 6.8 %correlate.5 = (f32[4,2,512,4096]{3,2,1,0:T(8,128)}, f32[8,128]{1,0:T(8,128)S(1)}, bf16[2,1024,512]{2,1,0:T(8,128)(2,1)S(1)}) custom-call(s32[4,2]{1,0:T(4,128)S(1)} %copy.24.where, f32[8,128]{1,0:T(8,128)S(1)} %broadcast_in_dim.3.token, bf16[1,4,128,512]{3,2,1,0:T(8,128)(2,1)S(1)} %bitcast.32, ...), custom_call_target="tpu_custom_call", output_to_operand_aliasing={{1}: (1, {})} | custom-call | tf_op jit(solution)/shard_map/correlate/pallas_call | solution.py:261
  60.5 9.4 %collective-permute-done.10 = bf16[2,2,64,512]{3,2,1,0:T(8,128)(2,1)} collective-permute-done((bf16[2,2,64,512]{3,2,1,0:T(8,128)(2,1)}, bf16[2,2,64,512]{3,2,1,0:T(8,128)(2,1)}, u32[]{:S(2)}, u32[]{:S(2)}) %collective-permute-start.10) | collective-permute-done | bytes 262176 | tf_op jit(solution)/shard_map/ppermute | solution.py:320
  70.0 0.5 collective-permute-start.18
  70.6 1.5 %collective-permute-start.13 = (bf16[3,2,2,64,512]{4,3,2,1,0:T(8,128)(2,1)}, bf16[3,2,2,64,512]{4,3,2,1,0:T(8,128)(2,1)S(1)}, u32[]{:S(2)}, u32[]{:S(2)}) collective-permute-start(bf16[3,2,2,64,512]{4,3,2,1,0:T(8,128)(2,1)} %collective-permute-done.7), channel_id=1, source_target_pairs={{0,2},{1,5},{2,0},{3,7},{4,6},{5,1},{6,4},{7,3},{8,10},{9,13},{10,... | collective-permute-start | bytes 2359304 | tf_op jit(solution)/shard_map/ppermute | solution.py:360
  72.1 1.7 %collective-permute-done.15 = bf16[4,2,64,512]{3,2,1,0:T(8,128)(2,1)S(1)} collective-permute-done((bf16[4,2,64,512]{3,2,1,0:T(8,128)(2,1)S(1)}, bf16[4,2,64,512]{3,2,1,0:T(8,128)(2,1)S(1)}, u32[]{:S(2)}, u32[]{:S(2)}) %collective-permute-start.15) | collective-permute-done | bytes 524320 | tf_op jit(solution)/shard_map/ppermute | solution.py:323
  73.8 1.0 collective-permute-start.14
  74.9 9.5 %correlate.6 = (f32[4,2,512,4096]{3,2,1,0:T(8,128)}, f32[8,128]{1,0:T(8,128)S(1)}) custom-call(s32[4,2]{1,0:T(4,128)S(1)} %copy.24.where, f32[8,128]{1,0:T(8,128)S(1)} %get-tuple-element.137.token, bf16[1,4,128,512]{3,2,1,0:T(8,128)(2,1)S(1)} %bitcast.36, bf16[3,2,128,512]{3,2,1,0:T(8,128)(2,1)} %bitcast.11.refs_1_, ...), custom_call_target="tpu_custom_call", output_to_operand_aliasing={{1}: (1, {}), {0}: (11, {})} | custom-call | tf_op jit(solution)/shard_map/correlate/pallas_call | solution.py:261
  84.4 1.1 pad_maximum_fusion.1
  85.5 0.2 collective-permute-start.22
  85.7 0.4 collective-permute-start.23
  86.1 1.3 %collective-permute-start.19 = (bf16[3,2,2,64,512]{4,3,2,1,0:T(8,128)(2,1)S(1)}, bf16[3,2,2,64,512]{4,3,2,1,0:T(8,128)(2,1)S(1)}, u32[]{:S(2)}, u32[]{:S(2)}) collective-permute-start(bf16[3,2,2,64,512]{4,3,2,1,0:T(8,128)(2,1)S(1)} %pad_maximum_fusion.1), channel_id=1, source_target_pairs={{0,4},{1,3},{2,6},{3,1},{4,0},{5,7},{6,2},{7,5},{8,12},{9,11},{10,... | collective-permute-start | bytes 2359304 | tf_op jit(solution)/shard_map/ppermute | solution.py:360
  87.4 1.0 collective-permute-start.20
  88.4 1.9 %collective-permute-done.21 = bf16[4,2,64,512]{3,2,1,0:T(8,128)(2,1)S(1)} collective-permute-done((bf16[4,2,64,512]{3,2,1,0:T(8,128)(2,1)S(1)}, bf16[4,2,64,512]{3,2,1,0:T(8,128)(2,1)S(1)}, u32[]{:S(2)}, u32[]{:S(2)}) %collective-permute-start.21) | collective-permute-done | bytes 524320 | tf_op jit(solution)/shard_map/ppermute | solution.py:323
  90.4 10.9 %correlate.7 = (f32[4,2,512,4096]{3,2,1,0:T(8,128)}, f32[8,128]{1,0:T(8,128)S(1)}, bf16[2,1024,512]{2,1,0:T(8,128)(2,1)S(1)}) custom-call(s32[4,2]{1,0:T(4,128)S(1)} %copy.24.where, f32[8,128]{1,0:T(8,128)S(1)} %get-tuple-element.152.token, bf16[1,4,128,512]{3,2,1,0:T(8,128)(2,1)S(1)} %bitcast.40, ...), custom_call_target="tpu_custom_call", output_to_operand_aliasing={{1}: (1, {}), {0}: (11, {})} | custom-call | tf_op jit(solution)/shard_map/correlate/pallas_call | solution.py:261
  101.2 5.0 %collective-permute-done.19 = bf16[3,2,2,64,512]{4,3,2,1,0:T(8,128)(2,1)S(1)} collective-permute-done((bf16[3,2,2,64,512]{4,3,2,1,0:T(8,128)(2,1)S(1)}, bf16[3,2,2,64,512]{4,3,2,1,0:T(8,128)(2,1)S(1)}, u32[]{:S(2)}, u32[]{:S(2)}) %collective-permute-start.19) | collective-permute-done | bytes 786464 | tf_op jit(solution)/shard_map/ppermute | solution.py:360
  106.2 0.1 collective-permute-start.25
  106.3 0.4 collective-permute-start.26
  106.7 1.2 collective-permute-start.24
  108.0 0.6 collective-permute-done.25
  108.5 1.1 collective-permute-done.26
  109.6 9.7 %correlate.8 = (f32[4,2,512,4096]{3,2,1,0:T(8,128)}, f32[8,128]{1,0:T(8,128)S(1)}) custom-call(s32[4,2]{1,0:T(4,128)S(1)} %copy.24.where, f32[8,128]{1,0:T(8,128)S(1)} %get-tuple-element.162.token, bf16[1,4,128,512]{3,2,1,0:T(8,128)(2,1)S(1)} %bitcast.37, bf16[3,2,128,512]{3,2,1,0:T(8,128)(2,1)S(1)} %bitcast.51, ...), custom_call_target="tpu_custom_call", output_to_operand_aliasing={{1}: (1, {}), {0}: (11, {})} | custom-call | tf_op jit(solution)/shard_map/correlate/pallas_call | solution.py:261
  119.3 0.2 collective-permute-start.27
  119.5 2.1 %collective-permute-done.27 = bf16[3,2,2,64,512]{4,3,2,1,0:T(8,128)(2,1)S(1)} collective-permute-done((bf16[3,2,2,64,512]{4,3,2,1,0:T(8,128)(2,1)S(1)}, bf16[3,2,2,64,512]{4,3,2,1,0:T(8,128)(2,1)S(1)}, u32[]{:S(2)}, u32[]{:S(2)}) %collective-permute-start.27) | collective-permute-done | bytes 786464 | tf_op jit(solution)/shard_map/ppermute | solution.py:323
  121.7 5.7 %correlate.9 = (f32[4,2,512,4096]{3,2,1,0:T(8,128)}, f32[8,128]{1,0:T(8,128)S(1)}) custom-call(s32[4,2]{1,0:T(4,128)S(1)} %copy.24.where, f32[8,128]{1,0:T(8,128)S(1)} %get-tuple-element.168.token, bf16[1,4,128,512]{3,2,1,0:T(8,128)(2,1)S(1)} %bitcast.41, bf16[3,2,128,512]{3,2,1,0:T(8,128)(2,1)S(1)} %bitcast.54, ...), custom_call_target="tpu_custom_call", output_to_operand_aliasing={{1}: (1, {}), {0}: (7, {})} | custom-call | tf_op jit(solution)/shard_map/correlate/pallas_call | solution.py:261
  (27 shorter events, 0.5 us)
Async XLA Ops:
  0.9 12.4 %collective-permute-start = (bf16[2,3,16,512]{3,2,1,0:T(8,128)(2,1)S(1)}, bf16[2,3,16,512]{3,2,1,0:T(8,128)(2,1)S(1)}, u32[]{:S(2)}, u32[]{:S(2)}) collective-permute-start(bf16[2,3,16,512]{3,2,1,0:T(8,128)(2,1)S(1)} %slice_convert_fusion), channel_id=1, source_target_pairs={{0,8},{8,16},{16,24},{1,9},{9,17},{17,25},{2,10},{10,18},{18,26},{... | collective-permute-start | bytes 294920 | tf_op jit(solution)/shard_map/ppermute | solution.py:310
  5.9 2.2 %copy-start = (s32[2,64,16,512]{3,2,1,0:T(8,128)S(1)}, s32[2,64,16,512]{3,2,1,0:T(8,128)}, u32[]{:S(2)}) copy-start(s32[2,64,16,512]{3,2,1,0:T(8,128)} %voltages.3) | copy-start | bytes 12582916
  8.1 0.7 copy-start.2
  15.1 0.7 copy-start.1
  15.8 23.3 %collective-permute-start.1 = (bf16[4,2,64,512]{3,2,1,0:T(8,128)(2,1)S(1)}, bf16[4,2,64,512]{3,2,1,0:T(8,128)(2,1)S(1)}, u32[]{:S(2)}, u32[]{:S(2)}) collective-permute-start(bf16[4,2,64,512]{3,2,1,0:T(8,128)(2,1)S(1)} %get-tuple-element.126), channel_id=1, source_target_pairs={{0,4},{1,3},{2,6},{3,1},{4,0},{5,7},{6,2},{7,5},{8,12},{9,11},{10,... | collective-permute-start | bytes 1572872 | tf_op jit(solution)/shard_map/ppermute | solution.py:360
  17.4 21.7 %collective-permute-start.2 = (bf16[4,2,64,512]{3,2,1,0:T(8,128)(2,1)S(1)}, bf16[4,2,64,512]{3,2,1,0:T(8,128)(2,1)S(1)}, u32[]{:S(2)}, u32[]{:S(2)}) collective-permute-start(bf16[4,2,64,512]{3,2,1,0:T(8,128)(2,1)S(1)} %get-tuple-element.126), channel_id=1, source_target_pairs={{0,2},{1,5},{2,0},{3,7},{4,6},{5,1},{6,4},{7,3},{8,10},{9,13},{10,... | collective-permute-start | bytes 1572872 | tf_op jit(solution)/shard_map/ppermute | solution.py:360
  18.9 11.1 %collective-permute-start.3 = (bf16[2,2,64,512]{3,2,1,0:T(8,128)(2,1)S(1)}, bf16[2,2,64,512]{3,2,1,0:T(8,128)(2,1)S(1)}, u32[]{:S(2)}, u32[]{:S(2)}) collective-permute-start(bf16[2,2,64,512]{3,2,1,0:T(8,128)(2,1)S(1)} %get-tuple-element.102), channel_id=1, source_target_pairs={{0,8},{8,16},{16,24},{24,0},{1,9},{9,17},{17,25},{25,1},{2,10},{10... | collective-permute-start | bytes 786440 | tf_op jit(solution)/shard_map/ppermute | solution.py:320
  20.4 18.7 %collective-permute-start.4 = (bf16[2,2,64,512]{3,2,1,0:T(8,128)(2,1)S(1)}, bf16[2,2,64,512]{3,2,1,0:T(8,128)(2,1)S(1)}, u32[]{:S(2)}, u32[]{:S(2)}) collective-permute-start(bf16[2,2,64,512]{3,2,1,0:T(8,128)(2,1)S(1)} %get-tuple-element.103), channel_id=1, source_target_pairs={{0,16},{8,24},{16,0},{24,8},{1,17},{9,25},{17,1},{25,9},{2,18},{10... | collective-permute-start | bytes 786440 | tf_op jit(solution)/shard_map/ppermute | solution.py:320
  39.1 9.2 %collective-permute-start.5 = (bf16[4,2,64,512]{3,2,1,0:T(8,128)(2,1)S(1)}, bf16[4,2,64,512]{3,2,1,0:T(8,128)(2,1)S(1)}, u32[]{:S(2)}, u32[]{:S(2)}) collective-permute-start(bf16[4,2,64,512]{3,2,1,0:T(8,128)(2,1)S(1)} %collective-permute-done.1), channel_id=1, source_target_pairs={{0,2},{1,5},{2,0},{3,7},{4,6},{5,1},{6,4},{7,3},{8,10},{9,13},{10,... | collective-permute-start | bytes 1572872 | tf_op jit(solution)/shard_map/ppermute | solution.py:360
  39.6 7.9 %collective-permute-start.6 = (bf16[2,2,64,512]{3,2,1,0:T(8,128)(2,1)S(1)}, bf16[2,2,64,512]{3,2,1,0:T(8,128)(2,1)S(1)}, u32[]{:S(2)}, u32[]{:S(2)}) collective-permute-start(bf16[2,2,64,512]{3,2,1,0:T(8,128)(2,1)S(1)} %get-tuple-element.112), channel_id=1, source_target_pairs={{0,24},{8,0},{16,8},{24,16},{1,25},{9,1},{17,9},{25,17},{2,26},{10... | collective-permute-start | bytes 786440 | tf_op jit(solution)/shard_map/ppermute | solution.py:320
  48.4 5.3 %collective-permute-start.12 = (bf16[3,2,2,64,512]{4,3,2,1,0:T(8,128)(2,1)S(1)}, bf16[3,2,2,64,512]{4,3,2,1,0:T(8,128)(2,1)}, u32[]{:S(2)}, u32[]{:S(2)}) collective-permute-start(bf16[3,2,2,64,512]{4,3,2,1,0:T(8,128)(2,1)S(1)} %pad_maximum_fusion), channel_id=1, source_target_pairs={{0,1},{1,0},{2,3},{3,2},{4,5},{5,4},{6,7},{7,6},{8,9},{9,8},{10,11... | collective-permute-start | bytes 2359304 | tf_op jit(solution)/shard_map/ppermute | solution.py:323
  48.5 3.0 %collective-permute-start.11 = (bf16[4,2,64,512]{3,2,1,0:T(8,128)(2,1)S(1)}, bf16[4,2,64,512]{3,2,1,0:T(8,128)(2,1)S(1)}, u32[]{:S(2)}, u32[]{:S(2)}) collective-permute-start(bf16[4,2,64,512]{3,2,1,0:T(8,128)(2,1)S(1)} %get-tuple-element.126), channel_id=1, source_target_pairs={{0,1},{1,0},{2,3},{3,2},{4,5},{5,4},{6,7},{7,6},{8,9},{9,8},{10,11... | collective-permute-start | bytes 1572872 | tf_op jit(solution)/shard_map/ppermute | solution.py:323
  49.0 21.0 %collective-permute-start.7 = (bf16[3,2,2,64,512]{4,3,2,1,0:T(8,128)(2,1)S(1)}, bf16[3,2,2,64,512]{4,3,2,1,0:T(8,128)(2,1)}, u32[]{:S(2)}, u32[]{:S(2)}) collective-permute-start(bf16[3,2,2,64,512]{4,3,2,1,0:T(8,128)(2,1)S(1)} %pad_maximum_fusion), channel_id=1, source_target_pairs={{0,4},{1,3},{2,6},{3,1},{4,0},{5,7},{6,2},{7,5},{8,12},{9,11},{10,... | collective-permute-start | bytes 2359304 | tf_op jit(solution)/shard_map/ppermute | solution.py:360
  49.8 20.2 %collective-permute-start.8 = (bf16[3,2,2,64,512]{4,3,2,1,0:T(8,128)(2,1)S(1)}, bf16[3,2,2,64,512]{4,3,2,1,0:T(8,128)(2,1)}, u32[]{:S(2)}, u32[]{:S(2)}) collective-permute-start(bf16[3,2,2,64,512]{4,3,2,1,0:T(8,128)(2,1)S(1)} %pad_maximum_fusion), channel_id=1, source_target_pairs={{0,2},{1,5},{2,0},{3,7},{4,6},{5,1},{6,4},{7,3},{8,10},{9,13},{10,... | collective-permute-start | bytes 2359304 | tf_op jit(solution)/shard_map/ppermute | solution.py:360
  50.3 19.6 %collective-permute-start.10 = (bf16[2,2,64,512]{3,2,1,0:T(8,128)(2,1)}, bf16[2,2,64,512]{3,2,1,0:T(8,128)(2,1)}, u32[]{:S(2)}, u32[]{:S(2)}) collective-permute-start(bf16[2,2,64,512]{3,2,1,0:T(8,128)(2,1)} %get-tuple-element.124), channel_id=1, source_target_pairs={{0,16},{8,24},{16,0},{24,8},{1,17},{9,25},{17,1},{25,9},{2,18},{10... | collective-permute-start | bytes 786440 | tf_op jit(solution)/shard_map/ppermute | solution.py:320
  51.5 18.4 %collective-permute-start.9 = (bf16[2,2,64,512]{3,2,1,0:T(8,128)(2,1)}, bf16[2,2,64,512]{3,2,1,0:T(8,128)(2,1)}, u32[]{:S(2)}, u32[]{:S(2)}) collective-permute-start(bf16[2,2,64,512]{3,2,1,0:T(8,128)(2,1)} %get-tuple-element.123), channel_id=1, source_target_pairs={{0,8},{8,16},{16,24},{24,0},{1,9},{9,17},{17,25},{25,1},{2,10},{10... | collective-permute-start | bytes 786440 | tf_op jit(solution)/shard_map/ppermute | solution.py:320
  69.9 5.0 %collective-permute-start.16 = (bf16[3,2,2,64,512]{4,3,2,1,0:T(8,128)(2,1)}, bf16[3,2,2,64,512]{4,3,2,1,0:T(8,128)(2,1)S(1)}, u32[]{:S(2)}, u32[]{:S(2)}) collective-permute-start(bf16[3,2,2,64,512]{4,3,2,1,0:T(8,128)(2,1)} %collective-permute-done.7), channel_id=1, source_target_pairs={{0,1},{1,0},{2,3},{3,2},{4,5},{5,4},{6,7},{7,6},{8,9},{9,8},{10,11... | collective-permute-start | bytes 2359304 | tf_op jit(solution)/shard_map/ppermute | solution.py:323
  70.0 4.9 %collective-permute-start.18 = (bf16[3,2,2,64,512]{4,3,2,1,0:T(8,128)(2,1)}, bf16[3,2,2,64,512]{4,3,2,1,0:T(8,128)(2,1)S(1)}, u32[]{:S(2)}, u32[]{:S(2)}) collective-permute-start(bf16[3,2,2,64,512]{4,3,2,1,0:T(8,128)(2,1)} %collective-permute-done.8), channel_id=1, source_target_pairs={{0,1},{1,0},{2,3},{3,2},{4,5},{5,4},{6,7},{7,6},{8,9},{9,8},{10,11... | collective-permute-start | bytes 2359304 | tf_op jit(solution)/shard_map/ppermute | solution.py:323
  70.5 3.3 %collective-permute-start.15 = (bf16[4,2,64,512]{3,2,1,0:T(8,128)(2,1)S(1)}, bf16[4,2,64,512]{3,2,1,0:T(8,128)(2,1)S(1)}, u32[]{:S(2)}, u32[]{:S(2)}) collective-permute-start(bf16[4,2,64,512]{3,2,1,0:T(8,128)(2,1)S(1)} %collective-permute-done.1), channel_id=1, source_target_pairs={{0,1},{1,0},{2,3},{3,2},{4,5},{5,4},{6,7},{7,6},{8,9},{9,8},{10,11... | collective-permute-start | bytes 1572872 | tf_op jit(solution)/shard_map/ppermute | solution.py:323
  70.6 13.8 %collective-permute-start.13 = (bf16[3,2,2,64,512]{4,3,2,1,0:T(8,128)(2,1)}, bf16[3,2,2,64,512]{4,3,2,1,0:T(8,128)(2,1)S(1)}, u32[]{:S(2)}, u32[]{:S(2)}) collective-permute-start(bf16[3,2,2,64,512]{4,3,2,1,0:T(8,128)(2,1)} %collective-permute-done.7), channel_id=1, source_target_pairs={{0,2},{1,5},{2,0},{3,7},{4,6},{5,1},{6,4},{7,3},{8,10},{9,13},{10,... | collective-permute-start | bytes 2359304 | tf_op jit(solution)/shard_map/ppermute | solution.py:360
  72.1 2.8 %collective-permute-start.17 = (bf16[4,2,64,512]{3,2,1,0:T(8,128)(2,1)S(1)}, bf16[4,2,64,512]{3,2,1,0:T(8,128)(2,1)S(1)}, u32[]{:S(2)}, u32[]{:S(2)}) collective-permute-start(bf16[4,2,64,512]{3,2,1,0:T(8,128)(2,1)S(1)} %collective-permute-done.2), channel_id=1, source_target_pairs={{0,1},{1,0},{2,3},{3,2},{4,5},{5,4},{6,7},{7,6},{8,9},{9,8},{10,11... | collective-permute-start | bytes 1572872 | tf_op jit(solution)/shard_map/ppermute | solution.py:323
  73.8 10.6 %collective-permute-start.14 = (bf16[2,2,64,512]{3,2,1,0:T(8,128)(2,1)}, bf16[2,2,64,512]{3,2,1,0:T(8,128)(2,1)S(1)}, u32[]{:S(2)}, u32[]{:S(2)}) collective-permute-start(bf16[2,2,64,512]{3,2,1,0:T(8,128)(2,1)} %copy-done.1), channel_id=1, source_target_pairs={{0,24},{8,0},{16,8},{24,16},{1,25},{9,1},{17,9},{25,17},{2,26},{10... | collective-permute-start | bytes 786440 | tf_op jit(solution)/shard_map/ppermute | solution.py:320
  85.5 4.8 %collective-permute-start.22 = (bf16[3,2,2,64,512]{4,3,2,1,0:T(8,128)(2,1)S(1)}, bf16[3,2,2,64,512]{4,3,2,1,0:T(8,128)(2,1)S(1)}, u32[]{:S(2)}, u32[]{:S(2)}) collective-permute-start(bf16[3,2,2,64,512]{4,3,2,1,0:T(8,128)(2,1)S(1)} %collective-permute-done.13), channel_id=1, source_target_pairs={{0,1},{1,0},{2,3},{3,2},{4,5},{5,4},{6,7},{7,6},{8,9},{9,8},{10,11... | collective-permute-start | bytes 2359304 | tf_op jit(solution)/shard_map/ppermute | solution.py:323
  85.7 4.6 %collective-permute-start.23 = (bf16[3,2,2,64,512]{4,3,2,1,0:T(8,128)(2,1)S(1)}, bf16[3,2,2,64,512]{4,3,2,1,0:T(8,128)(2,1)S(1)}, u32[]{:S(2)}, u32[]{:S(2)}) collective-permute-start(bf16[3,2,2,64,512]{4,3,2,1,0:T(8,128)(2,1)S(1)} %pad_maximum_fusion.1), channel_id=1, source_target_pairs={{0,1},{1,0},{2,3},{3,2},{4,5},{5,4},{6,7},{7,6},{8,9},{9,8},{10,11... | collective-permute-start | bytes 2359304 | tf_op jit(solution)/shard_map/ppermute | solution.py:323
  86.1 20.1 %collective-permute-start.19 = (bf16[3,2,2,64,512]{4,3,2,1,0:T(8,128)(2,1)S(1)}, bf16[3,2,2,64,512]{4,3,2,1,0:T(8,128)(2,1)S(1)}, u32[]{:S(2)}, u32[]{:S(2)}) collective-permute-start(bf16[3,2,2,64,512]{4,3,2,1,0:T(8,128)(2,1)S(1)} %pad_maximum_fusion.1), channel_id=1, source_target_pairs={{0,4},{1,3},{2,6},{3,1},{4,0},{5,7},{6,2},{7,5},{8,12},{9,11},{10,... | collective-permute-start | bytes 2359304 | tf_op jit(solution)/shard_map/ppermute | solution.py:360
  87.4 18.8 %collective-permute-start.20 = (bf16[3,2,2,64,512]{4,3,2,1,0:T(8,128)(2,1)S(1)}, bf16[3,2,2,64,512]{4,3,2,1,0:T(8,128)(2,1)S(1)}, u32[]{:S(2)}, u32[]{:S(2)}) collective-permute-start(bf16[3,2,2,64,512]{4,3,2,1,0:T(8,128)(2,1)S(1)} %pad_maximum_fusion.1), channel_id=1, source_target_pairs={{0,2},{1,5},{2,0},{3,7},{4,6},{5,1},{6,4},{7,3},{8,10},{9,13},{10,... | collective-permute-start | bytes 2359304 | tf_op jit(solution)/shard_map/ppermute | solution.py:360
  88.4 1.9 %collective-permute-start.21 = (bf16[4,2,64,512]{3,2,1,0:T(8,128)(2,1)S(1)}, bf16[4,2,64,512]{3,2,1,0:T(8,128)(2,1)S(1)}, u32[]{:S(2)}, u32[]{:S(2)}) collective-permute-start(bf16[4,2,64,512]{3,2,1,0:T(8,128)(2,1)S(1)} %collective-permute-done.5), channel_id=1, source_target_pairs={{0,1},{1,0},{2,3},{3,2},{4,5},{5,4},{6,7},{7,6},{8,9},{9,8},{10,11... | collective-permute-start | bytes 1572872 | tf_op jit(solution)/shard_map/ppermute | solution.py:323
  106.2 2.3 %collective-permute-start.25 = (bf16[3,2,2,64,512]{4,3,2,1,0:T(8,128)(2,1)S(1)}, bf16[3,2,2,64,512]{4,3,2,1,0:T(8,128)(2,1)S(1)}, u32[]{:S(2)}, u32[]{:S(2)}) collective-permute-start(bf16[3,2,2,64,512]{4,3,2,1,0:T(8,128)(2,1)S(1)} %collective-permute-done.19), channel_id=1, source_target_pairs={{0,1},{1,0},{2,3},{3,2},{4,5},{5,4},{6,7},{7,6},{8,9},{9,8},{10,11... | collective-permute-start | bytes 2359304 | tf_op jit(solution)/shard_map/ppermute | solution.py:323
  106.3 3.3 %collective-permute-start.26 = (bf16[3,2,2,64,512]{4,3,2,1,0:T(8,128)(2,1)S(1)}, bf16[3,2,2,64,512]{4,3,2,1,0:T(8,128)(2,1)S(1)}, u32[]{:S(2)}, u32[]{:S(2)}) collective-permute-start(bf16[3,2,2,64,512]{4,3,2,1,0:T(8,128)(2,1)S(1)} %collective-permute-done.20), channel_id=1, source_target_pairs={{0,1},{1,0},{2,3},{3,2},{4,5},{5,4},{6,7},{7,6},{8,9},{9,8},{10,11... | collective-permute-start | bytes 2359304 | tf_op jit(solution)/shard_map/ppermute | solution.py:323
  106.7 12.6 %collective-permute-start.24 = (bf16[3,2,2,64,512]{4,3,2,1,0:T(8,128)(2,1)S(1)}, bf16[3,2,2,64,512]{4,3,2,1,0:T(8,128)(2,1)S(1)}, u32[]{:S(2)}, u32[]{:S(2)}) collective-permute-start(bf16[3,2,2,64,512]{4,3,2,1,0:T(8,128)(2,1)S(1)} %collective-permute-done.19), channel_id=1, source_target_pairs={{0,2},{1,5},{2,0},{3,7},{4,6},{5,1},{6,4},{7,3},{8,10},{9,13},{10,... | collective-permute-start | bytes 2359304 | tf_op jit(solution)/shard_map/ppermute | solution.py:360
  119.3 2.4 %collective-permute-start.27 = (bf16[3,2,2,64,512]{4,3,2,1,0:T(8,128)(2,1)S(1)}, bf16[3,2,2,64,512]{4,3,2,1,0:T(8,128)(2,1)S(1)}, u32[]{:S(2)}, u32[]{:S(2)}) collective-permute-start(bf16[3,2,2,64,512]{4,3,2,1,0:T(8,128)(2,1)S(1)} %collective-permute-done.24), channel_id=1, source_target_pairs={{0,1},{1,0},{2,3},{3,2},{4,5},{5,4},{6,7},{7,6},{8,9},{9,8},{10,11... | collective-permute-start | bytes 2359304 | tf_op jit(solution)/shard_map/ppermute | solution.py:323
